TPU v7x, 32 devices: a whole 2x2x4 slice. The times are simulated.
32 devices in a mesh: seq: 16 (over z, y, x), row: 2 (over core).
Axes of the slice: x: 2, y: 2, z: 4, core: 2. Of those that a mesh axis runs over, the one named last changes fastest.
Arguments:
- block_input: bfloat16 [4, 2048, 2048], P('row', 'seq'), may hold values from -6 to 6
- out_grad: bfloat16 [4, 2048, 2048], P('row', 'seq'), may hold values from -6 to 6
- doc_starts: int32 [4, 4], P('row'), may hold values from 0 to 2047, as said below
- w_query: bfloat16 [2048, 2048], P(('seq', 'row')), may hold values from -0.125 to 0.125
- w_forget: bfloat16 [2048, 2048], P(('seq', 'row')), may hold values from -0.125 to 0.125
- w_input: bfloat16 [2048, 2048], P(('seq', 'row')), may hold values from -0.125 to 0.125
- w_outgate: bfloat16 [2048, 2048], P(('seq', 'row')), may hold values from -0.125 to 0.125
- w_out: bfloat16 [2048, 2048], P(('seq', 'row')), may hold values from -0.125 to 0.125
- w_gate: bfloat16 [2048, 5632], P('seq', 'row'), may hold values from -0.125 to 0.125
- w_up: bfloat16 [2048, 5632], P('seq', 'row'), may hold values from -0.125 to 0.125
- w_down: bfloat16 [5632, 2048], P('row', 'seq'), may hold values from -0.078125 to 0.078125
- norm_gain: bfloat16 [2048], P(('seq', 'row')), may hold values from 0.5 to 1.5
- mlp_gain: bfloat16 [2048], P(('seq', 'row')), may hold values from 0.5 to 1.5
- group_gain: bfloat16 [2048], P(('seq', 'row')), may hold values from 0.5 to 1.5
- forget_bias: bfloat16 [2048], P(('seq', 'row')), may hold values from -1.5 to 9.5
Outputs:
- block_output: bfloat16 [4, 2048, 2048], P('row', 'seq')
- input_grad: bfloat16 [4, 2048, 2048], P('row', 'seq')
- grad_query: float32 [2048, 2048], P(('seq', 'row'))
- grad_forget: float32 [2048, 2048], P(('seq', 'row'))
- grad_input: float32 [2048, 2048], P(('seq', 'row'))
- grad_outgate: float32 [2048, 2048], P(('seq', 'row'))
- grad_out: float32 [2048, 2048], P(('seq', 'row'))
- grad_gate: float32 [2048, 5632], P('seq', 'row')
- grad_up: float32 [2048, 5632], P('seq', 'row')
- grad_down: float32 [5632, 2048], P('row', 'seq')
- grad_norm_gain: float32 [2048], P(('seq', 'row'))
- grad_mlp_gain: float32 [2048], P(('seq', 'row'))
- grad_group_gain: float32 [2048], P(('seq', 'row'))
- grad_forget_bias: float32 [2048], P(('seq', 'row'))
Inputs may be any that keep to these rules, and one draw needn't show every extreme that they name: `doc_starts`: the first entry of every row is 0 and entries may repeat; in every aligned block of 2 rows one row has all entries 0.
All inputs are finite; a program needn't handle non-finite values.
Results may differ from a plain program's by a relative error of at most 0.013.
Values may be sent and summed in bfloat16 or wider, within the bound.
No kernel may reach another device: no remote copies, remote signals or barrier semaphores. Data moves between devices by JAX's collectives and lax.ppermute only.
A program may use at most 512 MiB of HBM per device.

v0:
```python
import jax
import jax.numpy as jnp
from jax import lax
from jax.sharding import PartitionSpec as P

HEADS = 16


lower_bound = 0.85
epsilon = 1e-06
highest = lax.Precision.HIGHEST


def prefix(part, axis, combine, identity, reverse):
    count = lax.axis_size(axis)
    place = lax.axis_index(axis)
    ahead = count - 1 - place if reverse else place
    gathered = jax.tree.map(lambda a: lax.all_gather(a, axis), part)
    state = jax.tree.map(lambda a, e: jnp.zeros_like(a) + jnp.asarray(e, a.dtype), part, identity)

    def one(step, state):
        source = count - 1 - step if reverse else step
        return combine(
            state, jax.tree.map(lambda a: lax.dynamic_index_in_dim(a, source, 0, False), gathered)
        )

    return lax.fori_loop(0, ahead, one, state)


def rms_scale(values, gain_vec):
    return (
        values * lax.rsqrt(jnp.mean(values * values, axis=-1, keepdims=True) + epsilon) * gain_vec
    )


def gate_local(mixer_out, gate_raw, gain_vec):
    shaped = mixer_out.reshape(mixer_out.shape[:-1] + (HEADS, mixer_out.shape[-1] // HEADS))
    normed = shaped * lax.rsqrt(jnp.mean(shaped * shaped, axis=-1, keepdims=True) + epsilon)
    return normed.reshape(mixer_out.shape) * gain_vec * jax.nn.silu(gate_raw)


def glu_local(gate_a, up_b):
    return jax.nn.silu(gate_a) * up_b


def split_heads(array_in):
    return array_in.reshape(array_in.shape[0], array_in.shape[1], HEADS, array_in.shape[2] // HEADS)


def head_view(span_decay):
    return span_decay.reshape(span_decay.shape[0], HEADS, -1)[..., None]


def chain_combine(earlier, later):
    return (earlier[0] * later[0], head_view(later[0]) * earlier[1] + later[1])


def forget_terms(forget_logit):
    forget_gate = lower_bound + (1.0 - lower_bound) * jax.nn.sigmoid(forget_logit)
    key_weight = (1.0 - lower_bound) * jax.nn.sigmoid(-forget_logit)
    log_decay = jnp.cumsum(jnp.log(forget_gate), axis=1)
    return (key_weight, log_decay)


def state_local(forget_logit, values, segment):
    key_weight, log_decay = forget_terms(forget_logit)
    last_decay = log_decay[:, -1, :]
    unbroken = (segment[:, -1] == 0).astype(jnp.float32)
    span_decay = jnp.exp(last_decay) * unbroken[:, None]
    tail_mask = (segment == segment[:, -1:]).astype(jnp.float32)
    weighted = key_weight * jnp.exp(last_decay[:, None, :] - log_decay) * tail_mask[:, :, None]
    span_state = jnp.einsum(
        "rshc,rshe->rhce", split_heads(weighted), split_heads(values), precision=highest
    )
    return (span_decay, span_state)


def out_local(query_raw, forget_logit, values, segment, carried_state):
    key_weight, log_decay = forget_terms(forget_logit)
    query_act = jax.nn.silu(query_raw)
    lifted = split_heads(query_act * jnp.exp(log_decay))
    lowered = split_heads(key_weight * jnp.exp(-log_decay))
    scores = jnp.einsum("rthc,rshc->rhts", lifted, lowered, precision=highest)
    step_index = jnp.arange(segment.shape[1], dtype=jnp.int32)
    causal = step_index[:, None] >= step_index[None, :]
    same_doc = (segment[:, :, None] == segment[:, None, :]) & causal[None]
    scores = jnp.where(same_doc[:, None], scores, 0.0)
    within = jnp.einsum("rhts,rshe->rthe", scores, split_heads(values), precision=highest)
    open_rows = (segment == 0).astype(jnp.float32)
    carried = (
        jnp.einsum("rthc,rhce->rthe", lifted, carried_state, precision=highest)
        * open_rows[:, :, None, None]
    )
    combined = within + carried
    return combined.reshape(values.shape)


def contract_rows(left, right):
    return lax.dot_general(
        left, right, (((0,), (0,)), ((), ())), preferred_element_type=jnp.float32
    )


def times_transpose(grad_rows, weight):
    return lax.dot_general(
        grad_rows, weight, (((1,), (1,)), ((), ())), preferred_element_type=jnp.float32
    )


def on_device(
    block_input,
    out_grad,
    doc_starts,
    w_query,
    w_forget,
    w_input,
    w_outgate,
    w_out,
    w_gate,
    w_up,
    w_down,
    norm_gain,
    mlp_gain,
    group_gain,
    forget_bias,
):
    row_count, span_len, feature_count = block_input.shape
    token_count = row_count * span_len
    gathered = (
        lax.all_gather(w_query, ("seq", "row"), axis=0, tiled=True),
        lax.all_gather(w_forget, ("seq", "row"), axis=0, tiled=True),
        lax.all_gather(w_input, ("seq", "row"), axis=0, tiled=True),
        lax.all_gather(w_outgate, ("seq", "row"), axis=0, tiled=True),
        lax.all_gather(w_out, ("seq", "row"), axis=0, tiled=True),
        lax.all_gather(norm_gain, ("seq", "row"), axis=0, tiled=True),
        lax.all_gather(mlp_gain, ("seq", "row"), axis=0, tiled=True),
        lax.all_gather(group_gain, ("seq", "row"), axis=0, tiled=True),
        lax.all_gather(forget_bias, ("seq", "row"), axis=0, tiled=True),
    )
    (
        full_query,
        full_forget,
        full_input,
        full_outgate,
        full_out,
        first_raw,
        second_raw,
        head_raw,
        bias_raw,
    ) = gathered
    full_gate, full_up, full_down = (
        lax.all_gather(w_gate, "seq", axis=0, tiled=True),
        lax.all_gather(w_up, "seq", axis=0, tiled=True),
        lax.all_gather(w_down, "seq", axis=1, tiled=True),
    )
    first_gain = first_raw.astype(jnp.float32)
    second_gain = second_raw.astype(jnp.float32)
    head_gain = head_raw.astype(jnp.float32)
    bias_values = bias_raw.astype(jnp.float32)
    input_float = block_input.astype(jnp.float32).reshape(token_count, feature_count)
    normed_in = rms_scale(input_float, first_gain).astype(jnp.bfloat16)
    query_raw = jnp.dot(normed_in, full_query, preferred_element_type=jnp.float32)
    forget_raw = jnp.dot(normed_in, full_forget, preferred_element_type=jnp.float32)
    values = jnp.dot(normed_in, full_input, preferred_element_type=jnp.float32)
    gate_raw = jnp.dot(normed_in, full_outgate, preferred_element_type=jnp.float32)
    forget_logit = forget_raw + bias_values
    positions = lax.axis_index("seq") * span_len + jnp.arange(span_len, dtype=jnp.int32)
    reset_mask = jnp.any(doc_starts[:, :, None] == positions[None, None, :], axis=1).astype(
        jnp.int32
    )
    segment = jnp.cumsum(reset_mask, axis=1)
    query_rows = query_raw.reshape(row_count, span_len, feature_count)
    logit_rows = forget_logit.reshape(row_count, span_len, feature_count)
    value_rows = values.reshape(row_count, span_len, feature_count)
    span_decay, span_state = state_local(logit_rows, value_rows, segment)
    unit_decay = jnp.ones_like(span_decay)
    zero_state = jnp.zeros_like(span_state)
    prior_decay, carried_state = prefix(
        (span_decay, span_state), "seq", chain_combine, (unit_decay, zero_state), False
    )
    mixer_rows = out_local(query_rows, logit_rows, value_rows, segment, carried_state)
    mixer_flat = mixer_rows.reshape(token_count, feature_count)
    mixed_out = gate_local(mixer_flat, gate_raw, head_gain).astype(jnp.bfloat16)
    hidden = input_float + jnp.dot(mixed_out, full_out, preferred_element_type=jnp.float32)
    normed_mid = rms_scale(hidden, second_gain).astype(jnp.bfloat16)
    grad_float = out_grad.astype(jnp.float32).reshape(token_count, feature_count)
    grad_low = out_grad.reshape(token_count, feature_count)
    mid_all, grad_all = (
        lax.all_gather(normed_mid, "row", axis=0, tiled=True),
        lax.all_gather(grad_low, "row", axis=0, tiled=True),
    )
    gate_a = jnp.dot(mid_all, full_gate, preferred_element_type=jnp.float32)
    up_b = jnp.dot(mid_all, full_up, preferred_element_type=jnp.float32)
    product = glu_local(gate_a, up_b).astype(jnp.bfloat16)
    down_part = jnp.dot(product, full_down, preferred_element_type=jnp.float32)
    down_total = lax.psum_scatter(
        down_part.astype(jnp.bfloat16), "row", scatter_dimension=0, tiled=True
    ).astype(jnp.float32)
    block_output = (hidden + down_total).astype(jnp.bfloat16).reshape(block_input.shape)
    back_gate, back_up, back_down = (
        lax.all_gather(w_gate, "seq", axis=0, tiled=True),
        lax.all_gather(w_up, "seq", axis=0, tiled=True),
        lax.all_gather(w_down, "seq", axis=1, tiled=True),
    )
    grad_down = contract_rows(product, grad_all)
    grad_product = times_transpose(grad_all, back_down)
    glu_value, glu_pull = jax.vjp(glu_local, gate_a, up_b)
    grad_a, grad_b = glu_pull(grad_product)
    grad_a_low = grad_a.astype(jnp.bfloat16)
    grad_b_low = grad_b.astype(jnp.bfloat16)
    grad_gate = contract_rows(mid_all, grad_a_low)
    grad_up = contract_rows(mid_all, grad_b_low)
    grad_mid_part = times_transpose(grad_a_low, back_gate) + times_transpose(grad_b_low, back_up)
    grad_mid = lax.psum_scatter(
        grad_mid_part.astype(jnp.bfloat16), "row", scatter_dimension=0, tiled=True
    ).astype(jnp.float32)
    mid_value, mid_pull = jax.vjp(rms_scale, hidden, second_gain)
    grad_hidden_norm, grad_mid_gain = mid_pull(grad_mid)
    grad_hidden = grad_float + grad_hidden_norm
    mlp_sums = (
        lax.psum_scatter(grad_gate, "seq", scatter_dimension=0, tiled=True),
        lax.psum_scatter(grad_up, "seq", scatter_dimension=0, tiled=True),
        lax.psum_scatter(grad_down, "seq", scatter_dimension=1, tiled=True),
    )
    back_query, back_forget, back_input, back_outgate, back_out, first_back_raw, head_back_raw = (
        lax.all_gather(w_query, ("seq", "row"), axis=0, tiled=True),
        lax.all_gather(w_forget, ("seq", "row"), axis=0, tiled=True),
        lax.all_gather(w_input, ("seq", "row"), axis=0, tiled=True),
        lax.all_gather(w_outgate, ("seq", "row"), axis=0, tiled=True),
        lax.all_gather(w_out, ("seq", "row"), axis=0, tiled=True),
        lax.all_gather(norm_gain, ("seq", "row"), axis=0, tiled=True),
        lax.all_gather(group_gain, ("seq", "row"), axis=0, tiled=True),
    )
    first_back = first_back_raw.astype(jnp.float32)
    head_back = head_back_raw.astype(jnp.float32)
    grad_mix_low = grad_hidden.astype(jnp.bfloat16)
    grad_out = contract_rows(mixed_out, grad_mix_low)
    grad_mixed = times_transpose(grad_mix_low, back_out)
    gate_value, gate_pull = jax.vjp(gate_local, mixer_flat, gate_raw, head_back)
    grad_mixer, grad_gate_raw, grad_head_gain = gate_pull(grad_mixed)

    def mixer_part(query_in, logit_in, value_in, carry_in):
        return out_local(query_in, logit_in, value_in, segment, carry_in)

    mixer_value, mixer_pull = jax.vjp(mixer_part, query_rows, logit_rows, value_rows, carried_state)
    grad_query_rows, grad_logit_out, grad_value_out, grad_carry_local = mixer_pull(
        grad_mixer.reshape(row_count, span_len, feature_count)
    )
    later_decay, later_grad = prefix(
        (span_decay, grad_carry_local), "seq", chain_combine, (unit_decay, zero_state), True
    )
    grad_decay = jnp.sum(carried_state * later_grad, axis=-1).reshape(row_count, feature_count)

    def state_part(logit_in, value_in):
        return state_local(logit_in, value_in, segment)

    state_value, state_pull = jax.vjp(state_part, logit_rows, value_rows)
    grad_logit_state, grad_value_state = state_pull((grad_decay, later_grad))
    grad_logit = (grad_logit_out + grad_logit_state).reshape(token_count, feature_count)
    grad_value = (grad_value_out + grad_value_state).reshape(token_count, feature_count)
    grad_bias = jnp.sum(grad_logit, axis=0)
    query_low = grad_query_rows.reshape(token_count, feature_count).astype(jnp.bfloat16)
    logit_low = grad_logit.astype(jnp.bfloat16)
    value_low = grad_value.astype(jnp.bfloat16)
    outgate_low = grad_gate_raw.astype(jnp.bfloat16)
    grad_query = contract_rows(normed_in, query_low)
    grad_forget = contract_rows(normed_in, logit_low)
    grad_input = contract_rows(normed_in, value_low)
    grad_outgate = contract_rows(normed_in, outgate_low)
    grad_normed = times_transpose(query_low, back_query) + times_transpose(logit_low, back_forget)
    grad_normed = (
        grad_normed
        + times_transpose(value_low, back_input)
        + times_transpose(outgate_low, back_outgate)
    )
    first_value, first_pull = jax.vjp(rms_scale, input_float, first_back)
    grad_input_norm, grad_first_gain = first_pull(grad_normed)
    input_grad = (grad_hidden + grad_input_norm).astype(jnp.bfloat16).reshape(block_input.shape)
    mixer_sums = (
        lax.psum_scatter(grad_query, ("seq", "row"), scatter_dimension=0, tiled=True),
        lax.psum_scatter(grad_forget, ("seq", "row"), scatter_dimension=0, tiled=True),
        lax.psum_scatter(grad_input, ("seq", "row"), scatter_dimension=0, tiled=True),
        lax.psum_scatter(grad_outgate, ("seq", "row"), scatter_dimension=0, tiled=True),
        lax.psum_scatter(grad_out, ("seq", "row"), scatter_dimension=0, tiled=True),
        lax.psum_scatter(grad_first_gain, ("seq", "row"), scatter_dimension=0, tiled=True),
        lax.psum_scatter(grad_mid_gain, ("seq", "row"), scatter_dimension=0, tiled=True),
        lax.psum_scatter(grad_head_gain, ("seq", "row"), scatter_dimension=0, tiled=True),
        lax.psum_scatter(grad_bias, ("seq", "row"), scatter_dimension=0, tiled=True),
    )
    return (
        block_output,
        input_grad,
        mixer_sums[0],
        mixer_sums[1],
        mixer_sums[2],
        mixer_sums[3],
        mixer_sums[4],
        mlp_sums[0],
        mlp_sums[1],
        mlp_sums[2],
        mixer_sums[5],
        mixer_sums[6],
        mixer_sums[7],
        mixer_sums[8],
    )


def solution(mesh):
    in_specs = (
        P("row", "seq", None),
        P("row", "seq", None),
        P("row", None),
        P(("seq", "row"), None),
        P(("seq", "row"), None),
        P(("seq", "row"), None),
        P(("seq", "row"), None),
        P(("seq", "row"), None),
        P("seq", "row"),
        P("seq", "row"),
        P("row", "seq"),
        P(("seq", "row")),
        P(("seq", "row")),
        P(("seq", "row")),
        P(("seq", "row")),
    )
    out_specs = (
        P("row", "seq", None),
        P("row", "seq", None),
        P(("seq", "row"), None),
        P(("seq", "row"), None),
        P(("seq", "row"), None),
        P(("seq", "row"), None),
        P(("seq", "row"), None),
        P("seq", "row"),
        P("seq", "row"),
        P("row", "seq"),
        P(("seq", "row")),
        P(("seq", "row")),
        P(("seq", "row")),
        P(("seq", "row")),
    )
    return jax.shard_map(
        on_device, mesh=mesh, in_specs=in_specs, out_specs=out_specs, check_vma=False
    )
```

profile of v0, /device:TPU:0, one launch (start us, length us, event | category | flops | bytes accessed | tf_op | source)
XLA Modules:
  0.0 4088.4 jit_solution(15041807699031036565)
XLA Ops:
  12.9 42.6 %all-reduce.10 = (bf16[2048]{0:T(1024)(128)(2,1)S(1)}, bf16[2048]{0:T(1024)(128)(2,1)S(1)}, bf16[2048]{0:T(1024)(128)(2,1)S(1)}, bf16[2048]{0:T(1024)(128)(2,1)S(1)}) all-reduce(bf16[2048]{0:T(1024)(128)(2,1)S(1)} %dynamic-update-slice.2, bf16[2048]{0:T(1024)(128)(2,1)S(1)} %dynamic-update-slice, ...), channel_id=1, replica_groups=mesh['seq'=16,'row'=2] {'seq','row'}, use_global_device_ids=true, to_apply=%add.3 | all-reduce | flops 8192 | bytes 32768
  60.1 31.4 all-gather.19.cloned.1.call-done
  107.8 62.6 %all-gather.15.cloned.1.call-done = bf16[2048,2048]{1,0:T(8,128)(2,1)} async-done(((bf16[64,2048]{1,0:T(8,128)(2,1)}), bf16[2048,2048]{1,0:T(8,128)(2,1)}) %all-gather.15.cloned.1.call-update) | async-done | bytes 8388624 | tf_op jit(solution)/shard_map/all_gather | solution.py:132
  170.3 12.4 copy.113
  200.5 48.8 %all-gather.17.cloned.1.call-done = bf16[2048,2048]{1,0:T(8,128)(2,1)} async-done(((bf16[64,2048]{1,0:T(8,128)(2,1)}), bf16[2048,2048]{1,0:T(8,128)(2,1)}) %all-gather.17.cloned.1.call-update) | async-done | bytes 8388624 | tf_op jit(solution)/shard_map/all_gather | solution.py:130
  265.8 42.7 %all_gather.75 = f32[16,2,2048]{2,1,0:T(2,128)S(1)} all-gather(f32[1,2,2048]{2,1,0:T(2,128)S(1)} %copy.119), channel_id=1, replica_groups=mesh['seq'=16,'row'=2] {'seq'}, dimensions={0}, use_global_device_ids=true | all-gather | bytes 278528 | tf_op jit(solution)/shard_map/all_gather | solution.py:18
  320.6 283.6 %all-gather.35.cloned.1.call-done = f32[32,16,128,128]{3,2,1,0:T(8,128)} async-done(((f32[2,16,128,128]{3,2,1,0:T(8,128)}), f32[32,16,128,128]{3,2,1,0:T(8,128)}) %all-gather.35.cloned.1.call-update) | async-done | bytes 33554448 | tf_op jit(solution)/shard_map/all_gather | solution.py:18
  616.0 66.6 %all-gather.21.cloned.1.call-done = bf16[2048,2048]{1,0:T(8,128)(2,1)} async-done(((bf16[64,2048]{1,0:T(8,128)(2,1)}), bf16[2048,2048]{1,0:T(8,128)(2,1)}) %all-gather.21.cloned.1.call-update) | async-done | bytes 8388624 | tf_op jit(solution)/shard_map/all_gather | solution.py:133
  693.9 67.5 %all-gather.23.cloned.1.call-done = bf16[2048,2048]{1,0:T(8,128)(2,1)} async-done(((bf16[64,2048]{1,0:T(8,128)(2,1)}), bf16[2048,2048]{1,0:T(8,128)(2,1)}) %all-gather.23.cloned.1.call-update) | async-done | bytes 8388624 | tf_op jit(solution)/shard_map/all_gather | solution.py:134
  770.9 134.0 %all-gather.27.cloned.1.call-done = bf16[2048,2816]{1,0:T(8,128)(2,1)} async-done(((bf16[128,2816]{1,0:T(8,128)(2,1)}), bf16[2048,2816]{1,0:T(8,128)(2,1)}) %all-gather.27.cloned.1.call-update) | async-done | bytes 11534352 | tf_op jit(solution)/shard_map/all_gather | solution.py:152
  904.9 10.9 all-gather.25.cloned.1.call-done
  915.8 12.7 fusion.110
  928.5 133.4 %all-gather.29.cloned.1.call-done = bf16[2048,2816]{1,0:T(8,128)(2,1)} async-done(((bf16[128,2816]{1,0:T(8,128)(2,1)}), bf16[2048,2816]{1,0:T(8,128)(2,1)}) %all-gather.29.cloned.1.call-update) | async-done | bytes 11534352 | tf_op jit(solution)/shard_map/all_gather | solution.py:153
  1061.9 12.5 fusion.111
  1074.4 184.2 %all-gather.31.cloned.1.call-done = bf16[2816,2048]{1,0:T(8,128)(2,1)} async-done(((bf16[2816,128]{1,0:T(8,128)(2,1)}), bf16[2816,2048]{1,0:T(8,128)(2,1)}) %all-gather.31.cloned.1.call-update) | async-done | bytes 11534352 | tf_op jit(solution)/shard_map/all_gather | solution.py:154
  1258.6 16.2 multiply_convert_fusion
  1347.3 11.1 fusion.89
  1369.2 13.1 fusion.116
  1382.3 13.3 fusion.117
  1395.7 13.2 fusion.118
  1414.8 283.5 %all-gather.37.cloned.1.call-done = f32[32,16,128,128]{3,2,1,0:T(8,128)} async-done(((f32[2,16,128,128]{3,2,1,0:T(8,128)}), f32[32,16,128,128]{3,2,1,0:T(8,128)}) %all-gather.37.cloned.1.call-update) | async-done | bytes 33554448 | tf_op jit(solution)/shard_map/all_gather | solution.py:18
  1698.5 42.5 %while.27 = (s32[]{:T(128)}, f32[2,16,128,128]{3,2,1,0:T(8,128)S(1)}, s32[]{:T(128)}, f32[16,2,2048]{2,1,0:T(2,128)}, f32[16,2,16,128,128]{4,3,2,1,0:T(8,128)}, ...) while((s32[]{:T(128)}, f32[2,16,128,128]{3,2,1,0:T(8,128)S(1)}, s32[]{:T(128)}, ...), condition=%wide.region_14.15_spmd, body=%wide.region_13.14_spmd.sunk | while | flops 1048582 | bytes 6373523 | solution.py:27
  1816.2 49.2 %reduce_window_sum.54 = f32[2,128,2048]{2,1,0:T(8,128)} reduce-window(f32[2,128,2048]{2,1,0:T(8,128)S(1)} %pad_add_fusion, f32[]{:T(128)} %constant.103.clone.1), window={size=1x128x1 pad=0_0x0_127x0_0}, to_apply=%region_17.18 | reduce-window | flops 66584576 | bytes 4194308 | tf_op jit(solution)/shard_map/transpose(jvp(jit(cumsum)))/reduce_window_sum | solution.py:61
  1865.4 37.8 reduce_window_sum.52
  1947.6 39.9 all-reduce.9
  1993.2 77.9 %reduce-scatter.21.cloned.1.call-done = f32[64,2048]{1,0:T(8,128)} async-done(((f32[2048,2048]{1,0:T(8,128)}), f32[64,2048]{1,0:T(8,128)}) %reduce-scatter.21.cloned.1.call-update) | async-done | bytes 524304 | tf_op jit(solution)/shard_map/reduce_scatter | solution.py:283
  2071.1 477.6 %reduce-scatter.25.cloned.1.call-done = f32[128,2816]{1,0:T(8,128)} async-done(((f32[2048,2816]{1,0:T(8,128)}), f32[128,2816]{1,0:T(8,128)}) %reduce-scatter.25.cloned.1.call-update) | async-done | bytes 1441808 | tf_op jit(solution)/shard_map/reduce_scatter | solution.py:221
  2548.7 482.6 %reduce-scatter.27.cloned.1.call-done = f32[128,2816]{1,0:T(8,128)} async-done(((f32[2048,2816]{1,0:T(8,128)}), f32[128,2816]{1,0:T(8,128)}) %reduce-scatter.27.cloned.1.call-update) | async-done | bytes 1441808 | tf_op jit(solution)/shard_map/reduce_scatter | solution.py:222
  3031.3 482.7 %reduce-scatter.29.cloned.1.call-done = f32[2816,128]{1,0:T(8,128)} async-done(((f32[2816,2048]{1,0:T(8,128)}), f32[2816,128]{1,0:T(8,128)}) %reduce-scatter.29.cloned.1.call-update) | async-done | bytes 1441808 | tf_op jit(solution)/shard_map/reduce_scatter | solution.py:223
  3513.9 192.2 %reduce-scatter.19.cloned.1.call-done = f32[64,2048]{1,0:T(8,128)} async-done(((f32[2048,2048]{1,0:T(8,128)}), f32[64,2048]{1,0:T(8,128)}) %reduce-scatter.19.cloned.1.call-update) | async-done | bytes 524304 | tf_op jit(solution)/shard_map/reduce_scatter | solution.py:282
  3706.2 187.5 %reduce-scatter.17.cloned.1.call-done = f32[64,2048]{1,0:T(8,128)} async-done(((f32[2048,2048]{1,0:T(8,128)}), f32[64,2048]{1,0:T(8,128)}) %reduce-scatter.17.cloned.1.call-update) | async-done | bytes 524304 | tf_op jit(solution)/shard_map/reduce_scatter | solution.py:281
  3893.7 187.5 %reduce-scatter.15.cloned.1.call-done = f32[64,2048]{1,0:T(8,128)} async-done(((f32[2048,2048]{1,0:T(8,128)}), f32[64,2048]{1,0:T(8,128)}) %reduce-scatter.15.cloned.1.call-update) | async-done | bytes 524304 | tf_op jit(solution)/shard_map/reduce_scatter | solution.py:280
  (327 shorter events, 361.1 us)
Async XLA Ops:
  7.2 51.2 %copy-start.23 = (bf16[2,128,2048]{2,1,0:T(8,128)(2,1)S(1)}, bf16[2,128,2048]{2,1,0:T(8,128)(2,1)}, u32[]{:S(2)}) copy-start(bf16[2,128,2048]{2,1,0:T(8,128)(2,1)} %param.19) | copy-start | bytes 3145732
  7.2 84.2 %all-gather.19.cloned.1.call-start = ((), (), s32[]{:S(2)}) async-start(), calls=%async_computation.12 | async-start | bytes 8650752 | tf_op jit(solution)/shard_map/all_gather | solution.py:131
  7.9 162.4 %all-gather.15.cloned.1.call-start = ((), (), s32[]{:S(2)}) async-start(), calls=%async_computation.10 | async-start | bytes 8650752 | tf_op jit(solution)/shard_map/all_gather | solution.py:132
  8.7 240.7 %all-gather.17.cloned.1.call-start = ((), (), s32[]{:S(2)}) async-start(), calls=%async_computation.11 | async-start | bytes 8650752 | tf_op jit(solution)/shard_map/all_gather | solution.py:130
  9.4 594.8 %all-gather.35.cloned.1.call-start = ((), (), s32[]{:S(2)}) async-start(), calls=%async_computation.30 | async-start | bytes 35651584 | tf_op jit(solution)/shard_map/all_gather | solution.py:18
  58.4 129.8 %copy-start.51 = (f32[2,128]{1,0:T(2,128)}, f32[2,128]{1,0:T(2,128)S(1)}, u32[]{:S(2)}) copy-start(f32[2,128]{1,0:T(2,128)S(1)} %get-tuple-element.219) | copy-start | bytes 3076
  103.7 157.3 %copy-start.3 = (f32[2,128,2048]{2,1,0:T(8,128)}, f32[2,128,2048]{2,1,0:T(8,128)S(1)}, u32[]{:S(2)}) copy-start(f32[2,128,2048]{2,1,0:T(8,128)S(1)} %reduce_window_sum.50) | copy-start | bytes 6291460
  103.7 84.5 %copy-start.46 = (f32[2,1,2048]{2,1,0:T(1,128)}, f32[2,1,2048]{2,1,0:T(1,128)S(1)}, u32[]{:S(2)}) copy-start(f32[2,1,2048]{2,1,0:T(1,128)S(1)} %slice.15) | copy-start | bytes 49156
  194.9 487.6 %all-gather.21.cloned.1.call-start = ((), (), s32[]{:S(2)}) async-start(), calls=%async_computation.13 | async-start | bytes 8650752 | tf_op jit(solution)/shard_map/all_gather | solution.py:133
  195.5 565.8 %all-gather.23.cloned.1.call-start = ((), (), s32[]{:S(2)}) async-start(), calls=%async_computation.14 | async-start | bytes 8650752 | tf_op jit(solution)/shard_map/all_gather | solution.py:134
  196.1 708.8 %all-gather.27.cloned.1.call-start = ((), (), s32[]{:S(2)}) async-start(), calls=%async_computation.16 | async-start | bytes 12255232 | tf_op jit(solution)/shard_map/all_gather | solution.py:152
  196.9 719.0 %all-gather.25.cloned.1.call-start = ((), (), s32[]{:S(2)}) async-start(), calls=%async_computation.15 | async-start | bytes 3145728 | tf_op jit(solution)/shard_map/all_gather | solution.py:189
  197.2 117.0 %copy-start.43 = (pred[2,128,128]{2,1,0:T(8,128)(4,1)}, pred[2,128,128]{2,1,0:T(8,128)(4,1)S(1)}, u32[]{:S(2)}) copy-start(pred[2,128,128]{2,1,0:T(8,128)(4,1)S(1)} %compare_and_fusion) | copy-start | bytes 98308
  262.7 45.8 %copy-start.7 = (f32[2,128,2048]{1,2,0:T(8,128)S(1)}, f32[2,128,2048]{1,2,0:T(8,128)}, u32[]{:S(2)}) copy-start(f32[2,128,2048]{1,2,0:T(8,128)} %copy.155) | copy-start | bytes 6291460
  616.0 68.4 %copy-start.27 = (bf16[256,2048]{1,0:T(8,128)(2,1)S(1)}, bf16[256,2048]{1,0:T(8,128)(2,1)}, u32[]{:S(2)}) copy-start(bf16[256,2048]{1,0:T(8,128)(2,1)} %copy-done.26) | copy-start | bytes 3145732
  768.8 293.1 %all-gather.29.cloned.1.call-start = ((), (), s32[]{:S(2)}) async-start(), calls=%async_computation.17 | async-start | bytes 12255232 | tf_op jit(solution)/shard_map/all_gather | solution.py:153
  769.6 304.9 %all-gather.33.cloned.1.call-start = ((), (), s32[]{:S(2)}) async-start(), calls=%async_computation.20 | async-start | bytes 3145728 | tf_op jit(solution)/shard_map/all_gather | solution.py:190
  770.1 488.5 %all-gather.31.cloned.1.call-start = ((), (), s32[]{:S(2)}) async-start(), calls=%async_computation.18 | async-start | bytes 12255232 | tf_op jit(solution)/shard_map/all_gather | solution.py:154
  770.9 536.1 %reduce-scatter.13.cloned.1.call-start = ((), (), s32[]{:S(2)}) async-start(), calls=%async_computation.21 | async-start | bytes 3145728 | tf_op jit(solution)/shard_map/reduce_scatter | solution.py:214
  1296.0 21.1 reduce-scatter.11.cloned.1.call-start
  1306.9 391.3 %all-gather.37.cloned.1.call-start = ((), (), s32[]{:S(2)}) async-start(), calls=%async_computation.31 | async-start | bytes 35651584 | tf_op jit(solution)/shard_map/all_gather | solution.py:18
  1340.2 68.7 %copy-start.5 = (f32[2,128,16,128]{1,3,2,0:T(8,128)}, f32[2,128,16,128]{1,3,2,0:T(8,128)S(1)}, u32[]{:S(2)}) copy-start(f32[2,128,16,128]{1,3,2,0:T(8,128)S(1)} %add_add_fusion.1) | copy-start | bytes 6291460
  1346.1 647.1 %reduce-scatter.23.cloned.1.call-start = ((), (), s32[]{:S(2)}) async-start(), calls=%async_computation.26 | async-start | bytes 17301504 | tf_op jit(solution)/shard_map/reduce_scatter | solution.py:284
  1358.3 712.8 %reduce-scatter.21.cloned.1.call-start = ((), (), s32[]{:S(2)}) async-start(), calls=%async_computation.25 | async-start | bytes 17301504 | tf_op jit(solution)/shard_map/reduce_scatter | solution.py:283
  1369.1 1179.6 %reduce-scatter.25.cloned.1.call-start = ((), (), s32[]{:S(2)}) async-start(), calls=%async_computation.27 | async-start | bytes 24510464 | tf_op jit(solution)/shard_map/reduce_scatter | solution.py:221
  1382.3 1649.0 %reduce-scatter.27.cloned.1.call-start = ((), (), s32[]{:S(2)}) async-start(), calls=%async_computation.28 | async-start | bytes 24510464 | tf_op jit(solution)/shard_map/reduce_scatter | solution.py:222
  1395.7 2118.3 %reduce-scatter.29.cloned.1.call-start = ((), (), s32[]{:S(2)}) async-start(), calls=%async_computation.29 | async-start | bytes 24510464 | tf_op jit(solution)/shard_map/reduce_scatter | solution.py:223
  1408.9 2297.3 %reduce-scatter.19.cloned.1.call-start = ((), (), s32[]{:S(2)}) async-start(), calls=%async_computation.24 | async-start | bytes 17301504 | tf_op jit(solution)/shard_map/reduce_scatter | solution.py:282
  1762.7 2131.0 %reduce-scatter.17.cloned.1.call-start = ((), (), s32[]{:S(2)}) async-start(), calls=%async_computation.23 | async-start | bytes 17301504 | tf_op jit(solution)/shard_map/reduce_scatter | solution.py:281
  1919.0 2162.1 %reduce-scatter.15.cloned.1.call-start = ((), (), s32[]{:S(2)}) async-start(), calls=%async_computation.22 | async-start | bytes 17301504 | tf_op jit(solution)/shard_map/reduce_scatter | solution.py:280
  1943.5 46.4 %copy-start.54 = (f32[2,128]{1,0:T(2,128)S(1)}, f32[2,128]{1,0:T(2,128)}, u32[]{:S(2)}) copy-start(f32[2,128]{1,0:T(2,128)} %copy-done.53) | copy-start | bytes 3076
  1943.5 46.5 %copy-start.18 = (f32[256,2048]{1,0:T(8,128)S(1)}, f32[256,2048]{1,0:T(8,128)}, u32[]{:S(2)}) copy-start(f32[256,2048]{1,0:T(8,128)} %copy-done.17) | copy-start | bytes 6291460
  (56 other events, 384.3 us)
Sparse Core Ops, SparseCore 0:
  10.9 80.4 all-gather.18
  94.3 76.0 all-gather.14
  173.2 76.0 all-gather.16
  252.0 352.1 all-gather.34
  606.9 75.6 all-gather.20
  685.3 76.0 all-gather.22
  764.1 140.7 all-gather.26
  907.0 8.7 all-gather.24
  918.6 143.3 all-gather.28
  1063.3 8.7 all-gather.32
  1074.8 183.7 all-gather.30
  1296.1 7.7 reduce-scatter.12
  1307.0 9.9 reduce-scatter.10
  1346.2 352.0 all-gather.36
  1701.0 180.8 reduce-scatter.22
  1884.6 186.4 reduce-scatter.20
  2073.8 474.8 reduce-scatter.24
  2551.4 479.7 reduce-scatter.26
  3034.1 479.7 reduce-scatter.28
  3516.7 189.4 reduce-scatter.18
  3709.0 184.6 reduce-scatter.16
  3896.6 184.5 reduce-scatter.14
where the time goes:
time: 4100 us; the launch traced here: 4090 us
  waiting for transfers between devices  3410 us (83%)
  matrix products  294 us (7%)
  other arithmetic  158 us (4%)
  blocking collectives  125 us (3%)
  local copies, waits for them, and re-layouts  86.4 us (2%)
    all_gather x2, waiting for transfers between devices, prefix(): gathered = jax.tree.map(lambda a: lax.all_gather(a, axis), part)  567 us
    reduce_scatter x1, waiting for transfers between devices, on_device(): lax.psum_scatter(grad_down, 'seq', scatter_dimension=1, tiled=True)  483 us
    reduce_scatter x1, waiting for transfers between devices, on_device(): lax.psum_scatter(grad_up, 'seq', scatter_dimension=0, tiled=True)  483 us
    reduce_scatter x1, waiting for transfers between devices, on_device(): lax.psum_scatter(grad_gate, 'seq', scatter_dimension=0, tiled=True)  478 us
    reduce_scatter x1, waiting for transfers between devices, on_device(): lax.psum_scatter(grad_input, ('seq', 'row'), scatter_dimension=0, tiled=T...  192 us
    reduce_scatter x1, waiting for transfers between devices, on_device(): lax.psum_scatter(grad_forget, ('seq', 'row'), scatter_dimension=0, tiled=...  188 us
    reduce_scatter x1, waiting for transfers between devices, on_device(): lax.psum_scatter(grad_query, ('seq', 'row'), scatter_dimension=0, tiled=T...  187 us
    all_gather x1, waiting for transfers between devices, on_device(): lax.all_gather(w_down, 'seq', axis=1, tiled=True)  184 us
  transfers between devices with their start and end apart: 22, of which 19 were waited for; matrix products, arithmetic and copies ran while one was open for 11% of the time, Pallas kernels for 0%

commit v1 on v0

v1 whole, which is shorter than its diff:
```python
import functools

import jax
import jax.numpy as jnp
from jax import lax
from jax.experimental import pallas as pl
from jax.experimental.pallas import tpu as pltpu
from jax.sharding import Mesh, PartitionSpec as P

HEADS = 16

lower_bound = 0.85
span_bound = 1.0 - lower_bound
epsilon = 1e-06
f32 = jnp.float32
bf16 = jnp.bfloat16
swap = ((0, 1), (1, 0))
everywhere = ("z", "y", "x", "row")
group = ("y", "x", "row")
plane = ("y", "x")


def swap_x(a):
    return lax.ppermute(a, "x", swap)


def swap_y(a):
    return lax.ppermute(a, "y", swap)


def swap_row(a):
    return lax.ppermute(a, "row", swap)


def gather_group(a):
    half = a.shape[0] // 2
    from_x = swap_x(a)
    from_y = swap_y(a)
    low = swap_y(from_x[:half])
    high = swap_x(from_y[half:])
    near = (a, from_x, from_y, low, high)
    far = tuple(swap_row(piece) for piece in near)
    return jnp.concatenate(near + far, axis=0)


def scatter_group(near, far):
    rows, columns = near.shape
    tokens = rows // 4
    half = columns // 2
    mine = near.astype(f32) + swap_row(far.astype(bf16)).astype(f32)
    mine = mine.reshape(2, 2, tokens, columns)
    left, right = mine[..., :half], mine[..., half:]
    left = left[:, 0] + swap_x(left[:, 1].astype(bf16)).astype(f32)
    right = right[0] + swap_y(right[1].astype(bf16)).astype(f32)
    left = left[0] + swap_y(left[1].astype(bf16)).astype(f32)
    right = right[0] + swap_x(right[1].astype(bf16)).astype(f32)
    return jnp.concatenate([left, right], axis=-1)


def relay(parts, forward):
    count = lax.axis_size("z")
    if forward:
        pairs = [(i, i + 1) for i in range(count - 1)]
    else:
        pairs = [(i + 1, i) for i in range(count - 1)]
    got = []
    for _ in range(count - 1):
        parts = jax.tree.map(lambda a: lax.ppermute(a, "z", pairs), parts)
        got.append(parts)
    return got


def carry_from(got):
    carry = got[-1][0]
    for state, decay in got[-2::-1]:
        carry = state + decay * carry
    return carry


def mm(a, b, dims):
    return lax.dot_general(
        a.astype(bf16), b.astype(bf16), (dims, ((), ())), preferred_element_type=f32
    )


def split_sum(ones_matrix, values, dims):
    first = values.astype(bf16)
    rest = values - first.astype(f32)
    second = rest.astype(bf16)
    third = (rest - second.astype(f32)).astype(bf16)
    total = lax.dot_general(ones_matrix, first, (dims, ((), ())), preferred_element_type=f32)
    total += lax.dot_general(ones_matrix, second, (dims, ((), ())), preferred_element_type=f32)
    total += lax.dot_general(ones_matrix, third, (dims, ((), ())), preferred_element_type=f32)
    return total


NT = ((1,), (1,))
NN = ((1,), (0,))
TN = ((0,), (0,))


def chunk_masks(docs_ref, row_at, start, size):
    at_row = lax.broadcasted_iota(jnp.int32, (size, size), 0)
    at_col = lax.broadcasted_iota(jnp.int32, (size, size), 1)
    same = at_row >= at_col
    opened = at_row >= 0
    tail = at_row >= 0
    whole = jnp.bool_(True)
    for entry in range(docs_ref.shape[1]):
        place = docs_ref[row_at, entry] - start
        same = same & ~((at_col < place) & (place <= at_row))
        opened = opened & ~((0 <= place) & (place <= at_row))
        tail = tail & ~((at_row < place) & (place <= size - 1))
        whole = whole & ~((0 <= place) & (place <= size - 1))
    return same, opened, tail, whole


def decay_terms(logit, tri):
    forget = lower_bound + span_bound * jax.nn.sigmoid(logit)
    key = span_bound * jax.nn.sigmoid(-logit)
    log_sum = split_sum(tri, jnp.log(forget), NN)
    return forget, key, log_sum


def lower_ones(size):
    at_row = lax.broadcasted_iota(jnp.int32, (size, size), 0)
    at_col = lax.broadcasted_iota(jnp.int32, (size, size), 1)
    return (at_row >= at_col).astype(f32).astype(bf16)


def head_rows(ref, head, width):
    return ref[0, 0, :, head * width : (head + 1) * width]


def state_kernel(at_ref, docs_ref, logit_ref, value_ref, bias_ref, state_ref, decay_ref):
    size = logit_ref.shape[2]
    heads = state_ref.shape[1]
    width = state_ref.shape[2]
    outer, inner, chunk = pl.program_id(0), pl.program_id(1), pl.program_id(2)
    row_at = outer * pl.num_programs(1) + inner
    _, _, tail, whole = chunk_masks(docs_ref, row_at, at_ref[1] + chunk * size, size)
    tri = lower_ones(size)

    @pl.when(chunk == 0)
    def _():
        state_ref[...] = jnp.zeros_like(state_ref)
        decay_ref[...] = jnp.ones_like(decay_ref)

    for head in range(heads):
        cut = slice(head * width, (head + 1) * width)
        logit = logit_ref[0, 0, :, cut] + bias_ref[:, cut]
        _, key, log_sum = decay_terms(logit, tri)
        last = log_sum[size - 1 : size, :]
        passed = jnp.where(whole, jnp.exp(last), 0.0)
        weighted = jnp.where(tail, key * jnp.exp(last - log_sum), 0.0)
        state_ref[0, head] = state_ref[0, head] * passed + mm(
            value_ref[0, 0, :, cut], weighted, TN
        )
        decay_ref[0, :, cut] = decay_ref[0, :, cut] * passed


def forward_kernel(
    at_ref, docs_ref, proj_ref, bias_ref, carry_ref, out_ref, mixed_ref, starts_ref, state
):
    size = proj_ref.shape[2]
    heads = state.shape[0]
    width = state.shape[1]
    wide = heads * width
    outer, inner, chunk = pl.program_id(0), pl.program_id(1), pl.program_id(2)
    row_at = outer * pl.num_programs(1) + inner
    same, opened, tail, whole = chunk_masks(docs_ref, row_at, at_ref[1] + chunk * size, size)
    tri = lower_ones(size)

    @pl.when(chunk == 0)
    def _():
        state[...] = carry_ref[0]

    for head in range(heads):
        cut = slice(head * width, (head + 1) * width)
        query = head_rows(proj_ref, head, width)
        logit = head_rows(proj_ref, heads + head, width) + bias_ref[:, cut]
        value = head_rows(proj_ref, 2 * heads + head, width).astype(bf16)
        gate = head_rows(proj_ref, 3 * heads + head, width)
        _, key, log_sum = decay_terms(logit, tri)
        last = log_sum[size - 1 : size, :]
        lifted = (query * jax.nn.sigmoid(query) * jnp.exp(log_sum)).astype(bf16)
        lowered = (key * jnp.exp(-log_sum)).astype(bf16)
        scores = jnp.where(same, mm(lifted, lowered, NT), 0.0)
        begin = state[head]
        starts_ref[0, 0, head] = begin
        out = mm(scores, value, NN) + jnp.where(opened, mm(lifted, begin, NT), 0.0)
        passed = jnp.where(whole, jnp.exp(last), 0.0)
        weighted = jnp.where(tail, key * jnp.exp(last - log_sum), 0.0)
        state[head] = begin * passed + mm(value, weighted, TN)
        scale = lax.rsqrt(jnp.mean(out * out, axis=-1, keepdims=True) + epsilon)
        out_ref[0, 0, :, cut] = out
        mixed_ref[0, 0, :, cut] = (out * scale * (gate * jax.nn.sigmoid(gate))).astype(bf16)


def out_grad_terms(out, gate, grad_mixed):
    gate_on = jax.nn.sigmoid(gate)
    scale = lax.rsqrt(jnp.mean(out * out, axis=-1, keepdims=True) + epsilon)
    normed = out * scale
    grad_normed = grad_mixed * (gate * gate_on)
    grad_out = scale * (
        grad_normed - normed * jnp.mean(grad_normed * normed, axis=-1, keepdims=True)
    )
    return gate_on, normed, grad_out


def back_state_kernel(
    at_ref, docs_ref, query_ref, logit_ref, gate_ref, out_ref, grad_ref, bias_ref, state_ref
):
    size = query_ref.shape[2]
    heads = state_ref.shape[1]
    width = state_ref.shape[2]
    outer, inner, step = pl.program_id(0), pl.program_id(1), pl.program_id(2)
    chunk = pl.num_programs(2) - 1 - step
    row_at = outer * pl.num_programs(1) + inner
    _, opened, _, whole = chunk_masks(docs_ref, row_at, at_ref[1] + chunk * size, size)
    tri = lower_ones(size)

    @pl.when(step == 0)
    def _():
        state_ref[...] = jnp.zeros_like(state_ref)

    for head in range(heads):
        cut = slice(head * width, (head + 1) * width)
        query = query_ref[0, 0, :, cut]
        logit = logit_ref[0, 0, :, cut] + bias_ref[:, cut]
        _, _, log_sum = decay_terms(logit, tri)
        last = log_sum[size - 1 : size, :]
        lifted = jnp.where(opened, query * jax.nn.sigmoid(query) * jnp.exp(log_sum), 0.0)
        _, _, grad_out = out_grad_terms(
            out_ref[0, 0, :, cut], gate_ref[0, 0, :, cut], grad_ref[0, 0, :, cut]
        )
        passed = jnp.where(whole, jnp.exp(last), 0.0)
        state_ref[0, head] = state_ref[0, head] * passed + mm(grad_out, lifted, TN)


def backward_kernel(
    at_ref,
    docs_ref,
    proj_ref,
    out_ref,
    grad_ref,
    bias_ref,
    starts_ref,
    carry_ref,
    all_ref,
    bias_grad_ref,
    state,
):
    size = proj_ref.shape[2]
    heads = state.shape[0]
    width = state.shape[1]
    wide = heads * width
    outer, inner, step = pl.program_id(0), pl.program_id(1), pl.program_id(2)
    chunk = pl.num_programs(2) - 1 - step
    row_at = outer * pl.num_programs(1) + inner
    same, opened, tail, whole = chunk_masks(docs_ref, row_at, at_ref[1] + chunk * size, size)
    tri = lower_ones(size)

    @pl.when((step == 0) & (row_at == 0))
    def _():
        bias_grad_ref[...] = jnp.zeros_like(bias_grad_ref)

    @pl.when(step == 0)
    def _():
        state[...] = carry_ref[0]

    for head in range(heads):
        cut = slice(head * width, (head + 1) * width)
        query = head_rows(proj_ref, head, width)
        logit = head_rows(proj_ref, heads + head, width) + bias_ref[:, cut]
        value = head_rows(proj_ref, 2 * heads + head, width).astype(bf16)
        gate = head_rows(proj_ref, 3 * heads + head, width)
        grad_mixed = grad_ref[0, 0, :, cut]
        forget, key, log_sum = decay_terms(logit, tri)
        last = log_sum[size - 1 : size, :]
        rise = jnp.exp(log_sum)
        fall = jnp.exp(-log_sum)
        remain = jnp.where(tail, jnp.exp(last - log_sum), 0.0)
        query_on = jax.nn.sigmoid(query)
        lifted = (query * query_on * rise).astype(bf16)
        lowered = (key * fall).astype(bf16)
        weighted = (key * remain).astype(bf16)
        scores = jnp.where(same, mm(lifted, lowered, NT), 0.0)
        gate_on, normed, grad_out = out_grad_terms(out_ref[0, 0, :, cut], gate, grad_mixed)
        grad_low = grad_out.astype(bf16)
        begin = starts_ref[0, 0, head]
        later = state[head]
        later_low = later.astype(bf16)
        grad_scores = jnp.where(same, mm(grad_low, value, NT), 0.0).astype(bf16)
        grad_value = mm(scores, grad_low, TN) + mm(weighted, later_low, NT)
        grad_lifted = mm(grad_scores, lowered, NN) + jnp.where(
            opened, mm(grad_low, begin, NN), 0.0
        )
        grad_lowered = mm(grad_scores, lifted, TN)
        grad_weighted = mm(value, later_low, NN)
        passed = jnp.where(whole, jnp.exp(last), 0.0)
        open_lifted = jnp.where(opened, lifted.astype(f32), 0.0)
        state[head] = later * passed + mm(grad_low, open_lifted, TN)
        through = jnp.sum(begin * later, axis=0, keepdims=True) * passed
        weighted_part = grad_weighted * weighted.astype(f32)
        grad_log = (
            grad_lifted * lifted.astype(f32) - grad_lowered * lowered.astype(f32) - weighted_part
        )
        grad_last = through + jnp.sum(weighted_part, axis=0, keepdims=True)
        grad_step = split_sum(tri, grad_log, TN) + grad_last
        grad_key = grad_lowered * fall + grad_weighted * remain
        grad_logit = (
            span_bound
            * jax.nn.sigmoid(logit)
            * jax.nn.sigmoid(-logit)
            * (grad_step / forget - grad_key)
        )
        grad_query = grad_lifted * rise * query_on * (1.0 + query * (1.0 - query_on))
        grad_gate = grad_mixed * normed * gate_on * (1.0 + gate * (1.0 - gate_on))
        bias_grad_ref[:, cut] += jnp.sum(grad_logit, axis=0, keepdims=True)
        for place, part in enumerate((grad_query, grad_logit, grad_value, grad_gate)):
            low = place * wide + head * width
            all_ref[0, 0, :, low : low + width] = part.astype(bf16)


def local_call(kernel, at, docs, ins, in_specs, out_shapes, out_specs, grid, scratch=()):
    return pl.pallas_call(
        kernel,
        grid_spec=pltpu.PrefetchScalarGridSpec(
            num_scalar_prefetch=2,
            grid=grid,
            in_specs=in_specs,
            out_specs=out_specs,
            scratch_shapes=scratch,
        ),
        out_shape=out_shapes,
        compiler_params=pltpu.CompilerParams(
            dimension_semantics=("arbitrary",) * 3, vmem_limit_bytes=40 * 1024 * 1024
        ),
    )(at, docs, *ins)


def contract_rows(left, right):
    return lax.dot_general(left, right, (TN, ((), ())), preferred_element_type=f32)


def times_transpose(left, right):
    return lax.dot_general(left, right, (NT, ((), ())), preferred_element_type=f32)


def times(left, right):
    return jnp.dot(left, right, preferred_element_type=f32)


def rms_rate(values):
    return lax.rsqrt(jnp.mean(values * values, axis=-1, keepdims=True) + epsilon)


def rms_back(grad, values, rate):
    return rate * grad - values * (
        rate * rate * rate * jnp.mean(grad * values, axis=-1, keepdims=True)
    )


def on_device(
    block_input,
    out_grad,
    doc_starts,
    w_query,
    w_forget,
    w_input,
    w_outgate,
    w_out,
    w_gate,
    w_up,
    w_down,
    norm_gain,
    mlp_gain,
    group_gain,
    forget_bias,
):
    row_count, span, features = block_input.shape
    groups = lax.axis_size("z")
    own_row = lax.axis_index("row")
    own_spot = lax.axis_index("y") * 2 + lax.axis_index("x")
    spots, members = 4, 8
    tokens = row_count * span
    width = features // HEADS
    heads = HEADS // members
    wide = heads * width
    share = w_query.shape[0]
    units = w_gate.shape[1] // spots
    block = w_gate.shape[0]

    input_float = block_input.astype(f32).reshape(tokens, features)
    first_rate = rms_rate(input_float)
    normed_all = gather_group((input_float * first_rate).astype(bf16))

    first_gain = norm_gain.astype(f32)[:, None]
    mixer_weights = (w_query, w_forget, w_input, w_outgate)
    scaled = jnp.stack([(w.astype(f32) * first_gain).astype(bf16) for w in mixer_weights])
    scaled = scaled.reshape(4, share, 2, heads, spots, width).transpose(4, 2, 1, 0, 3, 5)
    scaled = scaled.reshape(members, share, 4 * wide)
    scaled = lax.all_to_all(scaled, group, 0, 0, tiled=True)
    mixer_all = lax.all_gather(
        scaled.reshape(members * share, 4 * wide), "z", axis=0, tiled=True
    )

    bias_sent = jnp.broadcast_to(forget_bias.astype(f32), (groups * members, share))
    bias_all = lax.all_to_all(bias_sent, everywhere, 0, 0, tiled=True)
    bias_all = bias_all.reshape(2, heads, spots, width)
    bias_here = lax.dynamic_index_in_dim(bias_all, own_row, 0, False)
    bias_here = lax.dynamic_index_in_dim(bias_here, own_spot, 1, False).reshape(1, wide)

    head_gain = group_gain.astype(f32)[:, None]
    out_scaled = (w_out.astype(f32) * head_gain).astype(bf16)
    by_chip = 2 * share == width and groups == 2 * heads
    if by_chip:
        held = lax.all_gather(out_scaled, "z", axis=0, tiled=False)
        held = held.reshape(2, heads, share, features)
        keep = lax.dynamic_index_in_dim(held, own_row, 0, False)
        give = lax.dynamic_index_in_dim(held, 1 - own_row, 0, False)
        take = swap_row(give)
        own_first = own_row == 0
        out_here = jnp.stack(
            [jnp.where(own_first, keep, take), jnp.where(own_first, take, keep)], axis=1
        ).reshape(wide, features)
    else:
        held = lax.all_gather(out_scaled, everywhere, axis=0, tiled=True)
        held = held.reshape(2, heads, spots, width, features)
        held = lax.dynamic_index_in_dim(held, own_row, 0, False)
        out_here = lax.dynamic_index_in_dim(held, own_spot, 1, False).reshape(wide, features)

    gain_pair = swap_row(mlp_gain)
    mid_gain = jnp.where(
        own_row == 0,
        jnp.concatenate([mlp_gain, gain_pair]),
        jnp.concatenate([gain_pair, mlp_gain]),
    ).astype(f32)[:, None]
    gate_scaled = (w_gate.astype(f32) * mid_gain).astype(bf16)
    up_scaled = (w_up.astype(f32) * mid_gain).astype(bf16)
    down_turned = w_down.T
    gate_cut = gate_scaled.reshape(block, spots, units)
    up_cut = up_scaled.reshape(block, spots, units)
    down_cut = down_turned.reshape(block, spots, units)
    pair_cut = jnp.concatenate([gate_cut, up_cut], axis=-1).transpose(1, 0, 2)
    pair_cut = lax.all_to_all(pair_cut, plane, 0, 0, tiled=True)
    down_cut = lax.all_to_all(down_cut.transpose(1, 0, 2), plane, 0, 0, tiled=True)
    pair_all = lax.all_gather(
        pair_cut.reshape(spots * block, 2 * units), "z", axis=0, tiled=True
    )
    down_all = lax.all_gather(down_cut.reshape(spots * block, units), "z", axis=0, tiled=True)
    gate_all, up_all = pair_all[:, :units], pair_all[:, units:]

    grad_low = out_grad.reshape(tokens, features)
    grad_all = gather_group(grad_low)

    docs = jnp.concatenate([doc_starts, swap_row(doc_starts)], axis=0)
    at = jnp.stack([own_spot, lax.axis_index("z") * (spots * span)]).astype(jnp.int32)
    proj = times(normed_all, mixer_all).reshape(members, row_count, span, 4 * wide)

    grid = (2, row_count, spots)

    def there(place):
        return lambda o, i, c, at_ref, docs_ref: (o * spots + (c ^ at_ref[0]), i, 0, place)

    def back(place):
        return lambda o, i, c, at_ref, docs_ref: (
            o * spots + ((spots - 1 - c) ^ at_ref[0]),
            i,
            0,
            place,
        )

    slab = (1, 1, span, wide)
    full_slab = (1, 1, span, 4 * wide)
    state_slab = (1, heads, width, width)
    rows_all = 2 * row_count
    bias_spec = pl.BlockSpec((1, wide), lambda o, i, c, at_ref, docs_ref: (0, 0))

    def by_row(o, i, c, at_ref, docs_ref):
        return (o * row_count + i, 0, 0, 0)

    state_spec = pl.BlockSpec(state_slab, by_row)
    state_shape = jax.ShapeDtypeStruct((rows_all, heads, width, width), f32)

    span_state, span_decay = local_call(
        state_kernel,
        at,
        docs,
        (proj, proj, bias_here),
        [pl.BlockSpec(slab, there(1)), pl.BlockSpec(slab, there(2)), bias_spec],
        (state_shape, jax.ShapeDtypeStruct((rows_all, 1, wide), f32)),
        (
            state_spec,
            pl.BlockSpec(
                (1, 1, wide), lambda o, i, c, at_ref, docs_ref: (o * row_count + i, 0, 0)
            ),
        ),
        grid,
    )
    span_decay = span_decay.reshape(rows_all, heads, 1, width)
    carried = carry_from(relay((span_state, span_decay), True))

    mixer_out, mixed, starts = local_call(
        forward_kernel,
        at,
        docs,
        (proj, bias_here, carried),
        [pl.BlockSpec(full_slab, there(0)), bias_spec, state_spec],
        (
            jax.ShapeDtypeStruct((members, row_count, span, wide), f32),
            jax.ShapeDtypeStruct((members, row_count, span, wide), bf16),
            jax.ShapeDtypeStruct((rows_all, spots, heads, width, width), f32),
        ),
        (
            pl.BlockSpec(slab, there(0)),
            pl.BlockSpec(slab, there(0)),
            pl.BlockSpec(
                (1, 1, heads, width, width),
                lambda o, i, c, at_ref, docs_ref: (o * row_count + i, c, 0, 0, 0),
            ),
        ),
        grid,
        (pltpu.VMEM((heads, width, width), f32),),
    )
    half = spots * tokens
    mixed_flat = mixed.reshape(2 * half, wide)
    far_part = times(mixed_flat[half:], out_here)
    near_part = times(mixed_flat[:half], out_here)
    hidden = input_float + scatter_group(near_part, far_part)

    mid_rate = rms_rate(hidden)
    mid_all = gather_group((hidden * mid_rate).astype(bf16))
    gate_a = times(mid_all, gate_all)
    up_b = times(mid_all, up_all)
    gate_on = jax.nn.sigmoid(gate_a)
    gate_act = gate_a * gate_on
    product = (gate_act * up_b).astype(bf16)
    grad_product = times(grad_all, down_all)
    grad_a = (grad_product * up_b * gate_on * (1.0 + gate_a * (1.0 - gate_on))).astype(bf16)
    grad_b = (grad_product * gate_act).astype(bf16)
    far_mid = times_transpose(grad_a[half:], gate_all) + times_transpose(grad_b[half:], up_all)
    near_mid = times_transpose(grad_a[:half], gate_all) + times_transpose(grad_b[:half], up_all)
    grad_mid = scatter_group(near_mid, far_mid)
    grad_float = out_grad.astype(f32).reshape(tokens, features)
    grad_hidden = grad_float + rms_back(grad_mid, hidden, mid_rate)
    far_down = times_transpose(product[half:], down_all)
    near_down = times_transpose(product[:half], down_all)
    block_output = (hidden + scatter_group(near_down, far_down)).astype(bf16)

    def spread(partial, axis_size):
        return lax.psum_scatter(partial.astype(bf16), "z", scatter_dimension=0, tiled=True)

    grad_down = spread(contract_rows(grad_all, product), groups)
    grad_pair = spread(
        jnp.concatenate([contract_rows(mid_all, grad_a), contract_rows(mid_all, grad_b)], axis=-1),
        groups,
    )

    gm_all = gather_group(grad_hidden.astype(bf16))
    grad_mixed = times_transpose(gm_all, out_here).reshape(members, row_count, span, wide)
    local_back = local_call(
        back_state_kernel,
        at,
        docs,
        (proj, proj, proj, mixer_out, grad_mixed, bias_here),
        [
            pl.BlockSpec(slab, back(0)),
            pl.BlockSpec(slab, back(1)),
            pl.BlockSpec(slab, back(3)),
            pl.BlockSpec(slab, back(0)),
            pl.BlockSpec(slab, back(0)),
            bias_spec,
        ],
        state_shape,
        state_spec,
        grid,
    )
    later = carry_from(relay((local_back, span_decay), False))
    grads_flat, bias_part = local_call(
        backward_kernel,
        at,
        docs,
        (proj, mixer_out, grad_mixed, bias_here, starts, later),
        [
            pl.BlockSpec(full_slab, back(0)),
            pl.BlockSpec(slab, back(0)),
            pl.BlockSpec(slab, back(0)),
            bias_spec,
            pl.BlockSpec(
                (1, 1, heads, width, width),
                lambda o, i, c, at_ref, docs_ref: (o * row_count + i, spots - 1 - c, 0, 0, 0),
            ),
            state_spec,
        ],
        (
            jax.ShapeDtypeStruct((members, row_count, span, 4 * wide), bf16),
            jax.ShapeDtypeStruct((1, wide), f32),
        ),
        (pl.BlockSpec(full_slab, back(0)), bias_spec),
        grid,
        (pltpu.VMEM((heads, width, width), f32),),
    )
    grads_flat = grads_flat.reshape(2 * half, 4 * wide)
    grad_mixer = spread(contract_rows(normed_all, grads_flat), groups)
    far_in = times_transpose(grads_flat[half:], mixer_all)
    near_in = times_transpose(grads_flat[:half], mixer_all)
    grad_normed = scatter_group(near_in, far_in)
    input_grad = grad_hidden + rms_back(grad_normed, input_float, first_rate)
    input_grad = input_grad.astype(bf16).reshape(block_input.shape)

    grad_out_rows = contract_rows(mixed_flat, gm_all).astype(bf16)
    if by_chip:
        cut = grad_out_rows.reshape(heads, 2, share, features)
        keep = lax.dynamic_index_in_dim(cut, own_row, 1, False)
        give = lax.dynamic_index_in_dim(cut, 1 - own_row, 1, False)
        take = swap_row(give)
        cut = jnp.concatenate(
            [jnp.where(own_first, keep, take), jnp.where(own_first, take, keep)], axis=0
        )
        grad_out = lax.psum_scatter(
            cut.reshape(groups * share, features), "z", scatter_dimension=0, tiled=True
        )
    else:
        placed = jnp.zeros((2, heads, spots, width, features), bf16)
        placed = lax.dynamic_update_slice(
            placed,
            grad_out_rows.reshape(1, heads, 1, width, features),
            (own_row, 0, own_spot, 0, 0),
        )
        grad_out = lax.psum_scatter(
            placed.reshape(features, features), everywhere, scatter_dimension=0, tiled=True
        )
    grad_out = grad_out.astype(f32)
    grad_head_gain = jnp.sum(grad_out * w_out.astype(f32), axis=1)

    pair_back = lax.all_to_all(
        grad_pair.reshape(spots, block, 2 * units), plane, 0, 0, tiled=True
    ).astype(f32)
    grad_gate = pair_back[..., :units].transpose(1, 0, 2).reshape(block, spots * units)
    grad_up = pair_back[..., units:].transpose(1, 0, 2).reshape(block, spots * units)
    down_back = lax.all_to_all(grad_down.reshape(spots, block, units), plane, 0, 0, tiled=True)
    grad_down = down_back.transpose(0, 2, 1).reshape(spots * units, block).astype(f32)
    mid_part = jnp.sum(grad_gate * w_gate.astype(f32) + grad_up * w_up.astype(f32), axis=1)
    mid_part = mid_part.reshape(2, share)
    mid_keep = lax.dynamic_index_in_dim(mid_part, own_row, 0, False)
    mid_give = lax.dynamic_index_in_dim(mid_part, 1 - own_row, 0, False)
    grad_mid_gain = mid_keep + swap_row(mid_give)

    mixer_back = lax.all_to_all(
        grad_mixer.reshape(members, share, 4 * wide), group, 0, 0, tiled=True
    ).astype(f32)
    mixer_back = mixer_back.reshape(spots, 2, share, 4, heads, width).transpose(3, 2, 1, 4, 0, 5)
    mixer_back = mixer_back.reshape(4, share, features)
    grad_first_gain = jnp.zeros((share,), f32)
    for place, weight in enumerate(mixer_weights):
        grad_first_gain += jnp.sum(mixer_back[place] * weight.astype(f32), axis=1)

    bias_placed = jnp.zeros((2, heads, spots, width), f32)
    bias_placed = lax.dynamic_update_slice(
        bias_placed, bias_part.reshape(1, heads, 1, width), (own_row, 0, own_spot, 0)
    )
    bias_back = lax.all_to_all(
        bias_placed.reshape(groups * members, share), everywhere, 0, 0, tiled=True
    )
    grad_bias = jnp.sum(bias_back, axis=0)

    return (
        block_output.reshape(block_input.shape),
        input_grad,
        mixer_back[0] * first_gain,
        mixer_back[1] * first_gain,
        mixer_back[2] * first_gain,
        mixer_back[3] * first_gain,
        grad_out * head_gain,
        grad_gate * mid_gain,
        grad_up * mid_gain,
        grad_down,
        grad_first_gain,
        grad_mid_gain,
        grad_head_gain,
        grad_bias,
    )


def solution(mesh):
    count, rows = mesh.devices.shape
    folded = Mesh(mesh.devices.reshape(count // 4, 2, 2, rows), everywhere)
    seq = ("z", "y", "x")
    token_spec = P("row", seq, None)
    matrix_spec = P(everywhere, None)
    vector_spec = P(everywhere)
    wide_spec = P(seq, "row")
    tall_spec = P("row", seq)
    in_specs = (
        (token_spec, token_spec, P("row", None))
        + (matrix_spec,) * 5
        + (wide_spec, wide_spec, tall_spec)
        + (vector_spec,) * 4
    )
    out_specs = (
        (token_spec, token_spec)
        + (matrix_spec,) * 5
        + (wide_spec, wide_spec, tall_spec)
        + (vector_spec,) * 4
    )
    return jax.shard_map(
        on_device, mesh=folded, in_specs=in_specs, out_specs=out_specs, check_vma=False
    )
```

time: 4100 us -> 887 us (0.22)
  waiting for transfers between devices: 3410 us -> 327 us
  matrix products: 294 us -> 158 us
  starting transfers between devices: 0.88 us -> 110 us
  blocking collectives: 125 us -> 20.6 us
  other arithmetic: 158 us -> 65.4 us
  Pallas kernels: 0 us -> 71.1 us
    reduce_scatter x10 -> x4, waiting for transfers between devices: 2100 us -> 0.03 us  [the longest x3 0.02 us: spread(): lax.psum_scatter(partial.astype(bf16), 'z', scatter_dimension=0, tiled=True)]
    all_gather x12 -> x4, waiting for transfers between devices: 1310 us -> 7.72 us  [the longest x1 7.71 us: on_device(): lax.all_gather(scaled.reshape(members * share, 4 * wide), 'z', axis=0, ti...]
    ppermute x0 -> x71, waiting for transfers between devices: none -> 274 us  [the longest x16 131 us: swap_x(): return lax.ppermute(a, 'x', swap)]
    dot_general x36 -> x20, matrix products: 294 us -> 158 us  [the longest x6 58.8 us: times(): return jnp.dot(left, right, preferred_element_type=f32)]
    another operation x4 -> x6, other arithmetic: 90.5 us -> 3.28 us  [the longest x3 90.1 us: forget_terms(): log_decay = jnp.cumsum(jnp.log(forget_gate), axis=1)]
    unnamed x2 -> x0, blocking collectives: 82.6 us -> none
    ppermute x0 -> x71, starting transfers between devices: none -> 78.3 us  [the longest x10 34 us: relay(): parts = jax.tree.map(lambda a: lax.ppermute(a, 'z', pairs), parts)]
    pallas_call x0 -> x4, Pallas kernels: none -> 71.1 us  [local_call(): pl.pallas_call(kernel, grid_spec=pltpu.PrefetchScalarGridSpec(num_scalar_...]
  transfers between devices with their start and end apart: 22 -> 86, of which waited for: 19 -> 40; matrix products, arithmetic and copies ran while one was open for 11% -> 31% of each run, Pallas kernels for 0% -> 8%
where the time goes in v1:
time: 887 us; the launch traced here: 876 us
  waiting for transfers between devices  327 us (37%)
  matrix products  158 us (18%)
  starting transfers between devices  110 us (12%)
  local copies, waits for them, and re-layouts  108 us (12%)
  Pallas kernels  71.1 us (8%)
  other arithmetic  65.4 us (7%)
  blocking collectives  20.6 us (2%)
  between operations  16.3 us (2%)
    ppermute x16, waiting for transfers between devices, swap_x(): return lax.ppermute(a, 'x', swap)  131 us
    ppermute x10, waiting for transfers between devices, relay(): parts = jax.tree.map(lambda a: lax.ppermute(a, 'z', pairs), parts)  107 us
    pallas_call x4, Pallas kernels, local_call(): pl.pallas_call(kernel, grid_spec=pltpu.PrefetchScalarGridSpec(num_scalar_...  71.1 us
    unnamed x175, local copies, waits for them, and re-layouts  64.6 us
    dot_general x6, matrix products, times(): return jnp.dot(left, right, preferred_element_type=f32)  58.8 us
    dot_general x9, matrix products, times_transpose(): lax.dot_general(left, right, (NT, ((), ())), preferred_element_type=f32)  57.4 us
    dot_general x5, matrix products, contract_rows(): lax.dot_general(left, right, (TN, ((), ())), preferred_element_type=f32)  41.5 us
    ppermute x10, starting transfers between devices, relay(): parts = jax.tree.map(lambda a: lax.ppermute(a, 'z', pairs), parts)  34 us
  transfers between devices with their start and end apart: 86, of which 40 were waited for; matrix products, arithmetic and copies ran while one was open for 31% of the time, Pallas kernels for 8%

profile of v1, /device:TPU:0, one launch (start us, length us, event | category | flops | bytes accessed | tf_op | source)
XLA Modules:
  0.0 876.3 jit_solution(4002015392504125255)
XLA Ops:
  13.5 20.6 %all_to_all.45 = bf16[8,64,1024]{2,1,0:T(8,128)(2,1)} all-to-all(bf16[8,64,1024]{2,1,0:T(8,128)(2,1)S(1)} %reshape.323), channel_id=1, replica_groups=mesh['z'=4,'y'=2,'x'=2,'row'=2] {'y','x','row'}, dimensions={0} | all-to-all | bytes 2097152 | tf_op jit(solution)/shard_map/all_to_all | solution.py:404
  48.9 13.5 %all-to-all-done.1 = f32[32,1,64]{2,1,0:T(1,128)S(1)} async-done(((f32[32,1,64]{2,1,0:T(1,128)}), f32[32,1,64]{2,1,0:T(1,128)S(1)}, u32[]{:S(2)}, u32[]{:S(2)}) %all-to-all-start.1) | async-done | bytes 8224 | tf_op jit(solution)/shard_map/all_to_all | solution.py:410
  114.7 12.5 %fusion.84 = f32[2048,1024]{1,0:T(8,128)S(1)} fusion(bf16[2048,2048]{1,0:T(8,128)(2,1)} %constant_dynamic-update-slice_fusion, bf16[2048,1024]{1,0:T(8,128)(2,1)} %all-gather.6.cloned.1.call-done), kind=kOutput, calls=%fused_computation.235 | convolution fusion | flops 8589934592 | bytes 20971520 | tf_op jit(solution)/shard_map/dot_general | solution.py:352
  127.2 12.4 %shard_map.254 = (f32[4,2,128,128]{3,2,1,0:T(8,128)S(1)}, f32[4,1,256]{2,1,0:T(1,128)S(1)}) custom-call(s32[2]{0:T(128)S(1)} %pad_add_fusion.1.at_ref, s32[4,4]{1,0:T(4,128)S(1)} %pad_add_fusion.docs_ref, f32[8,2,128,1024]{3,2,1,0:T(8,128)S(1)} %bitcast.261, f32[8,2,128,1024]{3,2,1,0:T(8,128)S(1)} %bitcast.262, f32[1,256]{1,0:T(1,128)S(1)} %fusion.73.bias_ref), custom_call_target="tpu_custom_call" | custom-call | tf_op jit(solution)/shard_map/pallas_call | solution.py:327
  140.9 11.4 %collective-permute-done.10 = f32[4,2,128,128]{3,2,1,0:T(8,128)S(1)} collective-permute-done((f32[4,2,128,128]{3,2,1,0:T(8,128)S(1)}, f32[4,2,128,128]{3,2,1,0:T(8,128)S(1)}, u32[]{:S(2)}, u32[]{:S(2)}) %collective-permute-start.10) | collective-permute-done | bytes 524320 | tf_op jit(solution)/shard_map/ppermute | solution.py:68
  161.6 18.1 %collective-permute-done.12 = f32[4,2,128,128]{3,2,1,0:T(8,128)} collective-permute-done((f32[4,2,128,128]{3,2,1,0:T(8,128)S(1)}, f32[4,2,128,128]{3,2,1,0:T(8,128)}, u32[]{:S(2)}, u32[]{:S(2)}) %collective-permute-start.12) | collective-permute-done | bytes 524320 | tf_op jit(solution)/shard_map/ppermute | solution.py:68
  179.6 12.6 %collective-permute-start.14 = (f32[4,2,128,128]{3,2,1,0:T(8,128)}, f32[4,2,128,128]{3,2,1,0:T(8,128)S(1)}, u32[]{:S(2)}, u32[]{:S(2)}) collective-permute-start(f32[4,2,128,128]{3,2,1,0:T(8,128)} %collective-permute-done.12), channel_id=1, source_target_pairs={{0,8},{8,16},{16,24},{1,9},{9,17},{17,25},{2,10},{10,18},{18,26},{... | collective-permute-start | bytes 1572872 | tf_op jit(solution)/shard_map/ppermute | solution.py:68
  199.1 16.4 %collective-permute-done.13 = f32[4,2,1,128]{3,1,0,2:T(2,128)S(1)} collective-permute-done((f32[4,2,1,128]{3,1,0,2:T(2,128)S(1)}, f32[4,2,1,128]{3,1,0,2:T(2,128)S(1)}, u32[]{:S(2)}, u32[]{:S(2)}) %collective-permute-start.13) | collective-permute-done | bytes 4128 | tf_op jit(solution)/shard_map/ppermute | solution.py:68
  220.1 18.8 %shard_map.255 = (f32[8,2,128,256]{3,2,1,0:T(8,128)S(1)}, bf16[8,2,128,256]{3,2,1,0:T(8,128)(2,1)S(1)}, f32[4,4,2,128,128]{4,3,2,1,0:T(8,128)S(1)}) custom-call(s32[2]{0:T(128)S(1)} %pad_add_fusion.1.at_ref, s32[4,4]{1,0:T(4,128)S(1)} %pad_add_fusion.docs_ref, f32[8,2,128,1024]{3,2,1,0:T(8,128)S(1)} %bitcast.264, f32[1,256]{1,0:T(1,128)S(1)} %fusion.73.bias_ref, ...), custom_call_target="tpu_custom_call" | custom-call | tf_op jit(solution)/shard_map/pallas_call | solution.py:327
  263.8 14.6 %all-to-all-done.3 = bf16[4,128,704]{1,2,0:T(8,128)(2,1)} async-done(((bf16[4,128,704]{1,2,0:T(8,128)(2,1)}), bf16[4,128,704]{1,2,0:T(8,128)(2,1)}, u32[]{:S(2)}, u32[]{:S(2)}) %all-to-all-start.3) | async-done | bytes 720928 | tf_op jit(solution)/shard_map/all_to_all | solution.py:448
  302.6 14.3 %collective-permute-done.17 = bf16[2,256,1024]{2,1,0:T(8,128)(2,1)S(1)} collective-permute-done((bf16[2,256,1024]{2,1,0:T(8,128)(2,1)S(1)}, bf16[2,256,1024]{2,1,0:T(8,128)(2,1)S(1)}, u32[]{:S(2)}, u32[]{:S(2)}) %collective-permute-start.17) | collective-permute-done | bytes 1048608 | tf_op jit(solution)/shard_map/ppermute | solution.py:24
  343.1 14.0 %collective-permute-done.22 = bf16[256,2048]{1,0:T(8,128)(2,1)S(1)} collective-permute-done((bf16[256,2048]{1,0:T(8,128)(2,1)S(1)}, bf16[256,2048]{1,0:T(8,128)(2,1)S(1)}, u32[]{:S(2)}, u32[]{:S(2)}) %collective-permute-start.22) | collective-permute-done | bytes 1048608 | tf_op jit(solution)/shard_map/ppermute | solution.py:28
  376.4 13.1 %fusion.3 = f32[2048,704]{0,1:T(8,128)} fusion(bf16[2048,2048]{1,0:T(8,128)(2,1)} %constant_dynamic-update-slice_fusion.10, bf16[2048,1408]{1,0:T(8,128)(2,1)} %all-gather.8.cloned.1.call-done), kind=kOutput, calls=%fused_computation.21 | convolution fusion | flops 5905580032 | bytes 17301504 | tf_op jit(solution)/shard_map/dot_general | solution.py:352
  389.5 10.3 %fusion.9 = f32[2048,704]{0,1:T(8,128)} fusion(bf16[2048,2048]{1,0:T(8,128)(2,1)} %constant_dynamic-update-slice_fusion.10, bf16[2048,1408]{1,0:T(8,128)(2,1)S(1)} %copy-done.55), kind=kOutput, calls=%fused_computation.27 | convolution fusion | flops 5905580032 | bytes 17301504 | tf_op jit(solution)/shard_map/dot_general | solution.py:352
  399.8 15.6 %multiply_convert_fusion = (bf16[2048,704]{0,1:T(8,128)(2,1)}, bf16[2048,704]{0,1:T(8,128)(2,1)}, bf16[2048,704]{0,1:T(8,128)(2,1)S(1)}) fusion(f32[2048,704]{0,1:T(8,128)} %fusion.9, f32[2048,704]{0,1:T(8,128)} %fusion.3, bf16[2048,2048]{1,0:T(8,128)(2,1)} %constant_dynamic-update-slice_fusion.20, bf16[2048,704]{0,1:T(8,128)(2,1)} %all-gather.10.cloned.1.call-done), kind=kOutput, calls=%fused_computation.6 | convolution fusion | flops 5927206912 | bytes 31457280 | tf_op jit(solution)/shard_map/dot_general | solution.py:352
  417.1 11.0 %convolution_convert_fusion.4 = bf16[2048,704]{0,1:T(8,128)(2,1)} fusion(bf16[2048,704]{0,1:T(8,128)(2,1)S(1)} %get-tuple-element.58, bf16[2048,2048]{1,0:T(8,128)(2,1)} %constant_dynamic-update-slice_fusion.20), kind=kOutput, calls=%fused_computation.15 | convolution fusion | flops 5907021824 | bytes 14155776 | tf_op jit(solution)/shard_map/dot_general | solution.py:344
  434.2 9.0 %add_convert_fusion = bf16[1024,2048]{1,0:T(8,128)(2,1)} fusion(f32[1024,2048]{1,0:T(8,128)S(1)} %fusion.5, bf16[2048,1408]{1,0:T(8,128)(2,1)} %all-gather.8.cloned.1.call-done, bf16[2048,704]{0,1:T(8,128)(2,1)S(1)} %copy-done.60), kind=kOutput, calls=%fused_computation.2 | convolution fusion | flops 2956984320 | bytes 17170432 | tf_op jit(solution)/shard_map/dot_general | solution.py:348
  443.7 8.7 convolution_convert_fusion.5
  470.4 8.6 convert_add_fusion.1
  482.3 22.7 %collective-permute-done.46 = bf16[2,256,1024]{2,1,0:T(8,128)(2,1)S(1)} collective-permute-done((bf16[2,256,1024]{2,1,0:T(8,128)(2,1)S(1)}, bf16[2,256,1024]{2,1,0:T(8,128)(2,1)S(1)}, u32[]{:S(2)}, u32[]{:S(2)}) %collective-permute-start.46) | collective-permute-done | bytes 1048608 | tf_op jit(solution)/shard_map/ppermute | solution.py:24
  509.5 11.0 %collective-permute-done.49 = bf16[256,1024]{1,0:T(8,128)(2,1)S(1)} collective-permute-done((bf16[256,1024]{1,0:T(8,128)(2,1)S(1)}, bf16[256,1024]{1,0:T(8,128)(2,1)S(1)}, u32[]{:S(2)}, u32[]{:S(2)}) %collective-permute-start.49) | collective-permute-done | bytes 524320 | tf_op jit(solution)/shard_map/ppermute | solution.py:24
  531.3 16.1 %collective-permute-done.50 = bf16[256,2048]{1,0:T(8,128)(2,1)S(1)} collective-permute-done((bf16[256,2048]{1,0:T(8,128)(2,1)S(1)}, bf16[256,2048]{1,0:T(8,128)(2,1)S(1)}, u32[]{:S(2)}, u32[]{:S(2)}) %collective-permute-start.50) | collective-permute-done | bytes 1048608 | tf_op jit(solution)/shard_map/ppermute | solution.py:24
  550.7 15.7 %collective-permute-done.60 = f32[4,2,1,128]{3,1,0,2:T(2,128)S(1)} collective-permute-done((f32[4,2,1,128]{3,1,0,2:T(2,128)S(1)}, f32[4,2,1,128]{3,1,0,2:T(2,128)S(1)}, u32[]{:S(2)}, u32[]{:S(2)}) %collective-permute-start.60) | collective-permute-done | bytes 4128 | tf_op jit(solution)/shard_map/ppermute | solution.py:68
  574.6 12.4 %shard_map.256 = f32[4,2,128,128]{3,2,1,0:T(8,128)S(1)} custom-call(s32[2]{0:T(128)S(1)} %pad_add_fusion.1.at_ref, s32[4,4]{1,0:T(4,128)S(1)} %pad_add_fusion.docs_ref, f32[8,2,128,1024]{3,2,1,0:T(8,128)S(1)} %bitcast.267, f32[8,2,128,1024]{3,2,1,0:T(8,128)S(1)} %bitcast.268, f32[8,2,128,1024]{3,2,1,0:T(8,128)S(1)} %bitcast.269, ...), custom_call_target="tpu_custom_call" | custom-call | tf_op jit(solution)/shard_map/pallas_call | solution.py:327
  591.0 25.0 %collective-permute-done.59 = f32[4,2,128,128]{3,2,1,0:T(8,128)S(1)} collective-permute-done((f32[4,2,128,128]{3,2,1,0:T(8,128)S(1)}, f32[4,2,128,128]{3,2,1,0:T(8,128)S(1)}, u32[]{:S(2)}, u32[]{:S(2)}) %collective-permute-start.59) | collective-permute-done | bytes 524320 | tf_op jit(solution)/shard_map/ppermute | solution.py:68
  634.5 16.9 %collective-permute-done.63 = f32[4,2,128,128]{3,2,1,0:T(8,128)} collective-permute-done((f32[4,2,128,128]{3,2,1,0:T(8,128)}, f32[4,2,128,128]{3,2,1,0:T(8,128)}, u32[]{:S(2)}, u32[]{:S(2)}) %collective-permute-start.63) | collective-permute-done | bytes 524320 | tf_op jit(solution)/shard_map/ppermute | solution.py:68
  656.1 27.6 %shard_map.257 = (bf16[8,2,128,1024]{3,2,1,0:T(8,128)(2,1)S(1)}, f32[1,256]{1,0:T(1,128)S(1)}) custom-call(s32[2]{0:T(128)S(1)} %pad_add_fusion.1.at_ref, s32[4,4]{1,0:T(4,128)S(1)} %pad_add_fusion.docs_ref, f32[8,2,128,1024]{3,2,1,0:T(8,128)} %bitcast.263, f32[8,2,128,256]{3,2,1,0:T(8,128)S(1)} %get-tuple-element.24.out_ref, ...), custom_call_target="tpu_custom_call" | custom-call | tf_op jit(solution)/shard_map/pallas_call | solution.py:327
  692.9 10.9 %convolution_convert_fusion.3 = bf16[2048,1024]{1,0:T(8,128)(2,1)} fusion(bf16[2048,2048]{1,0:T(8,128)(2,1)S(1)} %bitcast.323, bf16[2048,1024]{1,0:T(8,128)(2,1)S(1)} %bitcast.271), kind=kOutput, calls=%fused_computation.14 | convolution fusion | flops 8592031744 | bytes 16777216 | tf_op jit(solution)/shard_map/dot_general | solution.py:344
  708.2 22.6 %collective-permute-done.32 = bf16[2,256,1024]{2,1,0:T(8,128)(2,1)S(1)} collective-permute-done((bf16[2,256,1024]{2,1,0:T(8,128)(2,1)S(1)}, bf16[2,256,1024]{2,1,0:T(8,128)(2,1)S(1)}, u32[]{:S(2)}, u32[]{:S(2)}) %collective-permute-start.32) | collective-permute-done | bytes 1048608 | tf_op jit(solution)/shard_map/ppermute | solution.py:24
  775.6 8.6 convert_add_fusion
  799.7 16.7 %collective-permute-done.65 = bf16[2,256,1024]{2,1,0:T(8,128)(2,1)} collective-permute-done((bf16[2,256,1024]{2,1,0:T(8,128)(2,1)}, bf16[2,256,1024]{2,1,0:T(8,128)(2,1)}, u32[]{:S(2)}, u32[]{:S(2)}) %collective-permute-start.65) | collective-permute-done | bytes 1048608 | tf_op jit(solution)/shard_map/ppermute | solution.py:24
  850.3 8.8 %all-to-all-done.4 = bf16[8,64,1024]{2,1,0:T(8,128)(2,1)} async-done(((bf16[8,64,1024]{2,1,0:T(8,128)(2,1)}), bf16[8,64,1024]{2,1,0:T(8,128)(2,1)}, u32[]{:S(2)}, u32[]{:S(2)}) %all-to-all-start.4) | async-done | bytes 1048608 | tf_op jit(solution)/shard_map/all_to_all | solution.py:651
  (467 shorter events, 389.4 us)
Async XLA Ops:
  7.2 107.5 %all-gather.6.cloned.1.call-start = ((), (), s32[]{:S(2)}) async-start(), calls=%async_computation.12 | async-start | bytes 5242880 | tf_op jit(solution)/shard_map/all_gather | solution.py:405
  36.6 34.2 %collective-permute-start.2 = (bf16[256,2048]{1,0:T(8,128)(2,1)}, bf16[256,2048]{1,0:T(8,128)(2,1)}, u32[]{:S(2)}, u32[]{:S(2)}) collective-permute-start(bf16[256,2048]{1,0:T(8,128)(2,1)} %get-tuple-element.105), channel_id=1, source_target_pairs={{0,4},{4,0},{1,5},{5,1},{2,6},{6,2},{3,7},{7,3},{8,12},{12,8},{9,1... | collective-permute-start | bytes 3145736 | tf_op jit(solution)/shard_map/ppermute | solution.py:28
  37.2 37.0 %collective-permute-start.1 = (bf16[256,2048]{1,0:T(8,128)(2,1)}, bf16[256,2048]{1,0:T(8,128)(2,1)}, u32[]{:S(2)}, u32[]{:S(2)}) collective-permute-start(bf16[256,2048]{1,0:T(8,128)(2,1)} %get-tuple-element.105), channel_id=1, source_target_pairs={{0,2},{2,0},{1,3},{3,1},{4,6},{6,4},{5,7},{7,5},{8,10},{10,8},{9,1... | collective-permute-start | bytes 3145736 | tf_op jit(solution)/shard_map/ppermute | solution.py:24
  44.2 113.2 %all-gather.12.cloned.1.call-start = ((), (), s32[]{:S(2)}) async-start(), calls=%async_computation.19 | async-start | bytes 1310720 | tf_op jit(solution)/shard_map/all_gather | solution.py:419
  66.7 309.7 %all-gather.8.cloned.1.call-start = ((), (), s32[]{:S(2)}) async-start(), calls=%async_computation.13 | async-start | bytes 7208960 | tf_op jit(solution)/shard_map/all_gather | solution.py:449
  66.8 34.0 %collective-permute-start.5 = (bf16[256,2048]{1,0:T(8,128)(2,1)}, bf16[256,2048]{1,0:T(8,128)(2,1)S(1)}, u32[]{:S(2)}, u32[]{:S(2)}) collective-permute-start(bf16[256,2048]{1,0:T(8,128)(2,1)} %get-tuple-element.105), channel_id=1, source_target_pairs={{0,1},{1,0},{2,3},{3,2},{4,5},{5,4},{6,7},{7,6},{8,9},{9,8},{10,11... | collective-permute-start | bytes 3145736 | tf_op jit(solution)/shard_map/ppermute | solution.py:32
  152.3 27.4 %collective-permute-start.12 = (f32[4,2,128,128]{3,2,1,0:T(8,128)S(1)}, f32[4,2,128,128]{3,2,1,0:T(8,128)}, u32[]{:S(2)}, u32[]{:S(2)}) collective-permute-start(f32[4,2,128,128]{3,2,1,0:T(8,128)S(1)} %collective-permute-done.10), channel_id=1, source_target_pairs={{0,8},{8,16},{16,24},{1,9},{9,17},{17,25},{2,10},{10,18},{18,26},{... | collective-permute-start | bytes 1572872 | tf_op jit(solution)/shard_map/ppermute | solution.py:68
  158.5 33.7 %collective-permute-start.15 = (bf16[2,64,2048]{2,1,0:T(8,128)(2,1)S(1)}, bf16[2,64,2048]{2,1,0:T(8,128)(2,1)S(1)}, u32[]{:S(2)}, u32[]{:S(2)}) collective-permute-start(bf16[2,64,2048]{2,1,0:T(8,128)(2,1)S(1)} %dynamic-slice_bitcast_fusion.1), channel_id=1, source_target_pairs={{0,1},{1,0},{2,3},{3,2},{4,5},{5,4},{6,7},{7,6},{8,9},{9,8},{10,11... | collective-permute-start | bytes 1572872 | tf_op jit(solution)/shard_map/ppermute | solution.py:32
  158.6 34.8 %collective-permute-start.11 = (f32[4,2,1,128]{3,1,0,2:T(2,128)S(1)}, f32[4,2,1,128]{3,1,0,2:T(2,128)S(1)}, u32[]{:S(2)}, u32[]{:S(2)}) collective-permute-start(f32[4,2,1,128]{3,1,0,2:T(2,128)S(1)} %bitcast.273), channel_id=1, source_target_pairs={{0,8},{8,16},{16,24},{1,9},{9,17},{17,25},{2,10},{10,18},{18,26},{... | collective-permute-start | bytes 12296 | tf_op jit(solution)/shard_map/ppermute | solution.py:68
  179.6 35.9 %collective-permute-start.14 = (f32[4,2,128,128]{3,2,1,0:T(8,128)}, f32[4,2,128,128]{3,2,1,0:T(8,128)S(1)}, u32[]{:S(2)}, u32[]{:S(2)}) collective-permute-start(f32[4,2,128,128]{3,2,1,0:T(8,128)} %collective-permute-done.12), channel_id=1, source_target_pairs={{0,8},{8,16},{16,24},{1,9},{9,17},{17,25},{2,10},{10,18},{18,26},{... | collective-permute-start | bytes 1572872 | tf_op jit(solution)/shard_map/ppermute | solution.py:68
  243.4 93.9 %collective-permute-start.40 = (bf16[256,2048]{1,0:T(8,128)(2,1)}, bf16[256,2048]{1,0:T(8,128)(2,1)}, u32[]{:S(2)}, u32[]{:S(2)}) collective-permute-start(bf16[256,2048]{1,0:T(8,128)(2,1)} %bitcast.50), channel_id=1, source_target_pairs={{0,1},{1,0},{2,3},{3,2},{4,5},{5,4},{6,7},{7,6},{8,9},{9,8},{10,11... | collective-permute-start | bytes 3145736 | tf_op jit(solution)/shard_map/ppermute | solution.py:32
  243.9 36.7 %collective-permute-start.37 = (bf16[256,2048]{1,0:T(8,128)(2,1)}, bf16[256,2048]{1,0:T(8,128)(2,1)}, u32[]{:S(2)}, u32[]{:S(2)}) collective-permute-start(bf16[256,2048]{1,0:T(8,128)(2,1)} %bitcast.50), channel_id=1, source_target_pairs={{0,4},{4,0},{1,5},{5,1},{2,6},{6,2},{3,7},{7,3},{8,12},{12,8},{9,1... | collective-permute-start | bytes 3145736 | tf_op jit(solution)/shard_map/ppermute | solution.py:28
  245.5 37.7 %collective-permute-start.36 = (bf16[256,2048]{1,0:T(8,128)(2,1)}, bf16[256,2048]{1,0:T(8,128)(2,1)}, u32[]{:S(2)}, u32[]{:S(2)}) collective-permute-start(bf16[256,2048]{1,0:T(8,128)(2,1)} %bitcast.50), channel_id=1, source_target_pairs={{0,2},{2,0},{1,3},{3,1},{4,6},{6,4},{5,7},{7,5},{8,10},{10,8},{9,1... | collective-permute-start | bytes 3145736 | tf_op jit(solution)/shard_map/ppermute | solution.py:24
  246.9 31.5 %all-to-all-start.3 = ((bf16[4,128,704]{1,2,0:T(8,128)(2,1)}), bf16[4,128,704]{1,2,0:T(8,128)(2,1)}, u32[]{:S(2)}, u32[]{:S(2)}) async-start(bf16[4,128,704]{1,2,0:T(8,128)(2,1)} %bitcast.321), calls=%async_computation.3 | async-start | bytes 1441792 | tf_op jit(solution)/shard_map/all_to_all | solution.py:448
  251.1 148.7 %all-gather.10.cloned.1.call-start = ((), (), s32[]{:S(2)}) async-start(), calls=%async_computation.14 | async-start | bytes 3604480 | tf_op jit(solution)/shard_map/all_gather | solution.py:452
  259.5 40.9 %collective-permute-start.19 = (bf16[2,256,1024]{2,1,0:T(8,128)(2,1)}, bf16[2,256,1024]{2,1,0:T(8,128)(2,1)}, u32[]{:S(2)}, u32[]{:S(2)}) collective-permute-start(bf16[2,256,1024]{2,1,0:T(8,128)(2,1)} %slice_bitcast_fusion.21), channel_id=1, source_target_pairs={{0,4},{4,0},{1,5},{5,1},{2,6},{6,2},{3,7},{7,3},{8,12},{12,8},{9,1... | collective-permute-start | bytes 3145736 | tf_op jit(solution)/shard_map/ppermute | solution.py:28
  280.5 459.6 %reduce-scatter.11.cloned.1.call-start = ((), (), s32[]{:S(2)}) async-start(), calls=%async_computation.18 | async-start | bytes 3604480 | tf_op jit(solution)/shard_map/reduce_scatter | solution.py:553
  281.6 54.3 %collective-permute-start.39 = (bf16[128,2048]{1,0:T(8,128)(2,1)S(1)}, bf16[128,2048]{1,0:T(8,128)(2,1)S(1)}, u32[]{:S(2)}, u32[]{:S(2)}) collective-permute-start(bf16[128,2048]{1,0:T(8,128)(2,1)S(1)} %slice.321), channel_id=1, source_target_pairs={{0,2},{2,0},{1,3},{3,1},{4,6},{6,4},{5,7},{7,5},{8,10},{10,8},{9,1... | collective-permute-start | bytes 1572872 | tf_op jit(solution)/shard_map/ppermute | solution.py:24
  284.3 36.1 %collective-permute-start.38 = (bf16[128,2048]{1,0:T(8,128)(2,1)S(1)}, bf16[128,2048]{1,0:T(8,128)(2,1)S(1)}, u32[]{:S(2)}, u32[]{:S(2)}) collective-permute-start(bf16[128,2048]{1,0:T(8,128)(2,1)S(1)} %slice.320), channel_id=1, source_target_pairs={{0,4},{4,0},{1,5},{5,1},{2,6},{6,2},{3,7},{7,3},{8,12},{12,8},{9,1... | collective-permute-start | bytes 1572872 | tf_op jit(solution)/shard_map/ppermute | solution.py:28
  287.6 29.3 %collective-permute-start.17 = (bf16[2,256,1024]{2,1,0:T(8,128)(2,1)S(1)}, bf16[2,256,1024]{2,1,0:T(8,128)(2,1)S(1)}, u32[]{:S(2)}, u32[]{:S(2)}) collective-permute-start(bf16[2,256,1024]{2,1,0:T(8,128)(2,1)S(1)} %slice_bitcast_fusion.23), channel_id=1, source_target_pairs={{0,2},{2,0},{1,3},{3,1},{4,6},{6,4},{5,7},{7,5},{8,10},{10,8},{9,1... | collective-permute-start | bytes 3145736 | tf_op jit(solution)/shard_map/ppermute | solution.py:24
  300.4 40.8 %collective-permute-start.42 = (bf16[256,2048]{1,0:T(8,128)(2,1)}, bf16[256,2048]{1,0:T(8,128)(2,1)S(1)}, u32[]{:S(2)}, u32[]{:S(2)}) collective-permute-start(bf16[256,2048]{1,0:T(8,128)(2,1)} %collective-permute-done.37), channel_id=1, source_target_pairs={{0,1},{1,0},{2,3},{3,2},{4,5},{5,4},{6,7},{7,6},{8,9},{9,8},{10,11... | collective-permute-start | bytes 3145736 | tf_op jit(solution)/shard_map/ppermute | solution.py:32
  343.1 28.4 %collective-permute-start.25 = (bf16[256,2048]{1,0:T(8,128)(2,1)S(1)}, bf16[256,2048]{1,0:T(8,128)(2,1)S(1)}, u32[]{:S(2)}, u32[]{:S(2)}) collective-permute-start(bf16[256,2048]{1,0:T(8,128)(2,1)S(1)} %get-tuple-element.107), channel_id=1, source_target_pairs={{0,1},{1,0},{2,3},{3,2},{4,5},{5,4},{6,7},{7,6},{8,9},{9,8},{10,11... | collective-permute-start | bytes 3145736 | tf_op jit(solution)/shard_map/ppermute | solution.py:32
  428.1 336.4 %reduce-scatter.9.cloned.1.call-start = ((), (), s32[]{:S(2)}) async-start(), calls=%async_computation.17 | async-start | bytes 7208960 | tf_op jit(solution)/shard_map/reduce_scatter | solution.py:553
  464.1 359.9 %reduce-scatter.7.cloned.1.call-start = ((), (), s32[]{:S(2)}) async-start(), calls=%async_computation.16 | async-start | bytes 1310720 | tf_op jit(solution)/shard_map/reduce_scatter | solution.py:622
  531.3 86.0 %collective-permute-start.31 = (bf16[1024,2048]{1,0:T(8,128)(2,1)}, bf16[1024,2048]{1,0:T(8,128)(2,1)}, u32[]{:S(2)}, u32[]{:S(2)}) collective-permute-start(bf16[1024,2048]{1,0:T(8,128)(2,1)} %convolution_convert_fusion), channel_id=1, source_target_pairs={{0,1},{1,0},{2,3},{3,2},{4,5},{5,4},{6,7},{7,6},{8,9},{9,8},{10,11... | collective-permute-start | bytes 12582920 | tf_op jit(solution)/shard_map/ppermute | solution.py:32
  567.2 67.3 %collective-permute-start.62 = (f32[4,2,1,128]{3,1,0,2:T(2,128)S(1)}, f32[4,2,1,128]{3,1,0,2:T(2,128)S(1)}, u32[]{:S(2)}, u32[]{:S(2)}) collective-permute-start(f32[4,2,1,128]{3,1,0,2:T(2,128)S(1)} %collective-permute-done.60), channel_id=1, source_target_pairs={{8,0},{16,8},{24,16},{9,1},{17,9},{25,17},{10,2},{18,10},{26,18},{... | collective-permute-start | bytes 12296 | tf_op jit(solution)/shard_map/ppermute | solution.py:68
  587.1 29.0 %collective-permute-start.59 = (f32[4,2,128,128]{3,2,1,0:T(8,128)S(1)}, f32[4,2,128,128]{3,2,1,0:T(8,128)S(1)}, u32[]{:S(2)}, u32[]{:S(2)}) collective-permute-start(f32[4,2,128,128]{3,2,1,0:T(8,128)S(1)} %shard_map.256), channel_id=1, source_target_pairs={{8,0},{16,8},{24,16},{9,1},{17,9},{25,17},{10,2},{18,10},{26,18},{... | collective-permute-start | bytes 1572872 | tf_op jit(solution)/shard_map/ppermute | solution.py:68
  590.8 42.5 %collective-permute-start.69 = (bf16[2,64,2048]{2,1,0:T(8,128)(2,1)S(1)}, bf16[2,64,2048]{2,1,0:T(8,128)(2,1)S(1)}, u32[]{:S(2)}, u32[]{:S(2)}) collective-permute-start(bf16[2,64,2048]{2,1,0:T(8,128)(2,1)S(1)} %dynamic-slice_bitcast_fusion), channel_id=1, source_target_pairs={{0,1},{1,0},{2,3},{3,2},{4,5},{5,4},{6,7},{7,6},{8,9},{9,8},{10,11... | collective-permute-start | bytes 1572872 | tf_op jit(solution)/shard_map/ppermute | solution.py:32
  634.5 204.7 %reduce-scatter.5.cloned.1.call-start = ((), (), s32[]{:S(2)}) async-start(), calls=%async_computation.15 | async-start | bytes 5242880 | tf_op jit(solution)/shard_map/reduce_scatter | solution.py:553
  692.9 82.7 %collective-permute-start.64 = (bf16[1024,2048]{1,0:T(8,128)(2,1)}, bf16[1024,2048]{1,0:T(8,128)(2,1)}, u32[]{:S(2)}, u32[]{:S(2)}) collective-permute-start(bf16[1024,2048]{1,0:T(8,128)(2,1)} %convolution_convert_fusion.2), channel_id=1, source_target_pairs={{0,1},{1,0},{2,3},{3,2},{4,5},{5,4},{6,7},{7,6},{8,9},{9,8},{10,11... | collective-permute-start | bytes 12582920 | tf_op jit(solution)/shard_map/ppermute | solution.py:32
  788.6 27.8 %collective-permute-start.65 = (bf16[2,256,1024]{2,1,0:T(8,128)(2,1)}, bf16[2,256,1024]{2,1,0:T(8,128)(2,1)}, u32[]{:S(2)}, u32[]{:S(2)}) collective-permute-start(bf16[2,256,1024]{2,1,0:T(8,128)(2,1)} %slice_bitcast_fusion.11), channel_id=1, source_target_pairs={{0,2},{2,0},{1,3},{3,1},{4,6},{6,4},{5,7},{7,5},{8,10},{10,8},{9,1... | collective-permute-start | bytes 3145736 | tf_op jit(solution)/shard_map/ppermute | solution.py:24
  799.6 32.7 %collective-permute-start.70 = (f32[64]{0:T(128)S(1)}, f32[64]{0:T(128)S(1)}, u32[]{:S(2)}, u32[]{:S(2)}) collective-permute-start(f32[64]{0:T(128)S(1)} %fusion.77), channel_id=1, source_target_pairs={{0,1},{1,0},{2,3},{3,2},{4,5},{5,4},{6,7},{7,6},{8,9},{9,8},{10,11... | collective-permute-start | bytes 776 | tf_op jit(solution)/shard_map/ppermute | solution.py:32
  (123 other events, 1615.6 us)
Sparse Core Ops, SparseCore 0:
  34.2 80.4 all-gather.5
  116.8 26.4 all-gather.11
  145.4 124.5 all-gather.7
  280.6 77.3 all-gather.9
  428.2 73.6 reduce-scatter.10
  504.1 103.6 reduce-scatter.8
  634.6 31.6 reduce-scatter.6
  704.0 77.3 reduce-scatter.4

commit v2 on v1

v2 whole, which is shorter than its diff:
```python
import jax
import jax.numpy as jnp
from jax import lax
from jax.experimental import pallas as pl
from jax.experimental.pallas import tpu as pltpu
from jax.sharding import Mesh, PartitionSpec as P

HEADS = 16

lower_bound = 0.85
span_bound = 1.0 - lower_bound
epsilon = 1e-06
f32 = jnp.float32
bf16 = jnp.bfloat16
swap = ((0, 1), (1, 0))
everywhere = ("z", "y", "x", "row")
group = ("y", "x", "row")
plane = ("y", "x")


def swap_x(a):
    return lax.ppermute(a, "x", swap)


def swap_y(a):
    return lax.ppermute(a, "y", swap)


def swap_row(a):
    return lax.ppermute(a, "row", swap)


def after(value, *others):
    return lax.optimization_barrier((value,) + others)[0]


def join(*groups):
    flat, tree = jax.tree.flatten(groups)
    return jax.tree.unflatten(tree, lax.optimization_barrier(flat))


def gather_first(a):
    return a, swap_x(a), swap_y(a)


def gather_second(a, from_x, from_y):
    half = a.shape[0] // 2
    return a, from_x, from_y, swap_y(from_x[:half]), swap_x(from_y[half:])


def lay_kernel(*refs):
    pieces, out_ref = refs[:-1], refs[-1]
    rows = out_ref.shape[0]
    start = 0
    for ref in pieces:
        block, low = start // rows, start % rows

        @pl.when(pl.program_id(0) == block)
        def _(ref=ref, low=low):
            out_ref[low : low + ref.shape[0], :] = ref[...]

        start += ref.shape[0]


def lay(pieces):
    rows, columns = pieces[0].shape
    total = sum(piece.shape[0] for piece in pieces)
    return pl.pallas_call(
        lay_kernel,
        grid=(total // rows,),
        in_specs=[pl.BlockSpec(piece.shape, lambda step: (0, 0)) for piece in pieces],
        out_specs=pl.BlockSpec((rows, columns), lambda step: (step, 0)),
        out_shape=jax.ShapeDtypeStruct((total, columns), pieces[0].dtype),
        compiler_params=pltpu.CompilerParams(
            dimension_semantics=("arbitrary",), vmem_limit_bytes=48 * 1024 * 1024
        ),
    )(*pieces)


def gather_last(near):
    return lay(near + tuple(swap_row(piece) for piece in near))


def gather_group(a):
    return gather_last(gather_second(*gather_first(a)))


def scatter_first(near, far):
    rows, columns = near.shape
    half = columns // 2
    mine = near.astype(f32) + swap_row(far.astype(bf16)).astype(f32)
    mine = mine.reshape(2, 2, rows // 4, columns)
    left, right = mine[..., :half], mine[..., half:]
    return left[:, 0], right[0], left[:, 1].astype(bf16), right[1].astype(bf16)


def scatter_second(left, right, to_x, to_y):
    return left, right, swap_x(to_x), swap_y(to_y)


def scatter_third(left, right, from_x, from_y):
    left = left + from_x.astype(f32)
    right = right + from_y.astype(f32)
    return left[0], right[0], swap_y(left[1].astype(bf16)), swap_x(right[1].astype(bf16))


def scatter_last(left, right, from_y, from_x):
    return jnp.concatenate([left + from_y.astype(f32), right + from_x.astype(f32)], axis=-1)


def scatter_group(near, far, first=(), second=()):
    state, first = join(scatter_second(*scatter_first(near, far)), first)
    state, second = join(scatter_third(*state), second)
    return scatter_last(*state), *first, *second


def hop(packed, forward):
    count = lax.axis_size("z")
    if forward:
        pairs = [(i, i + 1) for i in range(count - 1)]
    else:
        pairs = [(i + 1, i) for i in range(count - 1)]
    return lax.ppermute(packed, "z", pairs)


def relay(packed, forward):
    got = []
    for _ in range(lax.axis_size("z") - 1):
        packed = hop(packed, forward)
        got.append(packed)
    return got


def pair(values):
    high = values.astype(bf16)
    return high, (values - high.astype(f32)).astype(bf16)


def mm(a, b, dims):
    def dot(left, right):
        return lax.dot_general(left, right, (dims, ((), ())), preferred_element_type=f32)

    return dot(a[0], b[0]) + (dot(a[0], b[1]) + dot(a[1], b[0]))


def split_sum(ones_matrix, values, dims):
    first = values.astype(bf16)
    rest = values - first.astype(f32)
    second = rest.astype(bf16)
    third = (rest - second.astype(f32)).astype(bf16)
    total = lax.dot_general(ones_matrix, first, (dims, ((), ())), preferred_element_type=f32)
    total += lax.dot_general(ones_matrix, second, (dims, ((), ())), preferred_element_type=f32)
    total += lax.dot_general(ones_matrix, third, (dims, ((), ())), preferred_element_type=f32)
    return total


NT = ((1,), (1,))
NN = ((1,), (0,))
TN = ((0,), (0,))


def chunk_masks(docs_ref, row_at, start, size):
    at_row = lax.broadcasted_iota(jnp.int32, (size, size), 0)
    at_col = lax.broadcasted_iota(jnp.int32, (size, size), 1)
    same = at_row >= at_col
    opened = at_row >= 0
    tail = at_row >= 0
    whole = jnp.bool_(True)
    for entry in range(docs_ref.shape[1]):
        place = docs_ref[row_at, entry] - start
        same = same & ~((at_col < place) & (place <= at_row))
        opened = opened & ~((0 <= place) & (place <= at_row))
        tail = tail & ~((at_row < place) & (place <= size - 1))
        whole = whole & ~((0 <= place) & (place <= size - 1))
    return same, opened, tail, whole


def decay_terms(logit, tri):
    forget = lower_bound + span_bound * jax.nn.sigmoid(logit)
    key = span_bound * jax.nn.sigmoid(-logit)
    log_sum = split_sum(tri, jnp.log(forget), NN)
    return forget, key, log_sum


def lower_ones(size):
    at_row = lax.broadcasted_iota(jnp.int32, (size, size), 0)
    at_col = lax.broadcasted_iota(jnp.int32, (size, size), 1)
    return (at_row >= at_col).astype(f32).astype(bf16)


PAD = 16


def pack_state(ref, row, head, state, decay):
    width = state.shape[0]
    high = decay.astype(bf16).astype(f32)
    at_row = lax.broadcasted_iota(jnp.int32, (PAD, width), 0)
    extra = jnp.where(at_row == 0, high, jnp.where(at_row == 1, decay - high, 0.0))
    ref[row, head, :width, :] = state.astype(bf16)
    ref[row, head, width:, :] = extra.astype(bf16)


def unpack_carry(refs, row, head):
    width = refs[0].shape[3]
    carry = None
    for ref in refs[::-1]:
        state = ref[row, head, :width, :].astype(f32)
        if carry is not None:
            extra = ref[row, head, width:, :].astype(f32)
            state = state + (extra[0:1] + extra[1:2]) * carry
        carry = state
    return carry


def state_kernel(at_ref, docs_ref, zv_ref, bias_ref, packed_ref, state, decay):
    rows, size = zv_ref.shape[1:3]
    heads, width = state.shape[1:3]
    half, chunk = pl.program_id(0), pl.program_id(1)
    tri = lower_ones(size)

    @pl.when(chunk == 0)
    def _():
        state[...] = jnp.zeros_like(state)
        decay[...] = jnp.ones_like(decay)

    for row in range(rows):
        _, _, tail, whole = chunk_masks(
            docs_ref, half * rows + row, at_ref[1] + chunk * size, size
        )
        for head in range(heads):
            low = head * width
            logit = zv_ref[0, row, :, low : low + width] + bias_ref[:, low : low + width]
            value = zv_ref[0, row, :, heads * width + low : heads * width + low + width]
            _, key, log_sum = decay_terms(logit, tri)
            last = log_sum[size - 1 : size, :]
            passed = jnp.where(whole, jnp.exp(last), 0.0)
            weighted = jnp.where(tail, key * jnp.exp(last - log_sum), 0.0)
            state[row, head] = state[row, head] * passed + mm(pair(value), pair(weighted), TN)
            decay[row, head] = decay[row, head] * passed

    @pl.when(chunk == pl.num_programs(1) - 1)
    def _():
        for row in range(rows):
            for head in range(heads):
                pack_state(packed_ref, row, head, state[row, head], decay[row, head])


def forward_kernel(half, at_ref, docs_ref, qr_ref, zv_ref, bias_ref, gain_ref, *rest):
    carry_refs, (out_ref, mixed_ref, starts_ref, state) = rest[:-4], rest[-4:]
    rows, size = qr_ref.shape[1:3]
    heads, width = state.shape[1:3]
    chunk = pl.program_id(0)
    tri = lower_ones(size)

    @pl.when(chunk == 0)
    def _():
        for row in range(rows):
            for head in range(heads):
                state[row, head] = unpack_carry(carry_refs, row, head)

    for row in range(rows):
        same, opened, tail, whole = chunk_masks(
            docs_ref, half * rows + row, at_ref[1] + chunk * size, size
        )
        for head in range(heads):
            low = head * width
            high = (heads + head) * width
            query = qr_ref[0, row, :, low : low + width]
            gate = qr_ref[0, row, :, high : high + width]
            logit = zv_ref[0, row, :, low : low + width] + bias_ref[:, low : low + width]
            value = pair(zv_ref[0, row, :, high : high + width])
            _, key, log_sum = decay_terms(logit, tri)
            last = log_sum[size - 1 : size, :]
            lifted = pair(query * jax.nn.sigmoid(query) * jnp.exp(log_sum))
            lowered = pair(key * jnp.exp(-log_sum))
            scores = pair(jnp.where(same, mm(lifted, lowered, NT), 0.0))
            begin = state[row, head]
            starts_ref[0, row, head] = begin
            out = mm(scores, value, NN) + jnp.where(opened, mm(lifted, pair(begin), NT), 0.0)
            passed = jnp.where(whole, jnp.exp(last), 0.0)
            weighted = jnp.where(tail, key * jnp.exp(last - log_sum), 0.0)
            state[row, head] = begin * passed + mm(value, pair(weighted), TN)
            scale = lax.rsqrt(jnp.mean(out * out, axis=-1, keepdims=True) + epsilon)
            normed = out * scale * gain_ref[:, low : low + width]
            out_ref[0, row, :, low : low + width] = out
            mixed_ref[0, row, :, low : low + width] = (
                normed * (gate * jax.nn.sigmoid(gate))
            ).astype(bf16)


def open_kernel(
    at_ref,
    docs_ref,
    qr_ref,
    zv_ref,
    out_ref,
    grad_ref,
    bias_ref,
    gain_ref,
    starts_ref,
    qr_grad_ref,
    low_ref,
    part_ref,
    packed_ref,
    state,
    decay,
):
    rows, size = qr_ref.shape[1:3]
    heads, width = state.shape[1:3]
    half, step = pl.program_id(0), pl.program_id(1)
    chunk = pl.num_programs(1) - 1 - step
    tri = lower_ones(size)

    @pl.when(step == 0)
    def _():
        state[...] = jnp.zeros_like(state)
        decay[...] = jnp.ones_like(decay)

    for row in range(rows):
        same, opened, _, whole = chunk_masks(
            docs_ref, half * rows + row, at_ref[1] + chunk * size, size
        )
        for head in range(heads):
            low = head * width
            high = (heads + head) * width
            query = qr_ref[0, row, :, low : low + width]
            gate = qr_ref[0, row, :, high : high + width]
            logit = zv_ref[0, row, :, low : low + width] + bias_ref[:, low : low + width]
            value = pair(zv_ref[0, row, :, high : high + width])
            out = out_ref[0, row, :, low : low + width]
            grad_mixed = grad_ref[0, row, :, low : low + width] * gain_ref[:, low : low + width]
            _, key, log_sum = decay_terms(logit, tri)
            last = log_sum[size - 1 : size, :]
            rise = jnp.exp(log_sum)
            query_on = jax.nn.sigmoid(query)
            lifted = query * query_on * rise
            lowered = pair(key * jnp.exp(-log_sum))
            gate_on = jax.nn.sigmoid(gate)
            scale = lax.rsqrt(jnp.mean(out * out, axis=-1, keepdims=True) + epsilon)
            normed = out * scale
            grad_normed = grad_mixed * (gate * gate_on)
            grad_out = scale * (
                grad_normed - normed * jnp.mean(grad_normed * normed, axis=-1, keepdims=True)
            )
            grad_low = pair(grad_out)
            grad_scores = pair(jnp.where(same, mm(grad_low, value, NT), 0.0))
            grad_lifted = mm(grad_scores, lowered, NN) + jnp.where(
                opened, mm(grad_low, pair(starts_ref[0, row, head]), NN), 0.0
            )
            grad_query = grad_lifted * rise * query_on * (1.0 + query * (1.0 - query_on))
            grad_gate = grad_mixed * normed * gate_on * (1.0 + gate * (1.0 - gate_on))
            qr_grad_ref[0, row, :, low : low + width] = grad_query.astype(bf16)
            qr_grad_ref[0, row, :, high : high + width] = grad_gate.astype(bf16)
            low_ref[0, row, :, low : low + width] = grad_out
            part_ref[0, row, :, low : low + width] = grad_lifted * lifted
            passed = jnp.where(whole, jnp.exp(last), 0.0)
            state[row, head] = state[row, head] * passed + mm(
                grad_low, pair(jnp.where(opened, lifted, 0.0)), TN
            )
            decay[row, head] = decay[row, head] * passed

    @pl.when(step == pl.num_programs(1) - 1)
    def _():
        for row in range(rows):
            for head in range(heads):
                pack_state(packed_ref, row, head, state[row, head], decay[row, head])


def close_kernel(
    at_ref, docs_ref, kept_ref, qr_ref, zv_ref, low_ref, part_ref, bias_ref, starts_ref, *rest
):
    carry_refs, (zv_grad_ref, bias_grad_ref, state) = rest[:-3], rest[-3:]
    rows, size = qr_ref.shape[1:3]
    heads, width = state.shape[1:3]
    half, step = pl.program_id(0), pl.program_id(1)
    chunk = pl.num_programs(1) - 1 - step
    tri = lower_ones(size)

    @pl.when((step == 0) & (half == 0))
    def _():
        bias_grad_ref[...] = jnp.zeros_like(bias_grad_ref)

    @pl.when(step == 0)
    def _():
        for row in range(rows):
            for head in range(heads):
                state[row, head] = unpack_carry(carry_refs, row, head)

    for row in range(rows):
        same, opened, tail, whole = chunk_masks(
            docs_ref, half * rows + row, at_ref[1] + chunk * size, size
        )
        for head in range(heads):
            low = head * width
            high = (heads + head) * width
            query = qr_ref[0, row, :, low : low + width]
            logit = zv_ref[0, row, :, low : low + width] + bias_ref[:, low : low + width]
            value = pair(zv_ref[0, row, :, high : high + width])
            grad_low = pair(low_ref[0, row, :, low : low + width])
            forget, key, log_sum = decay_terms(logit, tri)
            last = log_sum[size - 1 : size, :]
            fall = jnp.exp(-log_sum)
            remain = jnp.where(tail, jnp.exp(last - log_sum), 0.0)
            lifted = query * jax.nn.sigmoid(query) * jnp.exp(log_sum)
            lowered = key * fall
            weighted = key * remain
            lifted_low = pair(lifted)
            scores = pair(jnp.where(same, mm(lifted_low, pair(lowered), NT), 0.0))
            begin = starts_ref[0, row, head]
            later = state[row, head]
            later_low = pair(later)
            grad_scores = pair(jnp.where(same, mm(grad_low, value, NT), 0.0))
            grad_value = mm(scores, grad_low, TN) + mm(pair(weighted), later_low, NT)
            grad_lowered = mm(grad_scores, lifted_low, TN)
            grad_weighted = mm(value, later_low, NN)
            passed = jnp.where(whole, jnp.exp(last), 0.0)
            open_lifted = pair(jnp.where(opened, lifted, 0.0))
            state[row, head] = later * passed + mm(grad_low, open_lifted, TN)
            through = jnp.sum(begin * later, axis=0, keepdims=True) * passed
            weighted_part = grad_weighted * weighted
            grad_log = (
                part_ref[0, row, :, low : low + width]
                - grad_lowered * lowered
                - weighted_part
            )
            grad_last = through + jnp.sum(weighted_part, axis=0, keepdims=True)
            grad_step = split_sum(tri, grad_log, TN) + grad_last
            grad_key = grad_lowered * fall + grad_weighted * remain
            grad_logit = (
                span_bound
                * jax.nn.sigmoid(logit)
                * jax.nn.sigmoid(-logit)
                * (grad_step / forget - grad_key)
            )
            bias_grad_ref[:, low : low + width] += jnp.sum(grad_logit, axis=0, keepdims=True)
            zv_grad_ref[0, row, :, low : low + width] = grad_logit.astype(bf16)
            zv_grad_ref[0, row, :, high : high + width] = grad_value.astype(bf16)


def local_call(
    kernel, at, docs, ins, in_specs, out_shapes, out_specs, grid, scratch, aliases=None
):
    return pl.pallas_call(
        kernel,
        grid_spec=pltpu.PrefetchScalarGridSpec(
            num_scalar_prefetch=2,
            grid=grid,
            in_specs=in_specs,
            out_specs=out_specs,
            scratch_shapes=scratch,
        ),
        out_shape=out_shapes,
        input_output_aliases=aliases or {},
        compiler_params=pltpu.CompilerParams(
            dimension_semantics=("arbitrary",) * len(grid), vmem_limit_bytes=48 * 1024 * 1024
        ),
    )(at, docs, *ins)


def contract_rows(left, right):
    return lax.dot_general(left, right, (TN, ((), ())), preferred_element_type=f32)


def times_transpose(left, right):
    return lax.dot_general(left, right, (NT, ((), ())), preferred_element_type=f32)


def times(left, right):
    return jnp.dot(left, right, preferred_element_type=f32)


def rms_rate(values):
    return lax.rsqrt(jnp.mean(values * values, axis=-1, keepdims=True) + epsilon)


def rms_back(grad, values, rate):
    return rate * grad - values * (
        rate * rate * rate * jnp.mean(grad * values, axis=-1, keepdims=True)
    )


def on_device(
    block_input,
    out_grad,
    doc_starts,
    w_query,
    w_forget,
    w_input,
    w_outgate,
    w_out,
    w_gate,
    w_up,
    w_down,
    norm_gain,
    mlp_gain,
    group_gain,
    forget_bias,
):
    row_count, span, features = block_input.shape
    groups = lax.axis_size("z")
    own_row = lax.axis_index("row")
    own_spot = lax.axis_index("y") * 2 + lax.axis_index("x")
    own_first = own_row == 0
    spots, members = 4, 8
    tokens = row_count * span
    width = features // HEADS
    heads = HEADS // members
    wide = heads * width
    share = w_query.shape[0]
    units = w_gate.shape[1] // spots
    block = w_gate.shape[0]
    half = spots * tokens

    by_chip = 2 * share == width and groups == 2 * heads
    if by_chip:
        held = lax.all_gather(w_out, "z", axis=0, tiled=False).reshape(2, heads, share, features)
    else:
        held = lax.all_gather(w_out, everywhere, axis=0, tiled=True)

    def cut_heads(first, second):
        both = jnp.stack([first, second]).reshape(2, share, 2, heads, spots, width)
        return both.transpose(4, 2, 1, 0, 3, 5).reshape(members, share, 2 * wide)

    def over_group(cut):
        return lax.all_to_all(cut, group, 0, 0, tiled=True)

    def over_plane(cut):
        return lax.all_to_all(cut, plane, 0, 0, tiled=True)

    def over_groups(cut):
        flat = cut.reshape(cut.shape[0] * cut.shape[1], cut.shape[2])
        return lax.all_gather(flat, "z", axis=0, tiled=True)

    vectors = jnp.stack([norm_gain, mlp_gain, group_gain, forget_bias]).astype(f32)
    vectors = jnp.broadcast_to(vectors.reshape(1, 4 * share), (groups * members, 4 * share))
    vectors = lax.all_to_all(vectors, everywhere, 0, 0, tiled=True)
    mixer_cut = over_group(
        after(
            jnp.stack([cut_heads(w_forget, w_input), cut_heads(w_query, w_outgate)], axis=1),
            vectors,
        )
    )
    zv_all = over_groups(mixer_cut[:, 0])
    qr_all = over_groups(mixer_cut[:, 1])

    vectors = vectors.reshape(groups * members, 4, share).transpose(1, 0, 2).reshape(4, features)
    here = lax.dynamic_index_in_dim(
        vectors.reshape(4, 2, heads, spots, width), own_row, 1, False
    )
    here = lax.dynamic_index_in_dim(here, own_spot, 2, False).reshape(4, wide)
    first_gain, mid_gain = vectors[0:1], vectors[1:2]
    gain_here, bias_here = here[2:3], here[3:4]

    input_float = block_input.astype(f32).reshape(tokens, features)
    first_rate = rms_rate(input_float)
    normed = (input_float * first_rate * first_gain).astype(bf16)
    normed_all = gather_group(normed)

    pair_cut = jnp.concatenate(
        [w_gate.reshape(block, spots, units), w_up.reshape(block, spots, units)], axis=-1
    ).transpose(1, 0, 2)
    pair_cut = over_plane(after(pair_cut, normed_all))
    down_cut = w_down.T.reshape(block, spots, units).transpose(1, 0, 2)
    down_cut = over_plane(after(down_cut, pair_cut)).reshape(spots * block, units)

    docs = jnp.concatenate([doc_starts, swap_row(doc_starts)], axis=0)
    at = jnp.stack([own_spot, lax.axis_index("z") * (spots * span)]).astype(jnp.int32)
    by_block = (members, row_count, span)
    zv = times(normed_all, zv_all).reshape(by_block + (2 * wide,))

    once = pl.BlockSpec((1, wide), lambda *_: (0, 0))
    packed_block = (row_count, heads, width + PAD, width)
    packed_shape = jax.ShapeDtypeStruct((2 * row_count,) + packed_block[1:], bf16)
    states = pltpu.VMEM((row_count, heads, width, width), f32)
    decays = pltpu.VMEM((row_count, heads, 1, width), f32)

    def slab(columns, index):
        return pl.BlockSpec((1, row_count, span, columns), index)

    def ahead(h, c, at_ref, docs_ref):
        return (h * spots + (c ^ at_ref[0]), 0, 0, 0)

    def behind(h, c, at_ref, docs_ref):
        return (h * spots + ((spots - 1 - c) ^ at_ref[0]), 0, 0, 0)

    by_half = pl.BlockSpec(packed_block, lambda h, c, at_ref, docs_ref: (h, 0, 0, 0))

    packed = local_call(
        state_kernel,
        at,
        docs,
        (zv, bias_here),
        [slab(2 * wide, ahead), once],
        packed_shape,
        by_half,
        (2, spots),
        (states, decays),
    )
    grad_low = out_grad.reshape(tokens, features)

    packed, pair_cut = join(packed, pair_cut.reshape(spots * block, 2 * units))
    pair_all = lax.all_gather(pair_cut, "z", axis=0, tiled=True)
    gate_all, up_all = pair_all[:, :units], pair_all[:, units:]
    carried = relay(packed, True)
    near = gather_second(*gather_first(after(grad_low, pair_cut)))
    qr = times(normed_all, qr_all)
    carried, near, qr, down_cut = join(carried, near, qr, down_cut)
    down_all = lax.all_gather(down_cut, "z", axis=0, tiled=True)
    grad_all = gather_last(near)
    qr = qr.reshape(by_block + (2 * wide,))

    def forward_half(side, qr):
        def place(c, at_ref, docs_ref):
            return (side * spots + (c ^ at_ref[0]), 0, 0, 0)

        def local(c, at_ref, docs_ref):
            return (c ^ at_ref[0], 0, 0, 0)

        def kernel(*refs):
            forward_kernel(side, *refs)

        return local_call(
            kernel,
            at,
            docs,
            (qr, zv, bias_here, gain_here, *carried),
            [slab(2 * wide, place), slab(2 * wide, place), once, once]
            + [pl.BlockSpec(packed_block, lambda c, at_ref, docs_ref: (side, 0, 0, 0))]
            * len(carried),
            (
                jax.ShapeDtypeStruct((spots,) + by_block[1:] + (wide,), f32),
                jax.ShapeDtypeStruct((spots,) + by_block[1:] + (wide,), bf16),
                jax.ShapeDtypeStruct((spots, row_count, heads, width, width), f32),
            ),
            (
                slab(wide, local),
                slab(wide, local),
                pl.BlockSpec(
                    (1, row_count, heads, width, width),
                    lambda c, at_ref, docs_ref: (c, 0, 0, 0, 0),
                ),
            ),
            (spots,),
            (states,),
        )

    if by_chip:
        keep = lax.dynamic_index_in_dim(held, own_row, 0, False)
        give = lax.dynamic_index_in_dim(held, 1 - own_row, 0, False)
        take = swap_row(give)
        out_here = jnp.stack(
            [jnp.where(own_first, keep, take), jnp.where(own_first, take, keep)], axis=1
        ).reshape(wide, features)
    else:
        held = held.reshape(2, heads, spots, width, features)
        held = lax.dynamic_index_in_dim(held, own_row, 0, False)
        out_here = lax.dynamic_index_in_dim(held, own_spot, 1, False).reshape(wide, features)

    far_out, far_mixed, far_starts = forward_half(1, qr)
    far_mixed = far_mixed.reshape(half, wide)
    far_part = times(far_mixed, out_here).astype(bf16)
    near_out, near_mixed, near_starts = forward_half(0, after(qr, far_part))
    near_mixed = near_mixed.reshape(half, wide)
    near_part = times(near_mixed, out_here)
    hidden = input_float + scatter_group(near_part, far_part)[0]

    mid_rate = rms_rate(hidden)
    first, grad_all, mixer_weights = join(
        gather_first((hidden * mid_rate * mid_gain).astype(bf16)),
        grad_all,
        jnp.concatenate([qr_all, zv_all], axis=1),
    )
    mid_all = gather_last(gather_second(*first))
    gate_a = times(mid_all, gate_all)
    up_b = times(mid_all, up_all)
    gate_on = jax.nn.sigmoid(gate_a)
    gate_act = gate_a * gate_on
    product = (gate_act * up_b).astype(bf16)

    def spread(partial):
        return lax.psum_scatter(partial.astype(bf16), "z", scatter_dimension=0, tiled=True)

    down_part = contract_rows(grad_all, product).astype(bf16)
    grad_down = spread(down_part)
    grad_product = times(after(grad_all, down_part), down_all)
    grad_a = (grad_product * up_b * gate_on * (1.0 + gate_a * (1.0 - gate_on))).astype(bf16)
    grad_b = (grad_product * gate_act).astype(bf16)
    far_mid = times_transpose(grad_a[half:], gate_all) + times_transpose(grad_b[half:], up_all)
    far_mid = far_mid.astype(bf16)
    near_mid = times_transpose(grad_a[:half], gate_all) + times_transpose(grad_b[:half], up_all)
    held_mid, held_a, held_b = lax.optimization_barrier((mid_all, grad_a, grad_b, near_mid))[:3]
    gate_part = contract_rows(held_mid, held_a).astype(bf16)
    up_part = contract_rows(held_mid, held_b).astype(bf16)
    grad_mid, gate_part, up_part, grad_down = scatter_group(
        near_mid, far_mid, (gate_part, up_part), (grad_down,)
    )
    grad_gate = spread(gate_part)
    grad_up = spread(up_part)
    grad_float = out_grad.astype(f32).reshape(tokens, features)
    grad_hidden = grad_float + rms_back(grad_mid * mid_gain, hidden, mid_rate)

    product_here = after(product, up_part)
    far_down = times_transpose(product_here[half:], down_all).astype(bf16)
    near_down = times_transpose(product_here[:half], down_all)
    first, sums = join(
        gather_first(grad_hidden.astype(bf16)), scatter_first(near_down, far_down)
    )
    near_gm = lay(gather_second(*first))
    far_gm = swap_row(near_gm)
    sums = scatter_second(*join(sums, near_gm)[0])
    grad_mixed = jnp.concatenate(
        [times_transpose(near_gm, out_here), times_transpose(far_gm, out_here)], axis=0
    ).reshape(by_block + (wide,))
    mixer_out = jnp.concatenate([near_out, far_out], axis=0)
    starts = jnp.concatenate([near_starts, far_starts], axis=0)
    starts_spec = pl.BlockSpec(
        (1, row_count, heads, width, width),
        lambda h, c, at_ref, docs_ref: (h * spots + spots - 1 - c, 0, 0, 0, 0),
    )
    all_grads, lows, parts, packed = local_call(
        open_kernel,
        at,
        docs,
        (qr, zv, mixer_out, grad_mixed, bias_here, gain_here, starts),
        [
            slab(2 * wide, behind),
            slab(2 * wide, behind),
            slab(wide, behind),
            slab(wide, behind),
            once,
            once,
            starts_spec,
        ],
        (
            jax.ShapeDtypeStruct(by_block + (4 * wide,), bf16),
            jax.ShapeDtypeStruct(by_block + (wide,), f32),
            jax.ShapeDtypeStruct(by_block + (wide,), f32),
            packed_shape,
        ),
        (slab(2 * wide, behind), slab(wide, behind), slab(wide, behind), by_half),
        (2, spots),
        (states, decays),
    )
    packed, sums, near_late, far_late = join(packed, sums, near_gm, far_gm)

    def out_rows():
        rows = contract_rows(near_mixed, near_late) + contract_rows(far_mixed, far_late)
        return rows.astype(bf16)

    def query_part():
        qr_grads = all_grads.reshape(2 * half, 4 * wide)[:, : 2 * wide]
        return contract_rows(normed_all, qr_grads).astype(bf16)

    def join_units(back):
        return back.astype(f32).transpose(1, 0, 2).reshape(block, spots * units)

    def turn_units(back):
        return back.transpose(0, 2, 1).reshape(spots * units, block).astype(f32)

    def units_back(cut):
        return over_plane(cut.reshape(spots, block, units))

    def beside(step):
        if step == 0:
            return (out_rows(), scatter_third(*sums))
        if step == 1:
            return (query_part(), turn_units(units_back(after(grad_down, later[0]))))
        if step == 2:
            return (join_units(units_back(after(grad_gate, later[1]))),)
        return ()

    later = []
    done = []
    for step in range(groups - 1):
        packed, extra = join(hop(packed, False), beside(step))
        later.append(packed)
        done += extra
    grad_out_rows, sums, qr_part, grad_down, grad_gate = done
    block_output = (hidden + scatter_last(*sums)).astype(bf16)
    if by_chip:
        cut = grad_out_rows.reshape(heads, 2, share, features)
        keep = lax.dynamic_index_in_dim(cut, own_row, 1, False)
        give = lax.dynamic_index_in_dim(cut, 1 - own_row, 1, False)
        take = swap_row(give)
        cut = jnp.concatenate(
            [jnp.where(own_first, keep, take), jnp.where(own_first, take, keep)], axis=0
        )
        grad_out = spread(cut.reshape(groups * share, features))
    else:
        placed = jnp.zeros((2, heads, spots, width, features), bf16)
        placed = lax.dynamic_update_slice(
            placed,
            grad_out_rows.reshape(1, heads, 1, width, features),
            (own_row, 0, own_spot, 0, 0),
        )
        grad_out = lax.psum_scatter(
            placed.reshape(features, features), everywhere, scatter_dimension=0, tiled=True
        )
    grad_qr = spread(qr_part)

    def behind_right(h, c, at_ref, docs_ref):
        return behind(h, c, at_ref, docs_ref)[:3] + (1,)

    all_grads, bias_part = local_call(
        close_kernel,
        at,
        docs,
        (all_grads, qr, zv, lows, parts, bias_here, starts, *later),
        [
            pl.BlockSpec(memory_space=pl.ANY),
            slab(2 * wide, behind),
            slab(2 * wide, behind),
            slab(wide, behind),
            slab(wide, behind),
            once,
            starts_spec,
        ]
        + [by_half] * len(later),
        (
            jax.ShapeDtypeStruct(by_block + (4 * wide,), bf16),
            jax.ShapeDtypeStruct((1, wide), f32),
        ),
        (slab(2 * wide, behind_right), once),
        (2, spots),
        (states,),
        {2: 0},
    )
    all_grads = all_grads.reshape(2 * half, 4 * wide)
    zv_part = contract_rows(normed_all, all_grads[:, 2 * wide :]).astype(bf16)
    grad_zv = spread(zv_part)
    late_grads = after(all_grads, zv_part)
    far_in = times_transpose(late_grads[half:], mixer_weights).astype(bf16)
    near_in = times_transpose(late_grads[:half], mixer_weights)
    bias_placed = jnp.zeros((2, heads, spots, width), f32)
    bias_placed = lax.dynamic_update_slice(
        bias_placed, bias_part.reshape(1, heads, 1, width), (own_row, 0, own_spot, 0)
    )
    bias_back = lax.all_to_all(
        bias_placed.reshape(groups * members, share), everywhere, 0, 0, tiled=True
    )
    grad_bias = jnp.sum(bias_back, axis=0)

    def join_heads(cut):
        back = over_group(cut.reshape(members, share, 2 * wide))
        back = back.reshape(spots, 2, share, 2, heads, width)
        return [
            back[:, :, :, at].transpose(2, 1, 3, 0, 4).reshape(share, features).astype(f32)
            for at in range(2)
        ]

    state, block_output, grad_out, grad_qr, grad_up = join(
        scatter_first(near_in, far_in), block_output, grad_out, grad_qr, grad_up
    )
    grad_out = grad_out.astype(f32)
    state, (query_back, outgate_back), grad_up, grad_out, block_output = join(
        scatter_second(*state),
        join_heads(grad_qr),
        join_units(units_back(grad_up)),
        grad_out,
        block_output,
    )
    grad_normed = scatter_last(*scatter_third(*state))
    input_grad = grad_hidden + rms_back(grad_normed * first_gain, input_float, first_rate)
    input_grad = input_grad.astype(bf16).reshape(block_input.shape)

    own_vectors = (norm_gain.astype(f32), mlp_gain.astype(f32), group_gain.astype(f32))
    grad_head_gain = jnp.sum(grad_out * w_out.astype(f32), axis=1) / own_vectors[2]

    mid_part = jnp.sum(grad_gate * w_gate.astype(f32) + grad_up * w_up.astype(f32), axis=1)
    mid_part = mid_part.reshape(2, share)
    mid_keep = lax.dynamic_index_in_dim(mid_part, own_row, 0, False)
    mid_give = lax.dynamic_index_in_dim(mid_part, 1 - own_row, 0, False)
    grad_mid_gain = (mid_keep + swap_row(mid_give)) / own_vectors[1]

    forget_back, input_back = join_heads(grad_zv)
    first_part = query_back * w_query.astype(f32) + outgate_back * w_outgate.astype(f32)
    first_part += forget_back * w_forget.astype(f32) + input_back * w_input.astype(f32)
    grad_first_gain = jnp.sum(first_part, axis=1) / own_vectors[0]

    return (
        block_output.reshape(block_input.shape),
        input_grad,
        query_back,
        forget_back,
        input_back,
        outgate_back,
        grad_out,
        grad_gate,
        grad_up,
        grad_down,
        grad_first_gain,
        grad_mid_gain,
        grad_head_gain,
        grad_bias,
    )


def solution(mesh):
    count, rows = mesh.devices.shape
    folded = Mesh(mesh.devices.reshape(count // 4, 2, 2, rows), everywhere)
    seq = ("z", "y", "x")
    token_spec = P("row", seq, None)
    matrix_spec = P(everywhere, None)
    vector_spec = P(everywhere)
    wide_spec = P(seq, "row")
    tall_spec = P("row", seq)
    in_specs = (
        (token_spec, token_spec, P("row", None))
        + (matrix_spec,) * 5
        + (wide_spec, wide_spec, tall_spec)
        + (vector_spec,) * 4
    )
    out_specs = (
        (token_spec, token_spec)
        + (matrix_spec,) * 5
        + (wide_spec, wide_spec, tall_spec)
        + (vector_spec,) * 4
    )
    return jax.shard_map(
        on_device, mesh=folded, in_specs=in_specs, out_specs=out_specs, check_vma=False
    )
```

time: 887 us -> 795 us (0.90)
  waiting for transfers between devices: 327 us -> 244 us
  Pallas kernels: 71.1 us -> 95.7 us
  matrix products: 158 us -> 179 us
  blocking collectives: 20.6 us -> 0 us
  local copies, waits for them, and re-layouts: 108 us -> 94 us
  starting transfers between devices: 110 us -> 96.3 us
    ppermute x10 -> x6, waiting for transfers between devices: 107 us -> 18.8 us  [hop(): return lax.ppermute(packed, 'z', pairs)]
    ppermute x16, waiting for transfers between devices: 131 us -> 80.1 us  [swap_x(): return lax.ppermute(a, 'x', swap)]
    unnamed x175 -> x245, local copies, waits for them, and re-layouts: 64.6 us -> 25.1 us
    all_to_all x6 -> x9, waiting for transfers between devices: 40.3 us -> 71.5 us  [the longest x5 37.5 us: over_plane(): return lax.all_to_all(cut, plane, 0, 0, tiled=True)]
    pallas_call x0 -> x4, Pallas kernels: none -> 24.7 us  [lay(): pl.pallas_call(lay_kernel, grid=(total // rows,), in_specs=[pl.BlockSpec(...]
    all_to_all x1 -> x0, blocking collectives: 20.6 us -> none  [on_device(): scaled = lax.all_to_all(scaled, group, 0, 0, tiled=True)]
    ppermute x10 -> x6, starting transfers between devices: 34 us -> 13.9 us  [hop(): return lax.ppermute(packed, 'z', pairs)]
    ppermute x16, waiting for transfers between devices: 31.3 us -> 51 us  [swap_y(): return lax.ppermute(a, 'y', swap)]
  transfers between devices with their start and end apart: 86 -> 83, of which waited for: 40 -> 34; matrix products, arithmetic and copies ran while one was open for 31% -> 36% of each run, Pallas kernels for 8% -> 11%
where the time goes in v2:
time: 795 us; the launch traced here: 784 us
  waiting for transfers between devices  244 us (31%)
  matrix products  179 us (23%)
  starting transfers between devices  96.3 us (12%)
  Pallas kernels  95.7 us (12%)
  local copies, waits for them, and re-layouts  94 us (12%)
  other arithmetic  58.5 us (7%)
  between operations  16.2 us (2%)
    ppermute x16, waiting for transfers between devices, swap_x(): return lax.ppermute(a, 'x', swap)  80.1 us
    pallas_call x5, Pallas kernels, local_call(): pl.pallas_call(kernel, grid_spec=pltpu.PrefetchScalarGridSpec(num_scalar_...  71 us
    dot_general x7, matrix products, times(): return jnp.dot(left, right, preferred_element_type=f32)  65 us
    dot_general x10, matrix products, times_transpose(): lax.dot_general(left, right, (NT, ((), ())), preferred_element_type=f32)  57.9 us
    dot_general x7, matrix products, contract_rows(): lax.dot_general(left, right, (TN, ((), ())), preferred_element_type=f32)  56.4 us
    ppermute x16, waiting for transfers between devices, swap_y(): return lax.ppermute(a, 'y', swap)  51 us
    all_to_all x5, waiting for transfers between devices, over_plane(): return lax.all_to_all(cut, plane, 0, 0, tiled=True)  37.5 us
    all_to_all x3, waiting for transfers between devices, over_group(): return lax.all_to_all(cut, group, 0, 0, tiled=True)  29.4 us
  transfers between devices with their start and end apart: 83, of which 34 were waited for; matrix products, arithmetic and copies ran while one was open for 36% of the time, Pallas kernels for 11%

profile of v2, /device:TPU:0, one launch (start us, length us, event | category | flops | bytes accessed | tf_op | source)
XLA Modules:
  0.0 784.0 jit_solution(6175912656951351602)
XLA Ops:
  20.0 15.3 %all-to-all-done.1 = bf16[8,2,64,512]{3,2,1,0:T(8,128)(2,1)S(1)} async-done(((bf16[8,2,64,512]{3,2,1,0:T(8,128)(2,1)}), bf16[8,2,64,512]{3,2,1,0:T(8,128)(2,1)S(1)}, u32[]{:S(2)}, u32[]{:S(2)}) %all-to-all-start.1) | async-done | bytes 1048608 | tf_op jit(solution)/shard_map/all_to_all | solution.py:525
  49.9 24.0 %collective-permute-done.1.refs_1_ = bf16[256,2048]{1,0:T(8,128)(2,1)S(1)} collective-permute-done((bf16[256,2048]{1,0:T(8,128)(2,1)S(1)}, bf16[256,2048]{1,0:T(8,128)(2,1)S(1)}, u32[]{:S(2)}, u32[]{:S(2)}) %collective-permute-start.1) | collective-permute-done | bytes 1048608 | tf_op jit(solution)/shard_map/ppermute | solution.py:22
  75.8 11.5 %collective-permute-done.3.refs_3_ = bf16[128,2048]{1,0:T(8,128)(2,1)} collective-permute-done((bf16[128,2048]{1,0:T(8,128)(2,1)S(1)}, bf16[128,2048]{1,0:T(8,128)(2,1)}, u32[]{:S(2)}, u32[]{:S(2)}) %collective-permute-start.3) | collective-permute-done | bytes 524320 | tf_op jit(solution)/shard_map/ppermute | solution.py:26
  111.8 14.2 %all-to-all-done.2 = bf16[4,128,1408]{1,2,0:T(8,128)(2,1)S(1)} async-done(((bf16[4,128,1408]{1,2,0:T(8,128)(2,1)}), bf16[4,128,1408]{1,2,0:T(8,128)(2,1)S(1)}, u32[]{:S(2)}, u32[]{:S(2)}) %all-to-all-start.2) | async-done | bytes 1441824 | tf_op jit(solution)/shard_map/all_to_all | solution.py:528
  127.5 7.6 fusion.60
  163.1 13.7 %all-to-all-done.3 = bf16[4,128,704]{1,2,0:T(8,128)(2,1)S(1)} async-done(((bf16[4,128,704]{1,2,0:T(8,128)(2,1)}), bf16[4,128,704]{1,2,0:T(8,128)(2,1)S(1)}, u32[]{:S(2)}, u32[]{:S(2)}) %all-to-all-start.3) | async-done | bytes 720928 | tf_op jit(solution)/shard_map/all_to_all | solution.py:528
  184.7 10.5 %fusion.61 = f32[2048,512]{1,0:T(8,128)} fusion(bf16[2048,2048]{1,0:T(8,128)(2,1)} %shard_map.254, bf16[2048,512]{1,0:T(8,128)(2,1)} %all-gather.9.cloned.1.call-done), kind=kOutput, calls=%fused_computation.187 | convolution fusion | flops 4294967296 | bytes 14680064 | tf_op jit(solution)/shard_map/dot_general | solution.py:469
  195.6 10.8 %shard_map.256 = (f32[4,2,128,256]{3,2,1,0:T(8,128)S(1)}, bf16[4,2,128,256]{3,2,1,0:T(8,128)(2,1)S(1)}, f32[4,2,2,128,128]{4,3,2,1,0:T(8,128)S(1)}) custom-call(s32[2]{0:T(128)S(1)} %pad_add_fusion.1.at_ref.refs_0_, s32[4,4]{1,0:T(4,128)S(1)} %pad_add_fusion.docs_ref.refs_1_, f32[8,2,128,512]{3,2,1,0:T(8,128)} %bitcast.288, f32[8,2,128,512]{3,2,1,0:T(8,128)} %bitcast.272, ...), custom_call_target="tpu_custom_call" | custom-call | tf_op jit(solution)/shard_map/pallas_call | solution.py:443
  210.5 10.8 %shard_map.257 = (f32[4,2,128,256]{3,2,1,0:T(8,128)S(1)}, bf16[4,2,128,256]{3,2,1,0:T(8,128)(2,1)S(1)}, f32[4,2,2,128,128]{4,3,2,1,0:T(8,128)S(1)}) custom-call(s32[2]{0:T(128)S(1)} %pad_add_fusion.1.at_ref.refs_0_, s32[4,4]{1,0:T(4,128)S(1)} %pad_add_fusion.docs_ref.refs_1_, f32[8,2,128,512]{3,2,1,0:T(8,128)} %bitcast.289, f32[8,2,128,512]{3,2,1,0:T(8,128)} %bitcast.273, ...), custom_call_target="tpu_custom_call" | custom-call | tf_op jit(solution)/shard_map/pallas_call | solution.py:443
  229.1 23.2 %collective-permute-done.19 = bf16[2,256,1024]{2,1,0:T(8,128)(2,1)S(1)} collective-permute-done((bf16[2,256,1024]{2,1,0:T(8,128)(2,1)S(1)}, bf16[2,256,1024]{2,1,0:T(8,128)(2,1)S(1)}, u32[]{:S(2)}, u32[]{:S(2)}) %collective-permute-start.19) | collective-permute-done | bytes 1048608 | tf_op jit(solution)/shard_map/ppermute | solution.py:22
  287.0 11.4 %collective-permute-done.23.refs_1_ = bf16[256,2048]{1,0:T(8,128)(2,1)} collective-permute-done((bf16[256,2048]{1,0:T(8,128)(2,1)S(1)}, bf16[256,2048]{1,0:T(8,128)(2,1)}, u32[]{:S(2)}, u32[]{:S(2)}) %collective-permute-start.23) | collective-permute-done | bytes 1048608 | tf_op jit(solution)/shard_map/ppermute | solution.py:22
  304.5 10.5 %collective-permute-done.30.refs_3_ = bf16[128,2048]{1,0:T(8,128)(2,1)S(1)} collective-permute-done((bf16[128,2048]{1,0:T(8,128)(2,1)S(1)}, bf16[128,2048]{1,0:T(8,128)(2,1)S(1)}, u32[]{:S(2)}, u32[]{:S(2)}) %collective-permute-start.30) | collective-permute-done | bytes 524320 | tf_op jit(solution)/shard_map/ppermute | solution.py:26
  319.1 7.7 shard_map.259
  326.8 11.4 %fusion.10 = f32[2048,704]{0,1:T(8,128)} fusion(bf16[2048,2048]{1,0:T(8,128)(2,1)} %shard_map.259, bf16[2048,1408]{1,0:T(8,128)(2,1)} %all-gather.11.cloned.1.call-done), kind=kOutput, calls=%fused_computation.30 | convolution fusion | flops 5905580032 | bytes 17301504 | tf_op jit(solution)/shard_map/dot_general | solution.py:469
  338.3 14.0 %multiply_convert_fusion.2 = (bf16[2048,704]{0,1:T(8,128)(2,1)}, f32[2048,704]{0,1:T(8,128)}) fusion(f32[2048,704]{0,1:T(8,128)} %fusion.10, bf16[2048,2048]{1,0:T(8,128)(2,1)} %shard_map.259, bf16[2048,1408]{1,0:T(8,128)(2,1)S(1)} %copy-done.108), kind=kOutput, calls=%fused_computation.7 | convolution fusion | flops 5914230784 | bytes 25952256 | tf_op jit(solution)/shard_map/dot_general | solution.py:469
  352.3 9.5 %convolution_convert_fusion.5 = bf16[2048,704]{0,1:T(8,128)(2,1)} fusion(bf16[2048,704]{0,1:T(8,128)(2,1)} %get-tuple-element.165, bf16[2048,2048]{1,0:T(8,128)(2,1)S(1)} %bitcast.325), kind=kOutput, calls=%fused_computation.17 | convolution fusion | flops 5907021824 | bytes 14155776 | tf_op jit(solution)/shard_map/dot_general | solution.py:461
  361.8 11.9 %all-gather.13.cloned.1.call-done = bf16[2048,704]{0,1:T(8,128)(2,1)} async-done(((bf16[512,704]{0,1:T(8,128)(2,1)}), bf16[2048,704]{0,1:T(8,128)(2,1)}) %all-gather.13.cloned.1.call-update) | async-done | bytes 2883600 | tf_op jit(solution)/shard_map/all_gather | solution.py:608
  373.7 13.8 %multiply_convert_fusion = (bf16[2048,704]{0,1:T(8,128)(2,1)S(1)}, bf16[2048,704]{0,1:T(8,128)(2,1)S(1)}) fusion(f32[2048,704]{0,1:T(8,128)} %fusion.10, f32[2048,704]{0,1:T(8,128)} %get-tuple-element.289, bf16[2048,2048]{1,0:T(8,128)(2,1)} %shard_map.258, bf16[2048,704]{0,1:T(8,128)(2,1)} %all-gather.13.cloned.1.call-done), kind=kOutput, calls=%fused_computation.5 | convolution fusion | flops 5924323328 | bytes 28573696 | tf_op jit(solution)/shard_map/dot_general | solution.py:469
  405.1 8.5 %convert_add_fusion.2 = f32[1024,2048]{1,0:T(8,128)S(1)} fusion(bf16[1024,2048]{1,0:T(8,128)(2,1)} %collective-permute-done.37, f32[1024,2048]{1,0:T(8,128)S(1)} %fusion.8, bf16[2048,1408]{1,0:T(8,128)(2,1)} %all-gather.11.cloned.1.call-done, bf16[2048,704]{0,1:T(8,128)(2,1)} %copy-done.111), kind=kOutput, calls=%fused_computation.2 | convolution fusion | flops 2959081472 | bytes 25559040 | tf_op jit(solution)/shard_map/dot_general | solution.py:465
  422.0 11.4 %convolution_convert_fusion.4 = bf16[2048,704]{0,1:T(8,128)(2,1)} fusion(bf16[2048,704]{0,1:T(8,128)(2,1)S(1)} %copy-done.113, bf16[2048,2048]{1,0:T(8,128)(2,1)} %shard_map.259), kind=kOutput, calls=%fused_computation.16 | convolution fusion | flops 5907021824 | bytes 14155776 | tf_op jit(solution)/shard_map/dot_general | solution.py:461
  433.3 10.7 %convolution_convert_fusion.3 = bf16[2048,704]{0,1:T(8,128)(2,1)} fusion(bf16[2048,704]{0,1:T(8,128)(2,1)} %copy-done.111, bf16[2048,2048]{1,0:T(8,128)(2,1)} %shard_map.259), kind=kOutput, calls=%fused_computation.15 | convolution fusion | flops 5907021824 | bytes 14155776 | tf_op jit(solution)/shard_map/dot_general | solution.py:461
  492.2 10.9 %collective-permute-done.42.refs_1_ = bf16[256,2048]{1,0:T(8,128)(2,1)S(1)} collective-permute-done((bf16[256,2048]{1,0:T(8,128)(2,1)S(1)}, bf16[256,2048]{1,0:T(8,128)(2,1)S(1)}, u32[]{:S(2)}, u32[]{:S(2)}) %collective-permute-start.42) | collective-permute-done | bytes 1048608 | tf_op jit(solution)/shard_map/ppermute | solution.py:22
  506.6 9.0 %collective-permute-done.45.refs_3_ = bf16[128,2048]{1,0:T(8,128)(2,1)S(1)} collective-permute-done((bf16[128,2048]{1,0:T(8,128)(2,1)S(1)}, bf16[128,2048]{1,0:T(8,128)(2,1)S(1)}, u32[]{:S(2)}, u32[]{:S(2)}) %collective-permute-start.45) | collective-permute-done | bytes 524320 | tf_op jit(solution)/shard_map/ppermute | solution.py:26
  532.0 18.0 %shard_map.261 = (bf16[8,2,128,1024]{3,2,1,0:T(8,128)(2,1)}, f32[8,2,128,256]{3,2,1,0:T(8,128)S(1)}, f32[8,2,128,256]{3,2,1,0:T(8,128)S(1)}, bf16[4,2,144,128]{3,2,1,0:T(8,128)(2,1)S(1)}) custom-call(s32[2]{0:T(128)S(1)} %copy-done.23, s32[4,4]{1,0:T(4,128)S(1)} %copy-done.17, f32[8,2,128,512]{3,2,1,0:T(8,128)} %bitcast.290, f32[8,2,128,512]{3,2,1,0:T(8,128)} %bitcast.274, ...), custom_call_target="tpu_custom_call" | custom-call | tf_op jit(solution)/shard_map/pallas_call | solution.py:443
  562.2 13.0 %collective-permute-done.50.rest_0_ = bf16[4,2,144,128]{3,2,1,0:T(8,128)(2,1)S(1)} collective-permute-done((bf16[4,2,144,128]{3,2,1,0:T(8,128)(2,1)S(1)}, bf16[4,2,144,128]{3,2,1,0:T(8,128)(2,1)S(1)}, u32[]{:S(2)}, u32[]{:S(2)}) %collective-permute-start.50) | collective-permute-done | bytes 294944 | tf_op jit(solution)/shard_map/ppermute | solution.py:123
  585.5 9.9 %convolution_convert_fusion.7 = bf16[2048,512]{1,0:T(8,128)(2,1)} fusion(bf16[2048,2048]{1,0:T(8,128)(2,1)} %shard_map.254, bf16[2048,1024]{1,0:T(8,128)(2,1)} %bitcast.330), kind=kOutput, calls=%fused_computation.19 | convolution fusion | flops 4296015872 | bytes 12582912 | tf_op jit(solution)/shard_map/dot_general | solution.py:461
  605.4 9.5 %all-to-all-done.5 = bf16[4,128,704]{1,2,0:T(8,128)(2,1)} async-done(((bf16[4,128,704]{1,2,0:T(8,128)(2,1)}), bf16[4,128,704]{1,2,0:T(8,128)(2,1)}, u32[]{:S(2)}, u32[]{:S(2)}) %all-to-all-start.5) | async-done | bytes 720928 | tf_op jit(solution)/shard_map/all_to_all | solution.py:528
  617.9 25.3 %shard_map.262 = (bf16[8,2,128,1024]{3,2,1,0:T(8,128)(2,1)}, f32[1,256]{1,0:T(1,128)S(1)}) custom-call(s32[2]{0:T(128)S(1)} %copy-done.23, s32[4,4]{1,0:T(4,128)S(1)} %copy-done.17, bf16[8,2,128,1024]{3,2,1,0:T(8,128)(2,1)} %get-tuple-element.171.kept_ref, f32[8,2,128,512]{3,2,1,0:T(8,128)} %bitcast.291, ...), custom_call_target="tpu_custom_call", output_to_operand_aliasing={{0}: (2, {})} | custom-call | tf_op jit(solution)/shard_map/pallas_call | solution.py:443
  643.2 9.9 %convolution_convert_fusion.6 = bf16[2048,512]{1,0:T(8,128)(2,1)} fusion(bf16[2048,2048]{1,0:T(8,128)(2,1)} %shard_map.254, bf16[2048,1024]{1,0:T(8,128)(2,1)} %bitcast.331), kind=kOutput, calls=%fused_computation.18 | convolution fusion | flops 4296015872 | bytes 12582912 | tf_op jit(solution)/shard_map/dot_general | solution.py:461
  653.1 9.5 %convolution_convert_fusion.2 = bf16[1024,2048]{1,0:T(8,128)(2,1)} fusion(bf16[2048,1024]{1,0:T(8,128)(2,1)} %pad_maximum_fusion, bf16[2048,1024]{1,0:T(8,128)(2,1)} %bitcast.332), kind=kOutput, calls=%fused_computation.14 | convolution fusion | flops 4297064448 | bytes 10485760 | tf_op jit(solution)/shard_map/dot_general | solution.py:465
  673.2 8.7 %convert_add_fusion = f32[1024,2048]{1,0:T(8,128)S(1)} fusion(bf16[1024,2048]{1,0:T(8,128)(2,1)} %collective-permute-done.55, bf16[2048,1024]{1,0:T(8,128)(2,1)} %pad_maximum_fusion, bf16[2048,1024]{1,0:T(8,128)(2,1)} %bitcast.333), kind=kOutput, calls=%fused_computation | convolution fusion | flops 4299161600 | bytes 18874368 | tf_op jit(solution)/shard_map/dot_general | solution.py:465
  715.7 14.1 %all-to-all-done.8 = bf16[8,64,512]{2,1,0:T(8,128)(2,1)} async-done(((bf16[8,64,512]{2,1,0:T(8,128)(2,1)}), bf16[8,64,512]{2,1,0:T(8,128)(2,1)}, u32[]{:S(2)}, u32[]{:S(2)}) %all-to-all-start.8) | async-done | bytes 524320 | tf_op jit(solution)/shard_map/all_to_all | solution.py:525
  (568 shorter events, 367.6 us)
Async XLA Ops:
  7.2 102.4 %all-gather.15.cloned.1.call-start = ((), (), s32[]{:S(2)}) async-start(), calls=%async_computation.26 | async-start | bytes 1310720 | tf_op jit(solution)/shard_map/all_gather | solution.py:516
  39.9 87.6 %all-gather.7.cloned.1.call-start = ((), (), s32[]{:S(2)}) async-start(), calls=%async_computation.16 | async-start | bytes 2621440 | tf_op jit(solution)/shard_map/all_gather | solution.py:532
  48.7 25.2 %collective-permute-start.1 = (bf16[256,2048]{1,0:T(8,128)(2,1)S(1)}, bf16[256,2048]{1,0:T(8,128)(2,1)S(1)}, u32[]{:S(2)}, u32[]{:S(2)}) collective-permute-start(bf16[256,2048]{1,0:T(8,128)(2,1)S(1)} %fusion.25.refs_0_), channel_id=1, source_target_pairs={{0,2},{2,0},{1,3},{3,1},{4,6},{6,4},{5,7},{7,5},{8,10},{10,8},{9,1... | collective-permute-start | bytes 3145736 | tf_op jit(solution)/shard_map/ppermute | solution.py:22
  49.2 25.3 %collective-permute-start.2 = (bf16[256,2048]{1,0:T(8,128)(2,1)S(1)}, bf16[256,2048]{1,0:T(8,128)(2,1)S(1)}, u32[]{:S(2)}, u32[]{:S(2)}) collective-permute-start(bf16[256,2048]{1,0:T(8,128)(2,1)S(1)} %fusion.25.refs_0_), channel_id=1, source_target_pairs={{0,4},{4,0},{1,5},{5,1},{2,6},{6,2},{3,7},{7,3},{8,12},{12,8},{9,1... | collective-permute-start | bytes 3145736 | tf_op jit(solution)/shard_map/ppermute | solution.py:26
  49.9 46.3 %collective-permute-start.5 = (bf16[256,2048]{1,0:T(8,128)(2,1)S(1)}, bf16[256,2048]{1,0:T(8,128)(2,1)}, u32[]{:S(2)}, u32[]{:S(2)}) collective-permute-start(bf16[256,2048]{1,0:T(8,128)(2,1)S(1)} %fusion.25.refs_0_), channel_id=1, source_target_pairs={{0,1},{1,0},{2,3},{3,2},{4,5},{5,4},{6,7},{7,6},{8,9},{9,8},{10,11... | collective-permute-start | bytes 3145736 | tf_op jit(solution)/shard_map/ppermute | solution.py:30
  107.2 77.5 %all-gather.9.cloned.1.call-start = ((), (), s32[]{:S(2)}) async-start(), calls=%async_computation.17 | async-start | bytes 2621440 | tf_op jit(solution)/shard_map/all_gather | solution.py:532
  111.5 39.7 %collective-permute-start.17 = (bf16[2,64,2048]{2,1,0:T(8,128)(2,1)}, bf16[2,64,2048]{2,1,0:T(8,128)(2,1)}, u32[]{:S(2)}, u32[]{:S(2)}) collective-permute-start(bf16[2,64,2048]{2,1,0:T(8,128)(2,1)} %dynamic-slice_bitcast_fusion.1), channel_id=1, source_target_pairs={{0,1},{1,0},{2,3},{3,2},{4,5},{5,4},{6,7},{7,6},{8,9},{9,8},{10,11... | collective-permute-start | bytes 1572872 | tf_op jit(solution)/shard_map/ppermute | solution.py:30
  143.1 37.6 %collective-permute-start.13 = (bf16[256,2048]{1,0:T(8,128)(2,1)S(1)}, bf16[256,2048]{1,0:T(8,128)(2,1)S(1)}, u32[]{:S(2)}, u32[]{:S(2)}) collective-permute-start(bf16[256,2048]{1,0:T(8,128)(2,1)S(1)} %bitcast.276), channel_id=1, source_target_pairs={{0,2},{2,0},{1,3},{3,1},{4,6},{6,4},{5,7},{7,5},{8,10},{10,8},{9,1... | collective-permute-start | bytes 3145736 | tf_op jit(solution)/shard_map/ppermute | solution.py:22
  144.5 36.8 %collective-permute-start.14 = (bf16[256,2048]{1,0:T(8,128)(2,1)S(1)}, bf16[256,2048]{1,0:T(8,128)(2,1)}, u32[]{:S(2)}, u32[]{:S(2)}) collective-permute-start(bf16[256,2048]{1,0:T(8,128)(2,1)S(1)} %bitcast.277), channel_id=1, source_target_pairs={{0,4},{4,0},{1,5},{5,1},{2,6},{6,2},{3,7},{7,3},{8,12},{12,8},{9,1... | collective-permute-start | bytes 3145736 | tf_op jit(solution)/shard_map/ppermute | solution.py:26
  145.1 31.7 %all-to-all-start.3 = ((bf16[4,128,704]{1,2,0:T(8,128)(2,1)}), bf16[4,128,704]{1,2,0:T(8,128)(2,1)S(1)}, u32[]{:S(2)}, u32[]{:S(2)}) async-start(bf16[4,128,704]{1,2,0:T(8,128)(2,1)} %bitcast.342), calls=%async_computation.3 | async-start | bytes 1441792 | tf_op jit(solution)/shard_map/all_to_all | solution.py:528
  148.6 178.2 %all-gather.11.cloned.1.call-start = ((), (), s32[]{:S(2)}) async-start(), calls=%async_computation.18 | async-start | bytes 7208960 | tf_op jit(solution)/shard_map/all_gather | solution.py:602
  209.9 163.8 %all-gather.13.cloned.1.call-start = ((), (), s32[]{:S(2)}) async-start(), calls=%async_computation.19 | async-start | bytes 3604480 | tf_op jit(solution)/shard_map/all_gather | solution.py:608
  226.7 25.6 %collective-permute-start.19 = (bf16[2,256,1024]{2,1,0:T(8,128)(2,1)S(1)}, bf16[2,256,1024]{2,1,0:T(8,128)(2,1)S(1)}, u32[]{:S(2)}, u32[]{:S(2)}) collective-permute-start(bf16[2,256,1024]{2,1,0:T(8,128)(2,1)S(1)} %slice_bitcast_fusion.23), channel_id=1, source_target_pairs={{0,2},{2,0},{1,3},{3,1},{4,6},{6,4},{5,7},{7,5},{8,10},{10,8},{9,1... | collective-permute-start | bytes 3145736 | tf_op jit(solution)/shard_map/ppermute | solution.py:22
  228.3 25.3 %collective-permute-start.20 = (bf16[2,256,1024]{2,1,0:T(8,128)(2,1)S(1)}, bf16[2,256,1024]{2,1,0:T(8,128)(2,1)S(1)}, u32[]{:S(2)}, u32[]{:S(2)}) collective-permute-start(bf16[2,256,1024]{2,1,0:T(8,128)(2,1)S(1)} %slice_bitcast_fusion.22), channel_id=1, source_target_pairs={{0,4},{4,0},{1,5},{5,1},{2,6},{6,2},{3,7},{7,3},{8,12},{12,8},{9,1... | collective-permute-start | bytes 3145736 | tf_op jit(solution)/shard_map/ppermute | solution.py:26
  272.6 25.7 %collective-permute-start.23 = (bf16[256,2048]{1,0:T(8,128)(2,1)S(1)}, bf16[256,2048]{1,0:T(8,128)(2,1)}, u32[]{:S(2)}, u32[]{:S(2)}) collective-permute-start(bf16[256,2048]{1,0:T(8,128)(2,1)S(1)} %multiply_convert_fusion.3.refs_0_), channel_id=1, source_target_pairs={{0,2},{2,0},{1,3},{3,1},{4,6},{6,4},{5,7},{7,5},{8,10},{10,8},{9,1... | collective-permute-start | bytes 3145736 | tf_op jit(solution)/shard_map/ppermute | solution.py:22
  274.1 25.4 %collective-permute-start.24 = (bf16[256,2048]{1,0:T(8,128)(2,1)S(1)}, bf16[256,2048]{1,0:T(8,128)(2,1)}, u32[]{:S(2)}, u32[]{:S(2)}) collective-permute-start(bf16[256,2048]{1,0:T(8,128)(2,1)S(1)} %multiply_convert_fusion.3.refs_0_), channel_id=1, source_target_pairs={{0,4},{4,0},{1,5},{5,1},{2,6},{6,2},{3,7},{7,3},{8,12},{12,8},{9,1... | collective-permute-start | bytes 3145736 | tf_op jit(solution)/shard_map/ppermute | solution.py:26
  317.1 146.2 %reduce-scatter.7.cloned.1.call-start = ((), (), s32[]{:S(2)}) async-start(), calls=%async_computation.20 | async-start | bytes 3604480 | tf_op jit(solution)/shard_map/reduce_scatter | solution.py:681
  397.6 200.0 %reduce-scatter.9.cloned.1.call-start = ((), (), s32[]{:S(2)}) async-start(), calls=%async_computation.21 | async-start | bytes 3604480 | tf_op jit(solution)/shard_map/reduce_scatter | solution.py:681
  419.0 28.9 %collective-permute-start.38 = (bf16[2,256,1024]{2,1,0:T(8,128)(2,1)}, bf16[2,256,1024]{2,1,0:T(8,128)(2,1)S(1)}, u32[]{:S(2)}, u32[]{:S(2)}) collective-permute-start(bf16[2,256,1024]{2,1,0:T(8,128)(2,1)} %slice_bitcast_fusion.19), channel_id=1, source_target_pairs={{0,2},{2,0},{1,3},{3,1},{4,6},{6,4},{5,7},{7,5},{8,10},{10,8},{9,1... | collective-permute-start | bytes 3145736 | tf_op jit(solution)/shard_map/ppermute | solution.py:22
  420.5 27.4 %collective-permute-start.39 = (bf16[2,256,1024]{2,1,0:T(8,128)(2,1)}, bf16[2,256,1024]{2,1,0:T(8,128)(2,1)S(1)}, u32[]{:S(2)}, u32[]{:S(2)}) collective-permute-start(bf16[2,256,1024]{2,1,0:T(8,128)(2,1)} %slice_bitcast_fusion.18), channel_id=1, source_target_pairs={{0,4},{4,0},{1,5},{5,1},{2,6},{6,2},{3,7},{7,3},{8,12},{12,8},{9,1... | collective-permute-start | bytes 3145736 | tf_op jit(solution)/shard_map/ppermute | solution.py:26
  453.7 27.0 %collective-permute-start.44 = (bf16[1024,2048]{1,0:T(8,128)(2,1)}, bf16[1024,2048]{1,0:T(8,128)(2,1)}, u32[]{:S(2)}, u32[]{:S(2)}) collective-permute-start(bf16[1024,2048]{1,0:T(8,128)(2,1)} %convolution_convert_fusion), channel_id=1, source_target_pairs={{0,1},{1,0},{2,3},{3,2},{4,5},{5,4},{6,7},{7,6},{8,9},{9,8},{10,11... | collective-permute-start | bytes 12582920 | tf_op jit(solution)/shard_map/ppermute | solution.py:30
  459.9 227.8 %reduce-scatter.15.cloned.1.call-start = ((), (), s32[]{:S(2)}) async-start(), calls=%async_computation.24 | async-start | bytes 3604480 | tf_op jit(solution)/shard_map/reduce_scatter | solution.py:681
  478.6 24.5 %collective-permute-start.42 = (bf16[256,2048]{1,0:T(8,128)(2,1)S(1)}, bf16[256,2048]{1,0:T(8,128)(2,1)S(1)}, u32[]{:S(2)}, u32[]{:S(2)}) collective-permute-start(bf16[256,2048]{1,0:T(8,128)(2,1)S(1)} %fusion.17.refs_0_), channel_id=1, source_target_pairs={{0,2},{2,0},{1,3},{3,1},{4,6},{6,4},{5,7},{7,5},{8,10},{10,8},{9,1... | collective-permute-start | bytes 3145736 | tf_op jit(solution)/shard_map/ppermute | solution.py:22
  479.2 24.1 %collective-permute-start.43 = (bf16[256,2048]{1,0:T(8,128)(2,1)S(1)}, bf16[256,2048]{1,0:T(8,128)(2,1)S(1)}, u32[]{:S(2)}, u32[]{:S(2)}) collective-permute-start(bf16[256,2048]{1,0:T(8,128)(2,1)S(1)} %fusion.17.refs_0_), channel_id=1, source_target_pairs={{0,4},{4,0},{1,5},{5,1},{2,6},{6,2},{3,7},{7,3},{8,12},{12,8},{9,1... | collective-permute-start | bytes 3145736 | tf_op jit(solution)/shard_map/ppermute | solution.py:26
  523.2 26.8 %collective-permute-start.48 = (bf16[2,256,1024]{2,1,0:T(8,128)(2,1)}, bf16[2,256,1024]{2,1,0:T(8,128)(2,1)S(1)}, u32[]{:S(2)}, u32[]{:S(2)}) collective-permute-start(bf16[2,256,1024]{2,1,0:T(8,128)(2,1)} %slice_bitcast_fusion.15), channel_id=1, source_target_pairs={{0,2},{2,0},{1,3},{3,1},{4,6},{6,4},{5,7},{7,5},{8,10},{10,8},{9,1... | collective-permute-start | bytes 3145736 | tf_op jit(solution)/shard_map/ppermute | solution.py:22
  524.6 25.4 %collective-permute-start.49 = (bf16[2,256,1024]{2,1,0:T(8,128)(2,1)S(1)}, bf16[2,256,1024]{2,1,0:T(8,128)(2,1)S(1)}, u32[]{:S(2)}, u32[]{:S(2)}) collective-permute-start(bf16[2,256,1024]{2,1,0:T(8,128)(2,1)S(1)} %copy-done.72), channel_id=1, source_target_pairs={{0,4},{4,0},{1,5},{5,1},{2,6},{6,2},{3,7},{7,3},{8,12},{12,8},{9,1... | collective-permute-start | bytes 3145736 | tf_op jit(solution)/shard_map/ppermute | solution.py:26
  550.1 25.1 %collective-permute-start.50 = (bf16[4,2,144,128]{3,2,1,0:T(8,128)(2,1)S(1)}, bf16[4,2,144,128]{3,2,1,0:T(8,128)(2,1)S(1)}, u32[]{:S(2)}, u32[]{:S(2)}) collective-permute-start(bf16[4,2,144,128]{3,2,1,0:T(8,128)(2,1)S(1)} %get-tuple-element.183), channel_id=1, source_target_pairs={{8,0},{16,8},{24,16},{9,1},{17,9},{25,17},{10,2},{18,10},{26,18},{... | collective-permute-start | bytes 884744 | tf_op jit(solution)/shard_map/ppermute | solution.py:123
  582.8 104.9 %reduce-scatter.11.cloned.1.call-start = ((), (), s32[]{:S(2)}) async-start(), calls=%async_computation.22 | async-start | bytes 1310720 | tf_op jit(solution)/shard_map/reduce_scatter | solution.py:681
  603.9 83.8 %reduce-scatter.13.cloned.1.call-start = ((), (), s32[]{:S(2)}) async-start(), calls=%async_computation.23 | async-start | bytes 2621440 | tf_op jit(solution)/shard_map/reduce_scatter | solution.py:681
  605.3 101.7 %reduce-scatter.17.cloned.1.call-start = ((), (), s32[]{:S(2)}) async-start(), calls=%async_computation.25 | async-start | bytes 2621440 | tf_op jit(solution)/shard_map/reduce_scatter | solution.py:681
  695.5 56.7 %collective-permute-start.57 = (bf16[2,256,1024]{2,1,0:T(8,128)(2,1)}, bf16[2,256,1024]{2,1,0:T(8,128)(2,1)}, u32[]{:S(2)}, u32[]{:S(2)}) collective-permute-start(bf16[2,256,1024]{2,1,0:T(8,128)(2,1)} %slice_bitcast_fusion.11), channel_id=1, source_target_pairs={{0,2},{2,0},{1,3},{3,1},{4,6},{6,4},{5,7},{7,5},{8,10},{10,8},{9,1... | collective-permute-start | bytes 3145736 | tf_op jit(solution)/shard_map/ppermute | solution.py:22
  697.5 54.8 %collective-permute-start.58 = (bf16[2,256,1024]{2,1,0:T(8,128)(2,1)}, bf16[2,256,1024]{2,1,0:T(8,128)(2,1)}, u32[]{:S(2)}, u32[]{:S(2)}) collective-permute-start(bf16[2,256,1024]{2,1,0:T(8,128)(2,1)} %slice_bitcast_fusion.10), channel_id=1, source_target_pairs={{0,4},{4,0},{1,5},{5,1},{2,6},{6,2},{3,7},{7,3},{8,12},{12,8},{9,1... | collective-permute-start | bytes 3145736 | tf_op jit(solution)/shard_map/ppermute | solution.py:26
  (171 other events, 1763.9 us)
Sparse Core Ops, SparseCore 0:
  9.6 30.6 all-gather.14
  42.9 47.1 all-gather.6
  110.2 44.6 all-gather.8
  210.0 104.0 all-gather.10
  317.2 56.4 all-gather.12
  397.8 55.0 reduce-scatter.6
  460.0 54.9 reduce-scatter.8
  519.6 61.0 reduce-scatter.14
  585.9 29.7 reduce-scatter.10
  618.0 42.9 reduce-scatter.12
  663.3 43.7 reduce-scatter.16

commit v3 on v2

--- a/solution.py
+++ b/solution.py
@@ -28,10 +28,6 @@
 
 def swap_row(a):
     return lax.ppermute(a, "row", swap)
-
-
-def after(value, *others):
-    return lax.optimization_barrier((value,) + others)[0]
 
 
 def join(*groups):
@@ -85,31 +81,30 @@
     return gather_last(gather_second(*gather_first(a)))
 
 
-def scatter_first(near, far):
-    rows, columns = near.shape
-    half = columns // 2
-    mine = near.astype(f32) + swap_row(far.astype(bf16)).astype(f32)
-    mine = mine.reshape(2, 2, rows // 4, columns)
-    left, right = mine[..., :half], mine[..., half:]
-    return left[:, 0], right[0], left[:, 1].astype(bf16), right[1].astype(bf16)
-
-
 def scatter_second(left, right, to_x, to_y):
     return left, right, swap_x(to_x), swap_y(to_y)
 
 
-def scatter_third(left, right, from_x, from_y):
+def scatter_sums(left, right, from_x, from_y):
     left = left + from_x.astype(f32)
     right = right + from_y.astype(f32)
-    return left[0], right[0], swap_y(left[1].astype(bf16)), swap_x(right[1].astype(bf16))
+    return left[0], right[0], left[1].astype(bf16), right[1].astype(bf16)
+
+
+def scatter_fourth(left, right, to_y, to_x):
+    return left, right, swap_y(to_y), swap_x(to_x)
+
+
+def scatter_third(*state):
+    return scatter_fourth(*scatter_sums(*state))
 
 
 def scatter_last(left, right, from_y, from_x):
     return jnp.concatenate([left + from_y.astype(f32), right + from_x.astype(f32)], axis=-1)
 
 
-def scatter_group(near, far, first=(), second=()):
-    state, first = join(scatter_second(*scatter_first(near, far)), first)
+def scatter_group(state, first=(), second=()):
+    state, first = join(scatter_second(*state), first)
     state, second = join(scatter_third(*state), second)
     return scatter_last(*state), *first, *second
 
@@ -457,6 +452,158 @@
     )(at, docs, *ins)
 
 
+def big_call(kernel, grid, ins, in_specs, out_shapes, out_specs):
+    return pl.pallas_call(
+        kernel,
+        grid=grid,
+        in_specs=in_specs,
+        out_shape=out_shapes,
+        out_specs=out_specs,
+        compiler_params=pltpu.CompilerParams(
+            dimension_semantics=("arbitrary",) * len(grid), vmem_limit_bytes=48 * 1024 * 1024
+        ),
+    )(*ins)
+
+
+def up_kernel(in_ref, pair_ref, slope_ref, product_ref):
+    both = jnp.dot(in_ref[...], pair_ref[...], preferred_element_type=f32)
+    units = both.shape[1] // 2
+    gate, up = both[:, :units], both[:, units:]
+    gate_on = jax.nn.sigmoid(gate)
+    active = gate * gate_on
+    product_ref[...] = (active * up).astype(bf16)
+    slope_ref[0] = up * (gate_on + active * (1.0 - gate_on))
+    slope_ref[1] = active
+
+
+def down_kernel(grad_ref, down_ref, slope_ref, out_ref):
+    grad = jnp.dot(grad_ref[...], down_ref[...], preferred_element_type=f32)
+    out_ref[...] = jnp.concatenate(
+        [grad * slope_ref[0], grad * slope_ref[1]], axis=-1
+    ).astype(bf16)
+
+
+def feed_up(mid_all, pair_all, tile):
+    rows, features = mid_all.shape
+    units = pair_all.shape[1]
+    return big_call(
+        up_kernel,
+        (rows // tile,),
+        (mid_all, pair_all),
+        [
+            pl.BlockSpec((tile, features), lambda i: (i, 0)),
+            pl.BlockSpec((features, units), lambda i: (0, 0)),
+        ],
+        (
+            jax.ShapeDtypeStruct((2, rows, units // 2), f32),
+            jax.ShapeDtypeStruct((rows, units // 2), bf16),
+        ),
+        (
+            pl.BlockSpec((2, tile, units // 2), lambda i: (0, i, 0)),
+            pl.BlockSpec((tile, units // 2), lambda i: (i, 0)),
+        ),
+    )
+
+
+def feed_back(grad_all, down_all, both, tile):
+    rows, features = grad_all.shape
+    units = 2 * both.shape[2]
+    return big_call(
+        down_kernel,
+        (rows // tile,),
+        (grad_all, down_all, both),
+        [
+            pl.BlockSpec((tile, features), lambda i: (i, 0)),
+            pl.BlockSpec((features, units // 2), lambda i: (0, 0)),
+            pl.BlockSpec((2, tile, units // 2), lambda i: (0, i, 0)),
+        ],
+        jax.ShapeDtypeStruct((rows, units), bf16),
+        pl.BlockSpec((tile, units), lambda i: (i, 0)),
+    )
+
+
+def scatter_product(left, far_left, right, tile):
+    depth = left.shape[1]
+    columns = right.shape[1]
+    half = columns // 2
+
+    def dot(a_ref, b_ref):
+        return jnp.dot(a_ref[...], b_ref[...], preferred_element_type=f32)
+
+    def right_spec(side):
+        return pl.BlockSpec((depth, half), lambda *_: (0, side))
+
+    def far_kernel(a_ref, b_ref, out_ref):
+        out_ref[...] = dot(a_ref, b_ref).astype(bf16)
+
+    def far_part(side):
+        return big_call(
+            far_kernel,
+            (4,),
+            (far_left, right),
+            [pl.BlockSpec((tile, depth), lambda i: (i, 0)), right_spec(side)],
+            jax.ShapeDtypeStruct((4 * tile, half), bf16),
+            pl.BlockSpec((tile, half), lambda i: (i, 0)),
+        )
+
+    def near_part(side, got):
+        def kernel(a_ref, b_ref, got_ref, keep_ref, send_ref):
+            value = dot(a_ref, b_ref) + got_ref[...].astype(f32)
+            sent = pl.program_id(0) if side else pl.program_id(1)
+
+            @pl.when(sent == 0)
+            def _():
+                keep_ref[0] = value
+
+            @pl.when(sent == 1)
+            def _():
+                send_ref[0] = value.astype(bf16)
+
+        if side:
+            keep_at = lambda y, x: (jnp.where(y == 0, x, 1), 0, 0)
+            send_at = lambda y, x: (jnp.where(y == 0, 0, x), 0, 0)
+        else:
+            keep_at = lambda y, x: (y, 0, 0)
+            send_at = lambda y, x: (y, 0, 0)
+        return big_call(
+            kernel,
+            (2, 2),
+            (left, right, got),
+            [
+                pl.BlockSpec((tile, depth), lambda y, x: (2 * y + x, 0)),
+                right_spec(side),
+                pl.BlockSpec((tile, half), lambda y, x: (2 * y + x, 0)),
+            ],
+            (
+                jax.ShapeDtypeStruct((2, tile, half), f32),
+                jax.ShapeDtypeStruct((2, tile, half), bf16),
+            ),
+            (
+                pl.BlockSpec((1, tile, half), keep_at),
+                pl.BlockSpec((1, tile, half), send_at),
+            ),
+        )
+
+    got = [swap_row(far_part(side)) for side in range(2)]
+    (keep_left, to_x), (keep_right, to_y) = [near_part(side, got[side]) for side in range(2)]
+    return keep_left, keep_right, to_x, to_y
+
+
+def scatter_turned(left, right):
+    half = left.shape[0] // 2
+    far = times_transpose(left[half:], right).astype(bf16)
+    near = times_transpose(left[:half], right)
+    rows, columns = near.shape
+    mine = (near + swap_row(far).astype(f32)).reshape(2, 2, rows // 4, columns)
+    left_side, right_side = mine[..., : columns // 2], mine[..., columns // 2 :]
+    return (
+        left_side[:, 0],
+        right_side[0],
+        left_side[:, 1].astype(bf16),
+        right_side[1].astype(bf16),
+    )
+
+
 def contract_rows(left, right):
     return lax.dot_general(left, right, (TN, ((), ())), preferred_element_type=f32)
 
@@ -534,12 +681,10 @@
     vectors = jnp.stack([norm_gain, mlp_gain, group_gain, forget_bias]).astype(f32)
     vectors = jnp.broadcast_to(vectors.reshape(1, 4 * share), (groups * members, 4 * share))
     vectors = lax.all_to_all(vectors, everywhere, 0, 0, tiled=True)
-    mixer_cut = over_group(
-        after(
-            jnp.stack([cut_heads(w_forget, w_input), cut_heads(w_query, w_outgate)], axis=1),
-            vectors,
-        )
-    )
+    mixer_cut, vectors = join(
+        jnp.stack([cut_heads(w_forget, w_input), cut_heads(w_query, w_outgate)], axis=1), vectors
+    )
+    mixer_cut = over_group(mixer_cut)
     zv_all = over_groups(mixer_cut[:, 0])
     qr_all = over_groups(mixer_cut[:, 1])
 
@@ -554,19 +699,20 @@
     input_float = block_input.astype(f32).reshape(tokens, features)
     first_rate = rms_rate(input_float)
     normed = (input_float * first_rate * first_gain).astype(bf16)
-    normed_all = gather_group(normed)
-
     pair_cut = jnp.concatenate(
         [w_gate.reshape(block, spots, units), w_up.reshape(block, spots, units)], axis=-1
     ).transpose(1, 0, 2)
-    pair_cut = over_plane(after(pair_cut, normed_all))
     down_cut = w_down.T.reshape(block, spots, units).transpose(1, 0, 2)
-    down_cut = over_plane(after(down_cut, pair_cut)).reshape(spots * block, units)
+
+    first, pair_cut, down_cut = join(gather_first(normed), pair_cut, down_cut)
+    normed_all = gather_last(gather_second(*first))
 
     docs = jnp.concatenate([doc_starts, swap_row(doc_starts)], axis=0)
     at = jnp.stack([own_spot, lax.axis_index("z") * (spots * span)]).astype(jnp.int32)
     by_block = (members, row_count, span)
     zv = times(normed_all, zv_all).reshape(by_block + (2 * wide,))
+    zv, pair_cut, down_cut = join(zv, pair_cut, down_cut)
+    pair_cut = over_plane(pair_cut)
 
     once = pl.BlockSpec((1, wide), lambda *_: (0, 0))
     packed_block = (row_count, heads, width + PAD, width)
@@ -598,11 +744,16 @@
     )
     grad_low = out_grad.reshape(tokens, features)
 
-    packed, pair_cut = join(packed, pair_cut.reshape(spots * block, 2 * units))
-    pair_all = lax.all_gather(pair_cut, "z", axis=0, tiled=True)
-    gate_all, up_all = pair_all[:, :units], pair_all[:, units:]
-    carried = relay(packed, True)
-    near = gather_second(*gather_first(after(grad_low, pair_cut)))
+    carried = []
+    for step in range(groups - 1):
+        packed = hop(packed, True)
+        if step == 0:
+            packed, pair_cut = join(packed, pair_cut.reshape(spots * block, 2 * units))
+            grad_sent, down_cut, pair_cut = join(grad_low, down_cut, pair_cut)
+            pair_all = lax.all_gather(pair_cut, "z", axis=0, tiled=True)
+            near = gather_second(*gather_first(grad_sent))
+            down_cut = over_plane(down_cut).reshape(spots * block, units)
+        carried.append(packed)
     qr = times(normed_all, qr_all)
     carried, near, qr, down_cut = join(carried, near, qr, down_cut)
     down_all = lax.all_gather(down_cut, "z", axis=0, tiled=True)
@@ -658,11 +809,10 @@
 
     far_out, far_mixed, far_starts = forward_half(1, qr)
     far_mixed = far_mixed.reshape(half, wide)
-    far_part = times(far_mixed, out_here).astype(bf16)
-    near_out, near_mixed, near_starts = forward_half(0, after(qr, far_part))
+    near_out, near_mixed, near_starts = forward_half(0, qr)
     near_mixed = near_mixed.reshape(half, wide)
-    near_part = times(near_mixed, out_here)
-    hidden = input_float + scatter_group(near_part, far_part)[0]
+    state = scatter_product(near_mixed, far_mixed, out_here, tokens)
+    hidden = input_float + scatter_group(state)[0]
 
     mid_rate = rms_rate(hidden)
     first, grad_all, mixer_weights = join(
@@ -671,39 +821,26 @@
         jnp.concatenate([qr_all, zv_all], axis=1),
     )
     mid_all = gather_last(gather_second(*first))
-    gate_a = times(mid_all, gate_all)
-    up_b = times(mid_all, up_all)
-    gate_on = jax.nn.sigmoid(gate_a)
-    gate_act = gate_a * gate_on
-    product = (gate_act * up_b).astype(bf16)
+    both, product = feed_up(mid_all, pair_all, tokens)
 
     def spread(partial):
         return lax.psum_scatter(partial.astype(bf16), "z", scatter_dimension=0, tiled=True)
 
     down_part = contract_rows(grad_all, product).astype(bf16)
     grad_down = spread(down_part)
-    grad_product = times(after(grad_all, down_part), down_all)
-    grad_a = (grad_product * up_b * gate_on * (1.0 + gate_a * (1.0 - gate_on))).astype(bf16)
-    grad_b = (grad_product * gate_act).astype(bf16)
-    far_mid = times_transpose(grad_a[half:], gate_all) + times_transpose(grad_b[half:], up_all)
-    far_mid = far_mid.astype(bf16)
-    near_mid = times_transpose(grad_a[:half], gate_all) + times_transpose(grad_b[:half], up_all)
-    held_mid, held_a, held_b = lax.optimization_barrier((mid_all, grad_a, grad_b, near_mid))[:3]
-    gate_part = contract_rows(held_mid, held_a).astype(bf16)
-    up_part = contract_rows(held_mid, held_b).astype(bf16)
-    grad_mid, gate_part, up_part, grad_down = scatter_group(
-        near_mid, far_mid, (gate_part, up_part), (grad_down,)
-    )
-    grad_gate = spread(gate_part)
-    grad_up = spread(up_part)
+    grad_both = feed_back(grad_all, down_all, both, tokens)
+    state, mid_late, both_late, product = join(
+        scatter_turned(grad_both, pair_all), mid_all, grad_both, product
+    )
+    pair_part = contract_rows(mid_late, both_late).astype(bf16)
+    grad_mid, pair_part, grad_down = scatter_group(state, (pair_part,), (grad_down,))
+    grad_pair = spread(pair_part)
     grad_float = out_grad.astype(f32).reshape(tokens, features)
     grad_hidden = grad_float + rms_back(grad_mid * mid_gain, hidden, mid_rate)
 
-    product_here = after(product, up_part)
-    far_down = times_transpose(product_here[half:], down_all).astype(bf16)
-    near_down = times_transpose(product_here[:half], down_all)
     first, sums = join(
-        gather_first(grad_hidden.astype(bf16)), scatter_first(near_down, far_down)
+        gather_first(grad_hidden.astype(bf16)),
+        scatter_turned(product, down_all),
     )
     near_gm = lay(gather_second(*first))
     far_gm = swap_row(near_gm)
@@ -751,22 +888,28 @@
         qr_grads = all_grads.reshape(2 * half, 4 * wide)[:, : 2 * wide]
         return contract_rows(normed_all, qr_grads).astype(bf16)
 
-    def join_units(back):
-        return back.astype(f32).transpose(1, 0, 2).reshape(block, spots * units)
-
     def turn_units(back):
         return back.transpose(0, 2, 1).reshape(spots * units, block).astype(f32)
 
-    def units_back(cut):
-        return over_plane(cut.reshape(spots, block, units))
+    def pair_parts(back):
+        return [
+            jnp.concatenate(
+                [back[spot, :, low : low + units].astype(f32) for spot in range(spots)], axis=1
+            )
+            for low in (0, units)
+        ]
+
+    packed, grad_down = join(packed, grad_down)
+    down_back = over_plane(grad_down.reshape(spots, block, units))
+    pair_back = over_plane(grad_pair.reshape(spots, block, 2 * units))
 
     def beside(step):
         if step == 0:
-            return (out_rows(), scatter_third(*sums))
+            return (out_rows(), scatter_third(*sums), down_back)
         if step == 1:
-            return (query_part(), turn_units(units_back(after(grad_down, later[0]))))
+            return (query_part(), turn_units(done[2]), pair_back)
         if step == 2:
-            return (join_units(units_back(after(grad_gate, later[1]))),)
+            return tuple(pair_parts(done[5]))
         return ()
 
     later = []
@@ -775,7 +918,7 @@
         packed, extra = join(hop(packed, False), beside(step))
         later.append(packed)
         done += extra
-    grad_out_rows, sums, qr_part, grad_down, grad_gate = done
+    grad_out_rows, sums, _, qr_part, grad_down, _, grad_gate, grad_up = done
     block_output = (hidden + scatter_last(*sums)).astype(bf16)
     if by_chip:
         cut = grad_out_rows.reshape(heads, 2, share, features)
@@ -827,10 +970,9 @@
     )
     all_grads = all_grads.reshape(2 * half, 4 * wide)
     zv_part = contract_rows(normed_all, all_grads[:, 2 * wide :]).astype(bf16)
+    late_grads, zv_part = join(all_grads, zv_part)
     grad_zv = spread(zv_part)
-    late_grads = after(all_grads, zv_part)
-    far_in = times_transpose(late_grads[half:], mixer_weights).astype(bf16)
-    near_in = times_transpose(late_grads[:half], mixer_weights)
+    state = scatter_turned(late_grads, mixer_weights)
     bias_placed = jnp.zeros((2, heads, spots, width), f32)
     bias_placed = lax.dynamic_update_slice(
         bias_placed, bias_part.reshape(1, heads, 1, width), (own_row, 0, own_spot, 0)
@@ -848,18 +990,14 @@
             for at in range(2)
         ]
 
-    state, block_output, grad_out, grad_qr, grad_up = join(
-        scatter_first(near_in, far_in), block_output, grad_out, grad_qr, grad_up
-    )
+    state, block_output, grad_out, grad_qr = join(state, block_output, grad_out, grad_qr)
     grad_out = grad_out.astype(f32)
-    state, (query_back, outgate_back), grad_up, grad_out, block_output = join(
-        scatter_second(*state),
-        join_heads(grad_qr),
-        join_units(units_back(grad_up)),
-        grad_out,
-        block_output,
-    )
-    grad_normed = scatter_last(*scatter_third(*state))
+    state, (query_back, outgate_back), grad_out, block_output = join(
+        scatter_second(*state), join_heads(grad_qr), grad_out, block_output
+    )
+    state, grad_zv = join(scatter_sums(*state), grad_zv)
+    state, (forget_back, input_back) = join(scatter_fourth(*state), join_heads(grad_zv))
+    grad_normed = scatter_last(*state)
     input_grad = grad_hidden + rms_back(grad_normed * first_gain, input_float, first_rate)
     input_grad = input_grad.astype(bf16).reshape(block_input.shape)
 
@@ -872,7 +1010,6 @@
     mid_give = lax.dynamic_index_in_dim(mid_part, 1 - own_row, 0, False)
     grad_mid_gain = (mid_keep + swap_row(mid_give)) / own_vectors[1]
 
-    forget_back, input_back = join_heads(grad_zv)
     first_part = query_back * w_query.astype(f32) + outgate_back * w_outgate.astype(f32)
     first_part += forget_back * w_forget.astype(f32) + input_back * w_input.astype(f32)
     grad_first_gain = jnp.sum(first_part, axis=1) / own_vectors[0]

time: 795 us -> 760 us (0.956)
  waiting for transfers between devices: 244 us -> 178 us
  matrix products: 179 us -> 126 us
  Pallas kernels: 95.7 us -> 143 us
  blocking collectives: 0 us -> 17.9 us
  other arithmetic: 58.5 us -> 67 us
    pallas_call x0 -> x6, Pallas kernels: none -> 48.3 us  [big_call(): pl.pallas_call(kernel, grid=grid, in_specs=in_specs, out_shape=out_shapes...]
    dot_general x7 -> x2, matrix products: 65 us -> 21 us  [times(): return jnp.dot(left, right, preferred_element_type=f32)]
    all_to_all x3 -> x2, waiting for transfers between devices: 29.4 us -> 6.52 us  [over_group(): return lax.all_to_all(cut, group, 0, 0, tiled=True)]
    all_to_all x5 -> x4, waiting for transfers between devices: 37.5 us -> 16.2 us  [over_plane(): return lax.all_to_all(cut, plane, 0, 0, tiled=True)]
    all_to_all x0 -> x1, blocking collectives: none -> 17.9 us  [over_group(): return lax.all_to_all(cut, group, 0, 0, tiled=True)]
    ppermute x6, starting transfers between devices: 13.9 us -> 29 us  [hop(): return lax.ppermute(packed, 'z', pairs)]
    ppermute x16, waiting for transfers between devices: 80.1 us -> 66.7 us  [swap_x(): return lax.ppermute(a, 'x', swap)]
    all_gather x1, waiting for transfers between devices: 11.9 us -> 0.01 us  [on_device(): down_all = lax.all_gather(down_cut, 'z', axis=0, tiled=True)]
  transfers between devices with their start and end apart: 83 -> 81, of which waited for: 34 -> 43; matrix products, arithmetic and copies ran while one was open for 36% -> 33% of each run, Pallas kernels for 11% -> 17%
where the time goes in v3:
time: 760 us; the launch traced here: 749 us
  waiting for transfers between devices  178 us (23%)
  Pallas kernels  143 us (19%)
  matrix products  126 us (17%)
  starting transfers between devices  101 us (13%)
  local copies, waits for them, and re-layouts  100 us (13%)
  other arithmetic  67 us (9%)
  blocking collectives  17.9 us (2%)
  between operations  16 us (2%)
    pallas_call x5, Pallas kernels, local_call(): pl.pallas_call(kernel, grid_spec=pltpu.PrefetchScalarGridSpec(num_scalar_...  71.5 us
    ppermute x16, waiting for transfers between devices, swap_x(): return lax.ppermute(a, 'x', swap)  66.7 us
    dot_general x8, matrix products, times_transpose(): lax.dot_general(left, right, (NT, ((), ())), preferred_element_type=f32)  54.7 us
    ppermute x16, waiting for transfers between devices, swap_y(): return lax.ppermute(a, 'y', swap)  53.8 us
    dot_general x6, matrix products, contract_rows(): lax.dot_general(left, right, (TN, ((), ())), preferred_element_type=f32)  50.3 us
    pallas_call x6, Pallas kernels, big_call(): pl.pallas_call(kernel, grid=grid, in_specs=in_specs, out_shape=out_shapes...  48.3 us
    unnamed x220, local copies, waits for them, and re-layouts  32.5 us
    ppermute x6, starting transfers between devices, hop(): return lax.ppermute(packed, 'z', pairs)  29 us
  transfers between devices with their start and end apart: 81, of which 43 were waited for; matrix products, arithmetic and copies ran while one was open for 33% of the time, Pallas kernels for 17%

profile of v3, /device:TPU:0, one launch (start us, length us, event | category | flops | bytes accessed | tf_op | source)
XLA Modules:
  0.0 748.9 jit_solution(10206870031890066989)
XLA Ops:
  8.6 7.3 all-to-all-start
  23.3 17.9 %all_to_all.53 = bf16[8,2,64,512]{3,2,1,0:T(8,128)(2,1)S(1)} all-to-all(bf16[8,2,64,512]{3,2,1,0:T(8,128)(2,1)S(1)} %copy.85), channel_id=1, replica_groups=mesh['z'=4,'y'=2,'x'=2,'row'=2] {'y','x','row'}, dimensions={0} | all-to-all | bytes 2097152 | tf_op jit(solution)/shard_map/all_to_all | solution.py:672
  52.7 16.1 %collective-permute-done.1.refs_1_ = bf16[256,2048]{1,0:T(8,128)(2,1)S(1)} collective-permute-done((bf16[256,2048]{1,0:T(8,128)(2,1)S(1)}, bf16[256,2048]{1,0:T(8,128)(2,1)S(1)}, u32[]{:S(2)}, u32[]{:S(2)}) %collective-permute-start.1) | collective-permute-done | bytes 1048608 | tf_op jit(solution)/shard_map/ppermute | solution.py:22
  73.3 12.0 %collective-permute-done.3.refs_3_ = bf16[128,2048]{1,0:T(8,128)(2,1)} collective-permute-done((bf16[128,2048]{1,0:T(8,128)(2,1)}, bf16[128,2048]{1,0:T(8,128)(2,1)}, u32[]{:S(2)}, u32[]{:S(2)}) %collective-permute-start.3) | collective-permute-done | bytes 524320 | tf_op jit(solution)/shard_map/ppermute | solution.py:26
  88.9 6.9 shard_map.254
  95.7 10.4 %fusion.48 = f32[2048,512]{1,0:T(8,128)} fusion(bf16[2048,2048]{1,0:T(8,128)(2,1)} %shard_map.254, bf16[2048,512]{1,0:T(8,128)(2,1)} %all-gather.7.cloned.1.call-done), kind=kOutput, calls=%fused_computation.168 | convolution fusion | flops 4294967296 | bytes 14680064 | tf_op jit(solution)/shard_map/dot_general | solution.py:616
  139.6 9.2 %collective-permute-start.11 = (bf16[4,2,144,128]{3,2,1,0:T(8,128)(2,1)S(1)}, bf16[4,2,144,128]{3,2,1,0:T(8,128)(2,1)}, u32[]{:S(2)}, u32[]{:S(2)}) collective-permute-start(bf16[4,2,144,128]{3,2,1,0:T(8,128)(2,1)S(1)} %collective-permute-done.10.refs_6_), channel_id=1, source_target_pairs={{0,8},{8,16},{16,24},{1,9},{9,17},{17,25},{2,10},{10,18},{18,26},{... | collective-permute-start | bytes 884744 | tf_op jit(solution)/shard_map/ppermute | solution.py:118
  154.3 7.1 collective-permute-done.11.refs_7_
  161.4 12.4 %collective-permute-start.12 = (bf16[4,2,144,128]{3,2,1,0:T(8,128)(2,1)}, bf16[4,2,144,128]{3,2,1,0:T(8,128)(2,1)}, u32[]{:S(2)}, u32[]{:S(2)}) collective-permute-start(bf16[4,2,144,128]{3,2,1,0:T(8,128)(2,1)} %collective-permute-done.11.refs_7_), channel_id=1, source_target_pairs={{0,8},{8,16},{16,24},{1,9},{9,17},{17,25},{2,10},{10,18},{18,26},{... | collective-permute-start | bytes 884744 | tf_op jit(solution)/shard_map/ppermute | solution.py:118
  177.2 10.6 %fusion.49 = f32[2048,512]{1,0:T(8,128)} fusion(bf16[2048,2048]{1,0:T(8,128)(2,1)} %shard_map.254, bf16[2048,512]{1,0:T(8,128)(2,1)} %all-gather.9.cloned.1.call-done), kind=kOutput, calls=%fused_computation.169 | convolution fusion | flops 4294967296 | bytes 14680064 | tf_op jit(solution)/shard_map/dot_general | solution.py:616
  190.1 11.0 %shard_map.257 = (f32[4,2,128,256]{3,2,1,0:T(8,128)S(1)}, bf16[4,2,128,256]{3,2,1,0:T(8,128)(2,1)S(1)}, f32[4,2,2,128,128]{4,3,2,1,0:T(8,128)S(1)}) custom-call(s32[2]{0:T(128)S(1)} %pad_add_fusion.1.at_ref.refs_0_, s32[4,4]{1,0:T(4,128)S(1)} %pad_add_fusion.docs_ref.refs_1_, f32[8,2,128,512]{3,2,1,0:T(8,128)} %bitcast.270, f32[8,2,128,512]{3,2,1,0:T(8,128)} %bitcast.248, ...), custom_call_target="tpu_custom_call" | custom-call | tf_op jit(solution)/shard_map/pallas_call | solution.py:438
  204.5 11.0 %shard_map.256 = (f32[4,2,128,256]{3,2,1,0:T(8,128)S(1)}, bf16[4,2,128,256]{3,2,1,0:T(8,128)(2,1)S(1)}, f32[4,2,2,128,128]{4,3,2,1,0:T(8,128)S(1)}) custom-call(s32[2]{0:T(128)S(1)} %pad_add_fusion.1.at_ref.refs_0_, s32[4,4]{1,0:T(4,128)S(1)} %pad_add_fusion.docs_ref.refs_1_, f32[8,2,128,512]{3,2,1,0:T(8,128)} %bitcast.271, f32[8,2,128,512]{3,2,1,0:T(8,128)} %bitcast.249, ...), custom_call_target="tpu_custom_call" | custom-call | tf_op jit(solution)/shard_map/pallas_call | solution.py:438
  234.0 14.8 %collective-permute-done.20 = bf16[2,256,1024]{2,1,0:T(8,128)(2,1)} collective-permute-done((bf16[2,256,1024]{2,1,0:T(8,128)(2,1)}, bf16[2,256,1024]{2,1,0:T(8,128)(2,1)}, u32[]{:S(2)}, u32[]{:S(2)}) %collective-permute-start.20) | collective-permute-done | bytes 1048608 | tf_op jit(solution)/shard_map/ppermute | solution.py:22
  248.8 8.2 %collective-permute-done.21 = bf16[2,256,1024]{2,1,0:T(8,128)(2,1)} collective-permute-done((bf16[2,256,1024]{2,1,0:T(8,128)(2,1)}, bf16[2,256,1024]{2,1,0:T(8,128)(2,1)}, u32[]{:S(2)}, u32[]{:S(2)}) %collective-permute-start.21) | collective-permute-done | bytes 1048608 | tf_op jit(solution)/shard_map/ppermute | solution.py:26
  289.1 7.4 shard_map.262.grad_ref
  296.6 11.3 %collective-permute-done.24.refs_1_ = bf16[256,2048]{1,0:T(8,128)(2,1)S(1)} collective-permute-done((bf16[256,2048]{1,0:T(8,128)(2,1)S(1)}, bf16[256,2048]{1,0:T(8,128)(2,1)S(1)}, u32[]{:S(2)}, u32[]{:S(2)}) %collective-permute-start.24) | collective-permute-done | bytes 1048608 | tf_op jit(solution)/shard_map/ppermute | solution.py:22
  311.0 11.6 %collective-permute-done.31.refs_3_ = bf16[128,2048]{1,0:T(8,128)(2,1)S(1)} collective-permute-done((bf16[128,2048]{1,0:T(8,128)(2,1)S(1)}, bf16[128,2048]{1,0:T(8,128)(2,1)S(1)}, u32[]{:S(2)}, u32[]{:S(2)}) %collective-permute-start.31) | collective-permute-done | bytes 524320 | tf_op jit(solution)/shard_map/ppermute | solution.py:26
  331.9 21.2 %shard_map.264 = (f32[2,2048,704]{2,1,0:T(8,128)}, bf16[2048,704]{1,0:T(8,128)(2,1)S(1)}) custom-call(bf16[2048,2048]{1,0:T(8,128)(2,1)} %shard_map.263.in_ref, bf16[2048,1408]{1,0:T(8,128)(2,1)} %all-gather.13.cloned.1.call-done.pair_ref), custom_call_target="tpu_custom_call" | custom-call | tf_op jit(solution)/shard_map/pallas_call | solution.py:456
  356.7 16.3 %shard_map.265 = bf16[2048,1408]{1,0:T(8,128)(2,1)} custom-call(bf16[2048,2048]{1,0:T(8,128)(2,1)} %shard_map.262.grad_ref, bf16[2048,704]{1,0:T(8,128)(2,1)S(1)} %copy-done.2, f32[2,2048,704]{2,1,0:T(8,128)} %get-tuple-element.194.slope_ref), custom_call_target="tpu_custom_call" | custom-call | tf_op jit(solution)/shard_map/pallas_call | solution.py:456
  372.9 10.2 %convolution_convert_fusion.1 = bf16[1024,2048]{1,0:T(8,128)(2,1)} fusion(bf16[2048,1408]{1,0:T(8,128)(2,1)S(1)} %copy-done.58, bf16[2048,1408]{1,0:T(8,128)(2,1)} %shard_map.265), kind=kOutput, calls=%fused_computation.5 | convolution fusion | flops 5907677184 | bytes 12845056 | tf_op jit(solution)/shard_map/dot_general | solution.py:612
  383.4 7.8 %convolution_convert_fusion.4 = bf16[2048,704]{0,1:T(8,128)(2,1)} fusion(bf16[2048,2048]{1,0:T(8,128)(2,1)S(1)} %bitcast.281, bf16[2048,704]{1,0:T(8,128)(2,1)S(1)} %copy-done.25), kind=kOutput, calls=%fused_computation.8 | convolution fusion | flops 5907021824 | bytes 14155776 | tf_op jit(solution)/shard_map/dot_general | solution.py:608
  391.2 10.4 %convert_add_fusion.2 = f32[1024,2048]{1,0:T(8,128)S(1)} fusion(bf16[1024,2048]{1,0:T(8,128)(2,1)} %collective-permute-done.38, bf16[2048,1408]{1,0:T(8,128)(2,1)} %all-gather.13.cloned.1.call-done.pair_ref, bf16[2048,1408]{1,0:T(8,128)(2,1)} %shard_map.265), kind=kOutput, calls=%fused_computation.2 | convolution fusion | flops 5909774336 | bytes 21233664 | tf_op jit(solution)/shard_map/dot_general | solution.py:612
  415.7 16.6 %convolution_convert_fusion = bf16[2048,1408]{1,0:T(8,128)(2,1)} fusion(bf16[2048,2048]{1,0:T(8,128)(2,1)S(1)} %bitcast.283, bf16[2048,1408]{1,0:T(8,128)(2,1)} %shard_map.265), kind=kOutput, calls=%fused_computation.3 | convolution fusion | flops 11814043648 | bytes 19922944 | tf_op jit(solution)/shard_map/dot_general | solution.py:608
  461.9 7.5 %convert_add_fusion.1 = f32[1024,2048]{1,0:T(8,128)} fusion(bf16[1024,2048]{1,0:T(8,128)(2,1)} %collective-permute-done.45, bf16[2048,704]{1,0:T(8,128)(2,1)S(1)} %copy-done.4, bf16[2048,704]{1,0:T(8,128)(2,1)S(1)} %copy-done.27), kind=kOutput, calls=%fused_computation.1 | convolution fusion | flops 2956984320 | bytes 17301504 | tf_op jit(solution)/shard_map/dot_general | solution.py:612
  485.9 8.3 %collective-permute-done.46.refs_3_ = bf16[128,2048]{1,0:T(8,128)(2,1)S(1)} collective-permute-done((bf16[128,2048]{1,0:T(8,128)(2,1)S(1)}, bf16[128,2048]{1,0:T(8,128)(2,1)S(1)}, u32[]{:S(2)}, u32[]{:S(2)}) %collective-permute-start.46) | collective-permute-done | bytes 524320 | tf_op jit(solution)/shard_map/ppermute | solution.py:26
  508.0 18.0 %shard_map.267 = (bf16[8,2,128,1024]{3,2,1,0:T(8,128)(2,1)}, f32[8,2,128,256]{3,2,1,0:T(8,128)S(1)}, f32[8,2,128,256]{3,2,1,0:T(8,128)S(1)}, bf16[4,2,144,128]{3,2,1,0:T(8,128)(2,1)S(1)}) custom-call(s32[2]{0:T(128)S(1)} %pad_add_fusion.1.at_ref.refs_0_, s32[4,4]{1,0:T(4,128)S(1)} %pad_add_fusion.docs_ref.refs_1_, f32[8,2,128,512]{3,2,1,0:T(8,128)} %bitcast.272, ...), custom_call_target="tpu_custom_call" | custom-call | tf_op jit(solution)/shard_map/pallas_call | solution.py:438
  564.0 10.1 %convolution_convert_fusion.6 = bf16[2048,512]{1,0:T(8,128)(2,1)} fusion(bf16[2048,2048]{1,0:T(8,128)(2,1)} %shard_map.254, bf16[2048,1024]{1,0:T(8,128)(2,1)} %bitcast.304), kind=kOutput, calls=%fused_computation.10 | convolution fusion | flops 4296015872 | bytes 12582912 | tf_op jit(solution)/shard_map/dot_general | solution.py:608
  598.8 25.4 %shard_map.268 = (bf16[8,2,128,1024]{3,2,1,0:T(8,128)(2,1)}, f32[1,256]{1,0:T(1,128)S(1)}) custom-call(s32[2]{0:T(128)S(1)} %pad_add_fusion.1.at_ref.refs_0_, s32[4,4]{1,0:T(4,128)S(1)} %pad_add_fusion.docs_ref.refs_1_, bf16[8,2,128,1024]{3,2,1,0:T(8,128)(2,1)} %get-tuple-element.216.kept_ref, ...), custom_call_target="tpu_custom_call", output_to_operand_aliasing={{0}: (2, {})} | custom-call | tf_op jit(solution)/shard_map/pallas_call | solution.py:438
  624.2 10.0 %convolution_convert_fusion.5 = bf16[2048,512]{1,0:T(8,128)(2,1)} fusion(bf16[2048,2048]{1,0:T(8,128)(2,1)} %shard_map.254, bf16[2048,1024]{1,0:T(8,128)(2,1)} %bitcast.305), kind=kOutput, calls=%fused_computation.9 | convolution fusion | flops 4296015872 | bytes 12582912 | tf_op jit(solution)/shard_map/dot_general | solution.py:608
  634.1 9.6 %convolution_convert_fusion.3 = bf16[1024,2048]{1,0:T(8,128)(2,1)} fusion(bf16[2048,1024]{1,0:T(8,128)(2,1)} %pad_maximum_fusion, bf16[2048,1024]{1,0:T(8,128)(2,1)} %bitcast.306), kind=kOutput, calls=%fused_computation.7 | convolution fusion | flops 4297064448 | bytes 10485760 | tf_op jit(solution)/shard_map/dot_general | solution.py:612
  651.2 9.2 %convert_add_fusion = f32[1024,2048]{1,0:T(8,128)S(1)} fusion(bf16[1024,2048]{1,0:T(8,128)(2,1)} %collective-permute-done.56, bf16[2048,1024]{1,0:T(8,128)(2,1)} %pad_maximum_fusion, bf16[2048,1024]{1,0:T(8,128)(2,1)} %bitcast.307), kind=kOutput, calls=%fused_computation | convolution fusion | flops 4299161600 | bytes 18874368 | tf_op jit(solution)/shard_map/dot_general | solution.py:612
  692.9 8.9 %collective-permute-done.58 = bf16[2,256,1024]{2,1,0:T(8,128)(2,1)} collective-permute-done((bf16[2,256,1024]{2,1,0:T(8,128)(2,1)}, bf16[2,256,1024]{2,1,0:T(8,128)(2,1)}, u32[]{:S(2)}, u32[]{:S(2)}) %collective-permute-start.58) | collective-permute-done | bytes 1048608 | tf_op jit(solution)/shard_map/ppermute | solution.py:22
  (534 shorter events, 358.2 us)
Async XLA Ops:
  15.9 79.8 %all-gather.7.cloned.1.call-start = ((), (), s32[]{:S(2)}) async-start(), calls=%async_computation.14 | async-start | bytes 2621440 | tf_op jit(solution)/shard_map/all_gather | solution.py:679
  42.2 92.4 %all-gather.15.cloned.1.call-start = ((), (), s32[]{:S(2)}) async-start(), calls=%async_computation.23 | async-start | bytes 1310720 | tf_op jit(solution)/shard_map/all_gather | solution.py:663
  43.0 134.2 %all-gather.9.cloned.1.call-start = ((), (), s32[]{:S(2)}) async-start(), calls=%async_computation.15 | async-start | bytes 2621440 | tf_op jit(solution)/shard_map/all_gather | solution.py:679
  44.5 24.3 %collective-permute-start.1 = (bf16[256,2048]{1,0:T(8,128)(2,1)S(1)}, bf16[256,2048]{1,0:T(8,128)(2,1)S(1)}, u32[]{:S(2)}, u32[]{:S(2)}) collective-permute-start(bf16[256,2048]{1,0:T(8,128)(2,1)S(1)} %fusion.19.refs_0_), channel_id=1, source_target_pairs={{0,2},{2,0},{1,3},{3,1},{4,6},{6,4},{5,7},{7,5},{8,10},{10,8},{9,1... | collective-permute-start | bytes 3145736 | tf_op jit(solution)/shard_map/ppermute | solution.py:22
  45.1 24.7 %collective-permute-start.2 = (bf16[256,2048]{1,0:T(8,128)(2,1)S(1)}, bf16[256,2048]{1,0:T(8,128)(2,1)S(1)}, u32[]{:S(2)}, u32[]{:S(2)}) collective-permute-start(bf16[256,2048]{1,0:T(8,128)(2,1)S(1)} %fusion.19.refs_0_), channel_id=1, source_target_pairs={{0,4},{4,0},{1,5},{5,1},{2,6},{6,2},{3,7},{7,3},{8,12},{12,8},{9,1... | collective-permute-start | bytes 3145736 | tf_op jit(solution)/shard_map/ppermute | solution.py:26
  109.9 222.1 %all-gather.13.cloned.1.call-start = ((), (), s32[]{:S(2)}) async-start(), calls=%async_computation.17 | async-start | bytes 7208960 | tf_op jit(solution)/shard_map/all_gather | solution.py:753
  135.8 38.0 %collective-permute-start.13 = (bf16[256,2048]{1,0:T(8,128)(2,1)S(1)}, bf16[256,2048]{1,0:T(8,128)(2,1)S(1)}, u32[]{:S(2)}, u32[]{:S(2)}) collective-permute-start(bf16[256,2048]{1,0:T(8,128)(2,1)S(1)} %bitcast.259), channel_id=1, source_target_pairs={{0,2},{2,0},{1,3},{3,1},{4,6},{6,4},{5,7},{7,5},{8,10},{10,8},{9,1... | collective-permute-start | bytes 3145736 | tf_op jit(solution)/shard_map/ppermute | solution.py:22
  138.2 36.5 %collective-permute-start.14 = (bf16[256,2048]{1,0:T(8,128)(2,1)S(1)}, bf16[256,2048]{1,0:T(8,128)(2,1)}, u32[]{:S(2)}, u32[]{:S(2)}) collective-permute-start(bf16[256,2048]{1,0:T(8,128)(2,1)S(1)} %bitcast.260), channel_id=1, source_target_pairs={{0,4},{4,0},{1,5},{5,1},{2,6},{6,2},{3,7},{7,3},{8,12},{12,8},{9,1... | collective-permute-start | bytes 3145736 | tf_op jit(solution)/shard_map/ppermute | solution.py:26
  150.0 37.8 %all-to-all-start.3 = ((bf16[4,128,704]{1,2,0:T(8,128)(2,1)}), bf16[4,128,704]{1,2,0:T(8,128)(2,1)}, u32[]{:S(2)}, u32[]{:S(2)}) async-start(bf16[4,128,704]{1,2,0:T(8,128)(2,1)} %bitcast.320), calls=%async_computation.3 | async-start | bytes 1441792 | tf_op jit(solution)/shard_map/all_to_all | solution.py:675
  154.2 200.6 %all-gather.11.cloned.1.call-start = ((), (), s32[]{:S(2)}) async-start(), calls=%async_computation.16 | async-start | bytes 3932160 | tf_op jit(solution)/shard_map/all_gather | solution.py:759
  161.4 28.7 %collective-permute-start.12 = (bf16[4,2,144,128]{3,2,1,0:T(8,128)(2,1)}, bf16[4,2,144,128]{3,2,1,0:T(8,128)(2,1)}, u32[]{:S(2)}, u32[]{:S(2)}) collective-permute-start(bf16[4,2,144,128]{3,2,1,0:T(8,128)(2,1)} %collective-permute-done.11.refs_7_), channel_id=1, source_target_pairs={{0,8},{8,16},{16,24},{1,9},{9,17},{17,25},{2,10},{10,18},{18,26},{... | collective-permute-start | bytes 884744 | tf_op jit(solution)/shard_map/ppermute | solution.py:118
  223.4 25.4 %collective-permute-start.20 = (bf16[2,256,1024]{2,1,0:T(8,128)(2,1)}, bf16[2,256,1024]{2,1,0:T(8,128)(2,1)}, u32[]{:S(2)}, u32[]{:S(2)}) collective-permute-start(bf16[2,256,1024]{2,1,0:T(8,128)(2,1)} %get-tuple-element.173), channel_id=1, source_target_pairs={{0,2},{2,0},{1,3},{3,1},{4,6},{6,4},{5,7},{7,5},{8,10},{10,8},{9,1... | collective-permute-start | bytes 3145736 | tf_op jit(solution)/shard_map/ppermute | solution.py:22
  231.4 25.6 %collective-permute-start.21 = (bf16[2,256,1024]{2,1,0:T(8,128)(2,1)}, bf16[2,256,1024]{2,1,0:T(8,128)(2,1)}, u32[]{:S(2)}, u32[]{:S(2)}) collective-permute-start(bf16[2,256,1024]{2,1,0:T(8,128)(2,1)} %get-tuple-element.174), channel_id=1, source_target_pairs={{0,4},{4,0},{1,5},{5,1},{2,6},{6,2},{3,7},{7,3},{8,12},{12,8},{9,1... | collective-permute-start | bytes 3145736 | tf_op jit(solution)/shard_map/ppermute | solution.py:26
  233.6 213.7 %reduce-scatter.6.cloned.1.call-start = ((), (), s32[]{:S(2)}) async-start(), calls=%async_computation.18 | async-start | bytes 3604480 | tf_op jit(solution)/shard_map/reduce_scatter | solution.py:827
  282.2 25.6 %collective-permute-start.24 = (bf16[256,2048]{1,0:T(8,128)(2,1)S(1)}, bf16[256,2048]{1,0:T(8,128)(2,1)S(1)}, u32[]{:S(2)}, u32[]{:S(2)}) collective-permute-start(bf16[256,2048]{1,0:T(8,128)(2,1)S(1)} %multiply_convert_fusion.refs_0_), channel_id=1, source_target_pairs={{0,2},{2,0},{1,3},{3,1},{4,6},{6,4},{5,7},{7,5},{8,10},{10,8},{9,1... | collective-permute-start | bytes 3145736 | tf_op jit(solution)/shard_map/ppermute | solution.py:22
  282.9 25.3 %collective-permute-start.25 = (bf16[256,2048]{1,0:T(8,128)(2,1)S(1)}, bf16[256,2048]{1,0:T(8,128)(2,1)S(1)}, u32[]{:S(2)}, u32[]{:S(2)}) collective-permute-start(bf16[256,2048]{1,0:T(8,128)(2,1)S(1)} %multiply_convert_fusion.refs_0_), channel_id=1, source_target_pairs={{0,4},{4,0},{1,5},{5,1},{2,6},{6,2},{3,7},{7,3},{8,12},{12,8},{9,1... | collective-permute-start | bytes 3145736 | tf_op jit(solution)/shard_map/ppermute | solution.py:26
  391.2 169.2 %reduce-scatter.8.cloned.1.call-start = ((), (), s32[]{:S(2)}) async-start(), calls=%async_computation.19 | async-start | bytes 7208960 | tf_op jit(solution)/shard_map/reduce_scatter | solution.py:827
  407.5 25.7 %collective-permute-start.39 = (bf16[2,256,1024]{2,1,0:T(8,128)(2,1)}, bf16[2,256,1024]{2,1,0:T(8,128)(2,1)}, u32[]{:S(2)}, u32[]{:S(2)}) collective-permute-start(bf16[2,256,1024]{2,1,0:T(8,128)(2,1)} %slice_bitcast_fusion.17), channel_id=1, source_target_pairs={{0,2},{2,0},{1,3},{3,1},{4,6},{6,4},{5,7},{7,5},{8,10},{10,8},{9,1... | collective-permute-start | bytes 3145736 | tf_op jit(solution)/shard_map/ppermute | solution.py:22
  409.1 25.3 %collective-permute-start.40 = (bf16[2,256,1024]{2,1,0:T(8,128)(2,1)}, bf16[2,256,1024]{2,1,0:T(8,128)(2,1)S(1)}, u32[]{:S(2)}, u32[]{:S(2)}) collective-permute-start(bf16[2,256,1024]{2,1,0:T(8,128)(2,1)} %slice_bitcast_fusion.16), channel_id=1, source_target_pairs={{0,4},{4,0},{1,5},{5,1},{2,6},{6,2},{3,7},{7,3},{8,12},{12,8},{9,1... | collective-permute-start | bytes 3145736 | tf_op jit(solution)/shard_map/ppermute | solution.py:26
  415.6 45.1 %collective-permute-start.45 = (bf16[1024,2048]{1,0:T(8,128)(2,1)}, bf16[1024,2048]{1,0:T(8,128)(2,1)}, u32[]{:S(2)}, u32[]{:S(2)}) collective-permute-start(bf16[1024,2048]{1,0:T(8,128)(2,1)} %convolution_convert_fusion.2), channel_id=1, source_target_pairs={{0,1},{1,0},{2,3},{3,2},{4,5},{5,4},{6,7},{7,6},{8,9},{9,8},{10,11... | collective-permute-start | bytes 12582920 | tf_op jit(solution)/shard_map/ppermute | solution.py:30
  459.8 22.9 %collective-permute-start.43 = (bf16[256,2048]{1,0:T(8,128)(2,1)S(1)}, bf16[256,2048]{1,0:T(8,128)(2,1)S(1)}, u32[]{:S(2)}, u32[]{:S(2)}) collective-permute-start(bf16[256,2048]{1,0:T(8,128)(2,1)S(1)} %fusion.11.refs_0_), channel_id=1, source_target_pairs={{0,2},{2,0},{1,3},{3,1},{4,6},{6,4},{5,7},{7,5},{8,10},{10,8},{9,1... | collective-permute-start | bytes 3145736 | tf_op jit(solution)/shard_map/ppermute | solution.py:22
  460.5 23.1 %collective-permute-start.44 = (bf16[256,2048]{1,0:T(8,128)(2,1)S(1)}, bf16[256,2048]{1,0:T(8,128)(2,1)S(1)}, u32[]{:S(2)}, u32[]{:S(2)}) collective-permute-start(bf16[256,2048]{1,0:T(8,128)(2,1)S(1)} %fusion.11.refs_0_), channel_id=1, source_target_pairs={{0,4},{4,0},{1,5},{5,1},{2,6},{6,2},{3,7},{7,3},{8,12},{12,8},{9,1... | collective-permute-start | bytes 3145736 | tf_op jit(solution)/shard_map/ppermute | solution.py:26
  500.5 26.2 %collective-permute-start.49 = (bf16[2,256,1024]{2,1,0:T(8,128)(2,1)}, bf16[2,256,1024]{2,1,0:T(8,128)(2,1)S(1)}, u32[]{:S(2)}, u32[]{:S(2)}) collective-permute-start(bf16[2,256,1024]{2,1,0:T(8,128)(2,1)} %slice_bitcast_fusion.13), channel_id=1, source_target_pairs={{0,2},{2,0},{1,3},{3,1},{4,6},{6,4},{5,7},{7,5},{8,10},{10,8},{9,1... | collective-permute-start | bytes 3145736 | tf_op jit(solution)/shard_map/ppermute | solution.py:22
  501.6 25.7 %collective-permute-start.50 = (bf16[2,256,1024]{2,1,0:T(8,128)(2,1)S(1)}, bf16[2,256,1024]{2,1,0:T(8,128)(2,1)S(1)}, u32[]{:S(2)}, u32[]{:S(2)}) collective-permute-start(bf16[2,256,1024]{2,1,0:T(8,128)(2,1)S(1)} %slice_bitcast_fusion.12), channel_id=1, source_target_pairs={{0,4},{4,0},{1,5},{5,1},{2,6},{6,2},{3,7},{7,3},{8,12},{12,8},{9,1... | collective-permute-start | bytes 3145736 | tf_op jit(solution)/shard_map/ppermute | solution.py:26
  527.3 22.5 %collective-permute-start.51 = (bf16[4,2,144,128]{3,2,1,0:T(8,128)(2,1)S(1)}, bf16[4,2,144,128]{3,2,1,0:T(8,128)(2,1)S(1)}, u32[]{:S(2)}, u32[]{:S(2)}) collective-permute-start(bf16[4,2,144,128]{3,2,1,0:T(8,128)(2,1)S(1)} %get-tuple-element.230), channel_id=1, source_target_pairs={{8,0},{16,8},{24,16},{9,1},{17,9},{25,17},{10,2},{18,10},{26,18},{... | collective-permute-start | bytes 884744 | tf_op jit(solution)/shard_map/ppermute | solution.py:118
  538.6 127.7 %reduce-scatter.10.cloned.1.call-start = ((), (), s32[]{:S(2)}) async-start(), calls=%async_computation.20 | async-start | bytes 1310720 | tf_op jit(solution)/shard_map/reduce_scatter | solution.py:827
  564.0 102.3 %reduce-scatter.12.cloned.1.call-start = ((), (), s32[]{:S(2)}) async-start(), calls=%async_computation.21 | async-start | bytes 2621440 | tf_op jit(solution)/shard_map/reduce_scatter | solution.py:827
  589.6 119.9 %reduce-scatter.14.cloned.1.call-start = ((), (), s32[]{:S(2)}) async-start(), calls=%async_computation.22 | async-start | bytes 2621440 | tf_op jit(solution)/shard_map/reduce_scatter | solution.py:827
  670.4 31.4 %collective-permute-start.58 = (bf16[2,256,1024]{2,1,0:T(8,128)(2,1)}, bf16[2,256,1024]{2,1,0:T(8,128)(2,1)}, u32[]{:S(2)}, u32[]{:S(2)}) collective-permute-start(bf16[2,256,1024]{2,1,0:T(8,128)(2,1)} %slice_bitcast_fusion.9), channel_id=1, source_target_pairs={{0,2},{2,0},{1,3},{3,1},{4,6},{6,4},{5,7},{7,5},{8,10},{10,8},{9,1... | collective-permute-start | bytes 3145736 | tf_op jit(solution)/shard_map/ppermute | solution.py:22
  672.4 29.5 %collective-permute-start.59 = (bf16[2,256,1024]{2,1,0:T(8,128)(2,1)}, bf16[2,256,1024]{2,1,0:T(8,128)(2,1)}, u32[]{:S(2)}, u32[]{:S(2)}) collective-permute-start(bf16[2,256,1024]{2,1,0:T(8,128)(2,1)} %slice_bitcast_fusion.8), channel_id=1, source_target_pairs={{0,4},{4,0},{1,5},{5,1},{2,6},{6,2},{3,7},{7,3},{8,12},{12,8},{9,1... | collective-permute-start | bytes 3145736 | tf_op jit(solution)/shard_map/ppermute | solution.py:26
  676.5 37.2 %collective-permute-start.62 = (f32[64]{0:T(128)S(1)}, f32[64]{0:T(128)S(1)}, u32[]{:S(2)}, u32[]{:S(2)}) collective-permute-start(f32[64]{0:T(128)S(1)} %fusion.42), channel_id=1, source_target_pairs={{0,1},{1,0},{2,3},{3,2},{4,5},{5,4},{6,7},{7,6},{8,9},{9,8},{10,11... | collective-permute-start | bytes 776 | tf_op jit(solution)/shard_map/ppermute | solution.py:30
  680.6 29.0 %all-to-all-start.8 = ((f32[32,1,64]{2,1,0:T(1,128)}), f32[32,1,64]{2,1,0:T(1,128)S(1)}, u32[]{:S(2)}, u32[]{:S(2)}) async-start(f32[32,1,64]{2,1,0:T(1,128)} %bitcast.108), calls=%async_computation.13 | async-start | bytes 32768 | tf_op jit(solution)/shard_map/all_to_all | solution.py:980
  (157 other events, 1147.8 us)
Sparse Core Ops, SparseCore 0:
  42.4 44.7 all-gather.6
  88.7 26.6 all-gather.14
  117.6 52.5 all-gather.8
  172.1 109.0 all-gather.12
  282.6 61.7 all-gather.10
  391.3 55.9 reduce-scatter.5
  449.6 108.3 reduce-scatter.7
  560.3 30.6 reduce-scatter.9
  593.3 43.9 reduce-scatter.11
  648.0 43.0 reduce-scatter.13

commit v4 on v3

--- a/solution.py
+++ b/solution.py
@@ -170,11 +170,12 @@
     return same, opened, tail, whole
 
 
-def decay_terms(logit, tri):
-    forget = lower_bound + span_bound * jax.nn.sigmoid(logit)
-    key = span_bound * jax.nn.sigmoid(-logit)
-    log_sum = split_sum(tri, jnp.log(forget), NN)
-    return forget, key, log_sum
+def key_of(logit):
+    return span_bound * jax.nn.sigmoid(-logit)
+
+
+def forget_of(logit):
+    return lower_bound + span_bound * jax.nn.sigmoid(logit)
 
 
 def lower_ones(size):
@@ -207,7 +208,7 @@
     return carry
 
 
-def state_kernel(at_ref, docs_ref, zv_ref, bias_ref, packed_ref, state, decay):
+def state_kernel(at_ref, docs_ref, zv_ref, bias_ref, packed_ref, logs_ref, state, decay):
     rows, size = zv_ref.shape[1:3]
     heads, width = state.shape[1:3]
     half, chunk = pl.program_id(0), pl.program_id(1)
@@ -226,7 +227,9 @@
             low = head * width
             logit = zv_ref[0, row, :, low : low + width] + bias_ref[:, low : low + width]
             value = zv_ref[0, row, :, heads * width + low : heads * width + low + width]
-            _, key, log_sum = decay_terms(logit, tri)
+            key = key_of(logit)
+            log_sum = split_sum(tri, jnp.log(forget_of(logit)), NN)
+            logs_ref[0, row, :, low : low + width] = log_sum
             last = log_sum[size - 1 : size, :]
             passed = jnp.where(whole, jnp.exp(last), 0.0)
             weighted = jnp.where(tail, key * jnp.exp(last - log_sum), 0.0)
@@ -240,12 +243,11 @@
                 pack_state(packed_ref, row, head, state[row, head], decay[row, head])
 
 
-def forward_kernel(half, at_ref, docs_ref, qr_ref, zv_ref, bias_ref, gain_ref, *rest):
-    carry_refs, (out_ref, mixed_ref, starts_ref, state) = rest[:-4], rest[-4:]
+def forward_kernel(half, at_ref, docs_ref, qr_ref, zv_ref, logs_ref, bias_ref, gain_ref, *rest):
+    carry_refs, (out_ref, mixed_ref, starts_ref, scores_ref, state) = rest[:-5], rest[-5:]
     rows, size = qr_ref.shape[1:3]
     heads, width = state.shape[1:3]
     chunk = pl.program_id(0)
-    tri = lower_ones(size)
 
     @pl.when(chunk == 0)
     def _():
@@ -264,11 +266,14 @@
             gate = qr_ref[0, row, :, high : high + width]
             logit = zv_ref[0, row, :, low : low + width] + bias_ref[:, low : low + width]
             value = pair(zv_ref[0, row, :, high : high + width])
-            _, key, log_sum = decay_terms(logit, tri)
+            key = key_of(logit)
+            log_sum = logs_ref[0, row, :, low : low + width]
             last = log_sum[size - 1 : size, :]
             lifted = pair(query * jax.nn.sigmoid(query) * jnp.exp(log_sum))
             lowered = pair(key * jnp.exp(-log_sum))
-            scores = pair(jnp.where(same, mm(lifted, lowered, NT), 0.0))
+            scores = jnp.where(same, mm(lifted, lowered, NT), 0.0)
+            scores_ref[0, row, head] = scores
+            scores = pair(scores)
             begin = state[row, head]
             starts_ref[0, row, head] = begin
             out = mm(scores, value, NN) + jnp.where(opened, mm(lifted, pair(begin), NT), 0.0)
@@ -288,6 +293,7 @@
     docs_ref,
     qr_ref,
     zv_ref,
+    logs_ref,
     out_ref,
     grad_ref,
     bias_ref,
@@ -297,6 +303,7 @@
     low_ref,
     part_ref,
     packed_ref,
+    slopes_ref,
     state,
     decay,
 ):
@@ -304,7 +311,6 @@
     heads, width = state.shape[1:3]
     half, step = pl.program_id(0), pl.program_id(1)
     chunk = pl.num_programs(1) - 1 - step
-    tri = lower_ones(size)
 
     @pl.when(step == 0)
     def _():
@@ -324,7 +330,8 @@
             value = pair(zv_ref[0, row, :, high : high + width])
             out = out_ref[0, row, :, low : low + width]
             grad_mixed = grad_ref[0, row, :, low : low + width] * gain_ref[:, low : low + width]
-            _, key, log_sum = decay_terms(logit, tri)
+            key = key_of(logit)
+            log_sum = logs_ref[0, row, :, low : low + width]
             last = log_sum[size - 1 : size, :]
             rise = jnp.exp(log_sum)
             query_on = jax.nn.sigmoid(query)
@@ -338,7 +345,9 @@
                 grad_normed - normed * jnp.mean(grad_normed * normed, axis=-1, keepdims=True)
             )
             grad_low = pair(grad_out)
-            grad_scores = pair(jnp.where(same, mm(grad_low, value, NT), 0.0))
+            grad_scores = jnp.where(same, mm(grad_low, value, NT), 0.0)
+            slopes_ref[0, row, head] = grad_scores
+            grad_scores = pair(grad_scores)
             grad_lifted = mm(grad_scores, lowered, NN) + jnp.where(
                 opened, mm(grad_low, pair(starts_ref[0, row, head]), NN), 0.0
             )
@@ -362,7 +371,19 @@
 
 
 def close_kernel(
-    at_ref, docs_ref, kept_ref, qr_ref, zv_ref, low_ref, part_ref, bias_ref, starts_ref, *rest
+    at_ref,
+    docs_ref,
+    kept_ref,
+    qr_ref,
+    zv_ref,
+    logs_ref,
+    low_ref,
+    part_ref,
+    bias_ref,
+    starts_ref,
+    scores_ref,
+    slopes_ref,
+    *rest,
 ):
     carry_refs, (zv_grad_ref, bias_grad_ref, state) = rest[:-3], rest[-3:]
     rows, size = qr_ref.shape[1:3]
@@ -382,7 +403,7 @@
                 state[row, head] = unpack_carry(carry_refs, row, head)
 
     for row in range(rows):
-        same, opened, tail, whole = chunk_masks(
+        _, opened, tail, whole = chunk_masks(
             docs_ref, half * rows + row, at_ref[1] + chunk * size, size
         )
         for head in range(heads):
@@ -392,7 +413,9 @@
             logit = zv_ref[0, row, :, low : low + width] + bias_ref[:, low : low + width]
             value = pair(zv_ref[0, row, :, high : high + width])
             grad_low = pair(low_ref[0, row, :, low : low + width])
-            forget, key, log_sum = decay_terms(logit, tri)
+            key = key_of(logit)
+            log_sum = logs_ref[0, row, :, low : low + width]
+            forget = forget_of(logit)
             last = log_sum[size - 1 : size, :]
             fall = jnp.exp(-log_sum)
             remain = jnp.where(tail, jnp.exp(last - log_sum), 0.0)
@@ -400,11 +423,11 @@
             lowered = key * fall
             weighted = key * remain
             lifted_low = pair(lifted)
-            scores = pair(jnp.where(same, mm(lifted_low, pair(lowered), NT), 0.0))
+            scores = pair(scores_ref[0, row, head])
             begin = starts_ref[0, row, head]
             later = state[row, head]
             later_low = pair(later)
-            grad_scores = pair(jnp.where(same, mm(grad_low, value, NT), 0.0))
+            grad_scores = pair(slopes_ref[0, row, head])
             grad_value = mm(scores, grad_low, TN) + mm(pair(weighted), later_low, NT)
             grad_lowered = mm(grad_scores, lifted_low, TN)
             grad_weighted = mm(value, later_low, NN)
@@ -466,21 +489,27 @@
 
 
 def up_kernel(in_ref, pair_ref, slope_ref, product_ref):
-    both = jnp.dot(in_ref[...], pair_ref[...], preferred_element_type=f32)
-    units = both.shape[1] // 2
-    gate, up = both[:, :units], both[:, units:]
-    gate_on = jax.nn.sigmoid(gate)
-    active = gate * gate_on
-    product_ref[...] = (active * up).astype(bf16)
-    slope_ref[0] = up * (gate_on + active * (1.0 - gate_on))
-    slope_ref[1] = active
+    rows = in_ref.shape[0] // 2
+    units = pair_ref.shape[1] // 2
+    cuts = [slice(0, rows), slice(rows, 2 * rows)]
+    boths = [jnp.dot(in_ref[cut, :], pair_ref[...], preferred_element_type=f32) for cut in cuts]
+    for cut, both in zip(cuts, boths):
+        gate, up = both[:, :units], both[:, units:]
+        gate_on = jax.nn.sigmoid(gate)
+        active = gate * gate_on
+        product_ref[cut, :] = (active * up).astype(bf16)
+        slope_ref[0, cut, :] = up * (gate_on + active * (1.0 - gate_on))
+        slope_ref[1, cut, :] = active
 
 
 def down_kernel(grad_ref, down_ref, slope_ref, out_ref):
-    grad = jnp.dot(grad_ref[...], down_ref[...], preferred_element_type=f32)
-    out_ref[...] = jnp.concatenate(
-        [grad * slope_ref[0], grad * slope_ref[1]], axis=-1
-    ).astype(bf16)
+    rows = grad_ref.shape[0] // 2
+    cuts = [slice(0, rows), slice(rows, 2 * rows)]
+    grads = [jnp.dot(grad_ref[cut, :], down_ref[...], preferred_element_type=f32) for cut in cuts]
+    for cut, grad in zip(cuts, grads):
+        out_ref[cut, :] = jnp.concatenate(
+            [grad * slope_ref[0, cut, :], grad * slope_ref[1, cut, :]], axis=-1
+        ).astype(bf16)
 
 
 def feed_up(mid_all, pair_all, tile):
@@ -704,6 +733,7 @@
     ).transpose(1, 0, 2)
     down_cut = w_down.T.reshape(block, spots, units).transpose(1, 0, 2)
 
+    normed, held = join(normed, held)
     first, pair_cut, down_cut = join(gather_first(normed), pair_cut, down_cut)
     normed_all = gather_last(gather_second(*first))
 
@@ -731,14 +761,14 @@
 
     by_half = pl.BlockSpec(packed_block, lambda h, c, at_ref, docs_ref: (h, 0, 0, 0))
 
-    packed = local_call(
+    packed, logs = local_call(
         state_kernel,
         at,
         docs,
         (zv, bias_here),
         [slab(2 * wide, ahead), once],
-        packed_shape,
-        by_half,
+        (packed_shape, jax.ShapeDtypeStruct(by_block + (wide,), f32)),
+        (by_half, slab(wide, ahead)),
         (2, spots),
         (states, decays),
     )
@@ -774,20 +804,25 @@
             kernel,
             at,
             docs,
-            (qr, zv, bias_here, gain_here, *carried),
-            [slab(2 * wide, place), slab(2 * wide, place), once, once]
+            (qr, zv, logs, bias_here, gain_here, *carried),
+            [slab(2 * wide, place), slab(2 * wide, place), slab(wide, place), once, once]
             + [pl.BlockSpec(packed_block, lambda c, at_ref, docs_ref: (side, 0, 0, 0))]
             * len(carried),
             (
                 jax.ShapeDtypeStruct((spots,) + by_block[1:] + (wide,), f32),
                 jax.ShapeDtypeStruct((spots,) + by_block[1:] + (wide,), bf16),
                 jax.ShapeDtypeStruct((spots, row_count, heads, width, width), f32),
+                jax.ShapeDtypeStruct((spots, row_count, heads, span, span), f32),
             ),
             (
                 slab(wide, local),
                 slab(wide, local),
                 pl.BlockSpec(
                     (1, row_count, heads, width, width),
+                    lambda c, at_ref, docs_ref: (c, 0, 0, 0, 0),
+                ),
+                pl.BlockSpec(
+                    (1, row_count, heads, span, span),
                     lambda c, at_ref, docs_ref: (c, 0, 0, 0, 0),
                 ),
             ),
@@ -807,9 +842,9 @@
         held = lax.dynamic_index_in_dim(held, own_row, 0, False)
         out_here = lax.dynamic_index_in_dim(held, own_spot, 1, False).reshape(wide, features)
 
-    far_out, far_mixed, far_starts = forward_half(1, qr)
+    far_out, far_mixed, far_starts, far_scores = forward_half(1, qr)
     far_mixed = far_mixed.reshape(half, wide)
-    near_out, near_mixed, near_starts = forward_half(0, qr)
+    near_out, near_mixed, near_starts, near_scores = forward_half(0, qr)
     near_mixed = near_mixed.reshape(half, wide)
     state = scatter_product(near_mixed, far_mixed, out_here, tokens)
     hidden = input_float + scatter_group(state)[0]
@@ -850,18 +885,24 @@
     ).reshape(by_block + (wide,))
     mixer_out = jnp.concatenate([near_out, far_out], axis=0)
     starts = jnp.concatenate([near_starts, far_starts], axis=0)
+    scores = jnp.concatenate([near_scores, far_scores], axis=0)
+    scores_spec = pl.BlockSpec(
+        (1, row_count, heads, span, span),
+        lambda h, c, at_ref, docs_ref: (h * spots + spots - 1 - c, 0, 0, 0, 0),
+    )
     starts_spec = pl.BlockSpec(
         (1, row_count, heads, width, width),
         lambda h, c, at_ref, docs_ref: (h * spots + spots - 1 - c, 0, 0, 0, 0),
     )
-    all_grads, lows, parts, packed = local_call(
+    all_grads, lows, parts, packed, slopes = local_call(
         open_kernel,
         at,
         docs,
-        (qr, zv, mixer_out, grad_mixed, bias_here, gain_here, starts),
+        (qr, zv, logs, mixer_out, grad_mixed, bias_here, gain_here, starts),
         [
             slab(2 * wide, behind),
             slab(2 * wide, behind),
+            slab(wide, behind),
             slab(wide, behind),
             slab(wide, behind),
             once,
@@ -873,8 +914,9 @@
             jax.ShapeDtypeStruct(by_block + (wide,), f32),
             jax.ShapeDtypeStruct(by_block + (wide,), f32),
             packed_shape,
+            jax.ShapeDtypeStruct((2 * spots, row_count, heads, span, span), f32),
         ),
-        (slab(2 * wide, behind), slab(wide, behind), slab(wide, behind), by_half),
+        (slab(2 * wide, behind), slab(wide, behind), slab(wide, behind), by_half, scores_spec),
         (2, spots),
         (states, decays),
     )
@@ -901,15 +943,12 @@
 
     packed, grad_down = join(packed, grad_down)
     down_back = over_plane(grad_down.reshape(spots, block, units))
-    pair_back = over_plane(grad_pair.reshape(spots, block, 2 * units))
 
     def beside(step):
         if step == 0:
             return (out_rows(), scatter_third(*sums), down_back)
         if step == 1:
-            return (query_part(), turn_units(done[2]), pair_back)
-        if step == 2:
-            return tuple(pair_parts(done[5]))
+            return (query_part(), turn_units(done[2]))
         return ()
 
     later = []
@@ -918,7 +957,9 @@
         packed, extra = join(hop(packed, False), beside(step))
         later.append(packed)
         done += extra
-    grad_out_rows, sums, _, qr_part, grad_down, _, grad_gate, grad_up = done
+    grad_out_rows, sums, _, qr_part, grad_down = done
+    later, grad_pair = join(later, grad_pair)
+    pair_back = over_plane(grad_pair.reshape(spots, block, 2 * units))
     block_output = (hidden + scatter_last(*sums)).astype(bf16)
     if by_chip:
         cut = grad_out_rows.reshape(heads, 2, share, features)
@@ -948,15 +989,18 @@
         close_kernel,
         at,
         docs,
-        (all_grads, qr, zv, lows, parts, bias_here, starts, *later),
+        (all_grads, qr, zv, logs, lows, parts, bias_here, starts, scores, slopes, *later),
         [
             pl.BlockSpec(memory_space=pl.ANY),
             slab(2 * wide, behind),
             slab(2 * wide, behind),
             slab(wide, behind),
             slab(wide, behind),
+            slab(wide, behind),
             once,
             starts_spec,
+            scores_spec,
+            scores_spec,
         ]
         + [by_half] * len(later),
         (
@@ -968,6 +1012,7 @@
         (states,),
         {2: 0},
     )
+    all_grads, pair_back = join(all_grads, pair_back)
     all_grads = all_grads.reshape(2 * half, 4 * wide)
     zv_part = contract_rows(normed_all, all_grads[:, 2 * wide :]).astype(bf16)
     late_grads, zv_part = join(all_grads, zv_part)
@@ -983,20 +1028,24 @@
     grad_bias = jnp.sum(bias_back, axis=0)
 
     def join_heads(cut):
-        back = over_group(cut.reshape(members, share, 2 * wide))
-        back = back.reshape(spots, 2, share, 2, heads, width)
+        back = cut.reshape(spots, 2, share, 2, heads, width)
         return [
             back[:, :, :, at].transpose(2, 1, 3, 0, 4).reshape(share, features).astype(f32)
             for at in range(2)
         ]
 
-    state, block_output, grad_out, grad_qr = join(state, block_output, grad_out, grad_qr)
+    state, block_output, grad_out, grad_qr = join(
+        state, block_output, grad_out, over_group(grad_qr.reshape(members, share, 2 * wide))
+    )
     grad_out = grad_out.astype(f32)
-    state, (query_back, outgate_back), grad_out, block_output = join(
-        scatter_second(*state), join_heads(grad_qr), grad_out, block_output
+    state, (query_back, outgate_back), grad_out, block_output, (grad_gate, grad_up) = join(
+        scatter_second(*state), join_heads(grad_qr), grad_out, block_output, pair_parts(pair_back)
     )
     state, grad_zv = join(scatter_sums(*state), grad_zv)
-    state, (forget_back, input_back) = join(scatter_fourth(*state), join_heads(grad_zv))
+    state, (forget_back, input_back) = join(
+        scatter_fourth(*state),
+        join_heads(over_group(grad_zv.reshape(members, share, 2 * wide))),
+    )
     grad_normed = scatter_last(*state)
     input_grad = grad_hidden + rms_back(grad_normed * first_gain, input_float, first_rate)
     input_grad = input_grad.astype(bf16).reshape(block_input.shape)

time: 760 us -> 752 us (0.989)
  Pallas kernels: 143 us -> 128 us
    pallas_call x5, Pallas kernels: 71.5 us -> 57.2 us  [local_call(): pl.pallas_call(kernel, grid_spec=pltpu.PrefetchScalarGridSpec(num_scalar_...]
    ppermute x6, starting transfers between devices: 29 us -> 19.1 us  [hop(): return lax.ppermute(packed, 'z', pairs)]
    all_to_all x4, waiting for transfers between devices: 16.2 us -> 6.79 us  [over_plane(): return lax.all_to_all(cut, plane, 0, 0, tiled=True)]
    unnamed x220 -> x226, local copies, waits for them, and re-layouts: 32.5 us -> 33.4 us
  transfers between devices with their start and end apart: 81 -> 81, of which waited for: 43 -> 41; matrix products, arithmetic and copies ran while one was open for 33% -> 34% of each run, Pallas kernels for 17% -> 15%
where the time goes in v4:
time: 752 us; the launch traced here: 741 us
  waiting for transfers between devices  181 us (24%)
  Pallas kernels  128 us (17%)
  matrix products  125 us (17%)
  local copies, waits for them, and re-layouts  106 us (14%)
  starting transfers between devices  96.3 us (13%)
  other arithmetic  70.1 us (9%)
  blocking collectives  17.9 us (2%)
  between operations  16.2 us (2%)
    ppermute x16, waiting for transfers between devices, swap_x(): return lax.ppermute(a, 'x', swap)  61.9 us
    pallas_call x5, Pallas kernels, local_call(): pl.pallas_call(kernel, grid_spec=pltpu.PrefetchScalarGridSpec(num_scalar_...  57.2 us
    dot_general x8, matrix products, times_transpose(): lax.dot_general(left, right, (NT, ((), ())), preferred_element_type=f32)  54.1 us
    ppermute x16, waiting for transfers between devices, swap_y(): return lax.ppermute(a, 'y', swap)  53.6 us
    dot_general x6, matrix products, contract_rows(): lax.dot_general(left, right, (TN, ((), ())), preferred_element_type=f32)  49.2 us
    pallas_call x6, Pallas kernels, big_call(): pl.pallas_call(kernel, grid=grid, in_specs=in_specs, out_shape=out_shapes...  47.8 us
    unnamed x226, local copies, waits for them, and re-layouts  33.4 us
    ppermute x6, waiting for transfers between devices, hop(): return lax.ppermute(packed, 'z', pairs)  25 us
  transfers between devices with their start and end apart: 81, of which 41 were waited for; matrix products, arithmetic and copies ran while one was open for 34% of the time, Pallas kernels for 15%

profile of v4, /device:TPU:0, one launch (start us, length us, event | category | flops | bytes accessed | tf_op | source)
XLA Modules:
  0.0 741.2 jit_solution(6916379183202997666)
XLA Ops:
  9.3 7.3 all-to-all-start
  24.0 17.9 %all_to_all.53 = bf16[8,2,64,512]{3,2,1,0:T(8,128)(2,1)S(1)} all-to-all(bf16[8,2,64,512]{3,2,1,0:T(8,128)(2,1)S(1)} %copy.85), channel_id=1, replica_groups=mesh['z'=4,'y'=2,'x'=2,'row'=2] {'y','x','row'}, dimensions={0} | all-to-all | bytes 2097152 | tf_op jit(solution)/shard_map/all_to_all | solution.py:701
  53.0 16.1 %collective-permute-done.1.refs_1_ = bf16[256,2048]{1,0:T(8,128)(2,1)S(1)} collective-permute-done((bf16[256,2048]{1,0:T(8,128)(2,1)S(1)}, bf16[256,2048]{1,0:T(8,128)(2,1)S(1)}, u32[]{:S(2)}, u32[]{:S(2)}) %collective-permute-start.1) | collective-permute-done | bytes 1048608 | tf_op jit(solution)/shard_map/ppermute | solution.py:22
  73.6 12.0 %collective-permute-done.3.refs_3_ = bf16[128,2048]{1,0:T(8,128)(2,1)} collective-permute-done((bf16[128,2048]{1,0:T(8,128)(2,1)}, bf16[128,2048]{1,0:T(8,128)(2,1)}, u32[]{:S(2)}, u32[]{:S(2)}) %collective-permute-start.3) | collective-permute-done | bytes 524320 | tf_op jit(solution)/shard_map/ppermute | solution.py:26
  96.1 10.7 %fusion.48 = f32[2048,512]{1,0:T(8,128)} fusion(bf16[2048,2048]{1,0:T(8,128)(2,1)} %shard_map.254, bf16[2048,512]{1,0:T(8,128)(2,1)} %all-gather.7.cloned.1.call-done), kind=kOutput, calls=%fused_computation.169 | convolution fusion | flops 4294967296 | bytes 14680064 | tf_op jit(solution)/shard_map/dot_general | solution.py:645
  112.9 8.3 %shard_map.255 = (bf16[4,2,144,128]{3,2,1,0:T(8,128)(2,1)S(1)}, f32[8,2,128,256]{3,2,1,0:T(8,128)S(1)}) custom-call(s32[2]{0:T(128)S(1)} %pad_add_fusion.1.at_ref.refs_0_, s32[4,4]{1,0:T(4,128)S(1)} %pad_add_fusion.docs_ref.refs_1_, f32[8,2,128,512]{3,2,1,0:T(8,128)} %bitcast.265, f32[1,256]{1,0:T(1,128)S(1)} %get-tuple-element.327.bias_ref.refs_5_), custom_call_target="tpu_custom_call" | custom-call | tf_op jit(solution)/shard_map/pallas_call | solution.py:461
  156.1 7.2 collective-permute-start.12
  171.6 10.6 %fusion.49 = f32[2048,512]{1,0:T(8,128)} fusion(bf16[2048,2048]{1,0:T(8,128)(2,1)} %shard_map.254, bf16[2048,512]{1,0:T(8,128)(2,1)} %all-gather.9.cloned.1.call-done), kind=kOutput, calls=%fused_computation.170 | convolution fusion | flops 4294967296 | bytes 14680064 | tf_op jit(solution)/shard_map/dot_general | solution.py:645
  184.4 7.6 %shard_map.257 = (f32[4,2,128,256]{3,2,1,0:T(8,128)S(1)}, bf16[4,2,128,256]{3,2,1,0:T(8,128)(2,1)S(1)}, f32[4,2,2,128,128]{4,3,2,1,0:T(8,128)S(1)}, f32[4,2,2,128,128]{4,3,2,1,0:T(8,128)S(1)}) custom-call(s32[2]{0:T(128)S(1)} %pad_add_fusion.1.at_ref.refs_0_, s32[4,4]{1,0:T(4,128)S(1)} %pad_add_fusion.docs_ref.refs_1_, f32[8,2,128,512]{3,2,1,0:T(8,128)} %bitcast.270, ...), custom_call_target="tpu_custom_call" | custom-call | tf_op jit(solution)/shard_map/pallas_call | solution.py:461
  196.3 7.6 %shard_map.256 = (f32[4,2,128,256]{3,2,1,0:T(8,128)S(1)}, bf16[4,2,128,256]{3,2,1,0:T(8,128)(2,1)S(1)}, f32[4,2,2,128,128]{4,3,2,1,0:T(8,128)S(1)}, f32[4,2,2,128,128]{4,3,2,1,0:T(8,128)S(1)}) custom-call(s32[2]{0:T(128)S(1)} %pad_add_fusion.1.at_ref.refs_0_, s32[4,4]{1,0:T(4,128)S(1)} %pad_add_fusion.docs_ref.refs_1_, f32[8,2,128,512]{3,2,1,0:T(8,128)} %bitcast.271, ...), custom_call_target="tpu_custom_call" | custom-call | tf_op jit(solution)/shard_map/pallas_call | solution.py:461
  222.8 14.9 %collective-permute-done.20 = bf16[2,256,1024]{2,1,0:T(8,128)(2,1)} collective-permute-done((bf16[2,256,1024]{2,1,0:T(8,128)(2,1)}, bf16[2,256,1024]{2,1,0:T(8,128)(2,1)}, u32[]{:S(2)}, u32[]{:S(2)}) %collective-permute-start.20) | collective-permute-done | bytes 1048608 | tf_op jit(solution)/shard_map/ppermute | solution.py:22
  237.7 8.2 %collective-permute-done.21 = bf16[2,256,1024]{2,1,0:T(8,128)(2,1)} collective-permute-done((bf16[2,256,1024]{2,1,0:T(8,128)(2,1)}, bf16[2,256,1024]{2,1,0:T(8,128)(2,1)}, u32[]{:S(2)}, u32[]{:S(2)}) %collective-permute-start.21) | collective-permute-done | bytes 1048608 | tf_op jit(solution)/shard_map/ppermute | solution.py:26
  275.6 7.4 shard_map.262.grad_ref
  283.0 12.3 %collective-permute-done.24.refs_1_ = bf16[256,2048]{1,0:T(8,128)(2,1)S(1)} collective-permute-done((bf16[256,2048]{1,0:T(8,128)(2,1)S(1)}, bf16[256,2048]{1,0:T(8,128)(2,1)S(1)}, u32[]{:S(2)}, u32[]{:S(2)}) %collective-permute-start.24) | collective-permute-done | bytes 1048608 | tf_op jit(solution)/shard_map/ppermute | solution.py:22
  298.4 11.7 %collective-permute-done.31.refs_3_ = bf16[128,2048]{1,0:T(8,128)(2,1)S(1)} collective-permute-done((bf16[128,2048]{1,0:T(8,128)(2,1)S(1)}, bf16[128,2048]{1,0:T(8,128)(2,1)S(1)}, u32[]{:S(2)}, u32[]{:S(2)}) %collective-permute-start.31) | collective-permute-done | bytes 524320 | tf_op jit(solution)/shard_map/ppermute | solution.py:26
  319.5 20.4 %shard_map.264 = (f32[2,2048,704]{2,1,0:T(8,128)}, bf16[2048,704]{1,0:T(8,128)(2,1)S(1)}) custom-call(bf16[2048,2048]{1,0:T(8,128)(2,1)} %shard_map.263.in_ref, bf16[2048,1408]{1,0:T(8,128)(2,1)} %all-gather.13.cloned.1.call-done.pair_ref), custom_call_target="tpu_custom_call" | custom-call | tf_op jit(solution)/shard_map/pallas_call | solution.py:479
  343.5 16.3 %shard_map.265 = bf16[2048,1408]{1,0:T(8,128)(2,1)} custom-call(bf16[2048,2048]{1,0:T(8,128)(2,1)} %shard_map.262.grad_ref, bf16[2048,704]{1,0:T(8,128)(2,1)S(1)} %copy-done.3, f32[2,2048,704]{2,1,0:T(8,128)} %get-tuple-element.209.slope_ref), custom_call_target="tpu_custom_call" | custom-call | tf_op jit(solution)/shard_map/pallas_call | solution.py:479
  359.8 10.2 %convolution_convert_fusion.1 = bf16[1024,2048]{1,0:T(8,128)(2,1)} fusion(bf16[2048,1408]{1,0:T(8,128)(2,1)S(1)} %copy-done.64, bf16[2048,1408]{1,0:T(8,128)(2,1)} %shard_map.265), kind=kOutput, calls=%fused_computation.5 | convolution fusion | flops 5907677184 | bytes 12845056 | tf_op jit(solution)/shard_map/dot_general | solution.py:641
  370.2 7.7 %convolution_convert_fusion.4 = bf16[2048,704]{0,1:T(8,128)(2,1)} fusion(bf16[2048,2048]{1,0:T(8,128)(2,1)S(1)} %bitcast.281, bf16[2048,704]{1,0:T(8,128)(2,1)S(1)} %copy-done.31), kind=kOutput, calls=%fused_computation.8 | convolution fusion | flops 5907021824 | bytes 14155776 | tf_op jit(solution)/shard_map/dot_general | solution.py:637
  378.0 10.4 %convert_add_fusion.2 = f32[1024,2048]{1,0:T(8,128)S(1)} fusion(bf16[1024,2048]{1,0:T(8,128)(2,1)} %collective-permute-done.38, bf16[2048,1408]{1,0:T(8,128)(2,1)} %all-gather.13.cloned.1.call-done.pair_ref, bf16[2048,1408]{1,0:T(8,128)(2,1)} %shard_map.265), kind=kOutput, calls=%fused_computation.2 | convolution fusion | flops 5909774336 | bytes 21233664 | tf_op jit(solution)/shard_map/dot_general | solution.py:641
  402.5 15.6 %convolution_convert_fusion = bf16[2048,1408]{1,0:T(8,128)(2,1)} fusion(bf16[2048,2048]{1,0:T(8,128)(2,1)S(1)} %bitcast.283, bf16[2048,1408]{1,0:T(8,128)(2,1)S(1)} %bitcast.303), kind=kOutput, calls=%fused_computation.3 | convolution fusion | flops 11814043648 | bytes 19922944 | tf_op jit(solution)/shard_map/dot_general | solution.py:637
  448.4 7.6 %convert_add_fusion.1 = f32[1024,2048]{1,0:T(8,128)} fusion(bf16[1024,2048]{1,0:T(8,128)(2,1)} %collective-permute-done.45, bf16[2048,704]{1,0:T(8,128)(2,1)S(1)} %copy-done.5, bf16[2048,704]{1,0:T(8,128)(2,1)S(1)} %copy-done.33), kind=kOutput, calls=%fused_computation.1 | convolution fusion | flops 2956984320 | bytes 17301504 | tf_op jit(solution)/shard_map/dot_general | solution.py:641
  472.1 8.8 %collective-permute-done.46.refs_3_ = bf16[128,2048]{1,0:T(8,128)(2,1)S(1)} collective-permute-done((bf16[128,2048]{1,0:T(8,128)(2,1)S(1)}, bf16[128,2048]{1,0:T(8,128)(2,1)S(1)}, u32[]{:S(2)}, u32[]{:S(2)}) %collective-permute-start.46) | collective-permute-done | bytes 524320 | tf_op jit(solution)/shard_map/ppermute | solution.py:26
  494.6 17.7 %shard_map.267 = (bf16[8,2,128,1024]{3,2,1,0:T(8,128)(2,1)}, f32[8,2,128,256]{3,2,1,0:T(8,128)S(1)}, f32[8,2,128,256]{3,2,1,0:T(8,128)S(1)}, bf16[4,2,144,128]{3,2,1,0:T(8,128)(2,1)S(1)}, f32[8,2,2,128,128]{4,3,2,1,0:T(8,128)}) custom-call(s32[2]{0:T(128)S(1)} %pad_add_fusion.1.at_ref.refs_0_, s32[4,4]{1,0:T(4,128)S(1)} %pad_add_fusion.docs_ref.refs_1_, ...), custom_call_target="tpu_custom_call" | custom-call | tf_op jit(solution)/shard_map/pallas_call | solution.py:461
  543.1 9.9 %convolution_convert_fusion.6 = bf16[2048,512]{1,0:T(8,128)(2,1)} fusion(bf16[2048,2048]{1,0:T(8,128)(2,1)} %shard_map.254, bf16[2048,1024]{1,0:T(8,128)(2,1)} %bitcast.306), kind=kOutput, calls=%fused_computation.10 | convolution fusion | flops 4296015872 | bytes 12582912 | tf_op jit(solution)/shard_map/dot_general | solution.py:637
  556.8 10.7 %collective-permute-done.55.rest_2_ = bf16[4,2,144,128]{3,2,1,0:T(8,128)(2,1)S(1)} collective-permute-done((bf16[4,2,144,128]{3,2,1,0:T(8,128)(2,1)}, bf16[4,2,144,128]{3,2,1,0:T(8,128)(2,1)S(1)}, u32[]{:S(2)}, u32[]{:S(2)}) %collective-permute-start.55) | collective-permute-done | bytes 294944 | tf_op jit(solution)/shard_map/ppermute | solution.py:118
  578.3 16.0 %shard_map.268 = (bf16[8,2,128,1024]{3,2,1,0:T(8,128)(2,1)}, f32[1,256]{1,0:T(1,128)S(1)}) custom-call(s32[2]{0:T(128)S(1)} %pad_add_fusion.1.at_ref.refs_0_, s32[4,4]{1,0:T(4,128)S(1)} %pad_add_fusion.docs_ref.refs_1_, bf16[8,2,128,1024]{3,2,1,0:T(8,128)(2,1)} %get-tuple-element.231.kept_ref, ...), custom_call_target="tpu_custom_call", output_to_operand_aliasing={{0}: (2, {})} | custom-call | tf_op jit(solution)/shard_map/pallas_call | solution.py:461
  594.3 10.0 %convolution_convert_fusion.5 = bf16[2048,512]{1,0:T(8,128)(2,1)} fusion(bf16[2048,2048]{1,0:T(8,128)(2,1)} %shard_map.254, bf16[2048,1024]{1,0:T(8,128)(2,1)} %bitcast.307), kind=kOutput, calls=%fused_computation.9 | convolution fusion | flops 4296015872 | bytes 12582912 | tf_op jit(solution)/shard_map/dot_general | solution.py:637
  604.3 9.5 %convolution_convert_fusion.3 = bf16[1024,2048]{1,0:T(8,128)(2,1)} fusion(bf16[2048,1024]{1,0:T(8,128)(2,1)} %pad_maximum_fusion, bf16[2048,1024]{1,0:T(8,128)(2,1)} %bitcast.308), kind=kOutput, calls=%fused_computation.7 | convolution fusion | flops 4297064448 | bytes 10485760 | tf_op jit(solution)/shard_map/dot_general | solution.py:641
  614.5 6.9 collective-permute-done.57
  632.5 8.6 %convert_add_fusion = f32[1024,2048]{1,0:T(8,128)S(1)} fusion(bf16[1024,2048]{1,0:T(8,128)(2,1)} %collective-permute-done.56, bf16[2048,1024]{1,0:T(8,128)(2,1)} %pad_maximum_fusion, bf16[2048,1024]{1,0:T(8,128)(2,1)} %bitcast.309), kind=kOutput, calls=%fused_computation | convolution fusion | flops 4299161600 | bytes 18874368 | tf_op jit(solution)/shard_map/dot_general | solution.py:641
  708.2 7.8 %all-to-all-done.7 = bf16[8,64,512]{2,1,0:T(8,128)(2,1)} async-done(((bf16[8,64,512]{2,1,0:T(8,128)(2,1)}), bf16[8,64,512]{2,1,0:T(8,128)(2,1)}, u32[]{:S(2)}, u32[]{:S(2)}) %all-to-all-start.7) | async-done | bytes 524320 | tf_op jit(solution)/shard_map/all_to_all | solution.py:701
  (542 shorter events, 371.0 us)
Async XLA Ops:
  7.2 37.4 %all-gather.15.cloned.1.call-start = ((), (), s32[]{:S(2)}) async-start(), calls=%async_computation.23 | async-start | bytes 1310720 | tf_op jit(solution)/shard_map/all_gather | solution.py:692
  16.7 79.5 %all-gather.7.cloned.1.call-start = ((), (), s32[]{:S(2)}) async-start(), calls=%async_computation.14 | async-start | bytes 2621440 | tf_op jit(solution)/shard_map/all_gather | solution.py:708
  43.0 128.5 %all-gather.9.cloned.1.call-start = ((), (), s32[]{:S(2)}) async-start(), calls=%async_computation.15 | async-start | bytes 2621440 | tf_op jit(solution)/shard_map/all_gather | solution.py:708
  44.8 24.2 %collective-permute-start.1 = (bf16[256,2048]{1,0:T(8,128)(2,1)S(1)}, bf16[256,2048]{1,0:T(8,128)(2,1)S(1)}, u32[]{:S(2)}, u32[]{:S(2)}) collective-permute-start(bf16[256,2048]{1,0:T(8,128)(2,1)S(1)} %fusion.19.refs_0_), channel_id=1, source_target_pairs={{0,2},{2,0},{1,3},{3,1},{4,6},{6,4},{5,7},{7,5},{8,10},{10,8},{9,1... | collective-permute-start | bytes 3145736 | tf_op jit(solution)/shard_map/ppermute | solution.py:22
  45.4 24.7 %collective-permute-start.2 = (bf16[256,2048]{1,0:T(8,128)(2,1)S(1)}, bf16[256,2048]{1,0:T(8,128)(2,1)S(1)}, u32[]{:S(2)}, u32[]{:S(2)}) collective-permute-start(bf16[256,2048]{1,0:T(8,128)(2,1)S(1)} %fusion.19.refs_0_), channel_id=1, source_target_pairs={{0,4},{4,0},{1,5},{5,1},{2,6},{6,2},{3,7},{7,3},{8,12},{12,8},{9,1... | collective-permute-start | bytes 3145736 | tf_op jit(solution)/shard_map/ppermute | solution.py:26
  111.3 208.2 %all-gather.13.cloned.1.call-start = ((), (), s32[]{:S(2)}) async-start(), calls=%async_computation.17 | async-start | bytes 7208960 | tf_op jit(solution)/shard_map/all_gather | solution.py:783
  138.4 26.1 %collective-permute-start.13 = (bf16[256,2048]{1,0:T(8,128)(2,1)S(1)}, bf16[256,2048]{1,0:T(8,128)(2,1)}, u32[]{:S(2)}, u32[]{:S(2)}) collective-permute-start(bf16[256,2048]{1,0:T(8,128)(2,1)S(1)} %bitcast.254), channel_id=1, source_target_pairs={{0,2},{2,0},{1,3},{3,1},{4,6},{6,4},{5,7},{7,5},{8,10},{10,8},{9,1... | collective-permute-start | bytes 3145736 | tf_op jit(solution)/shard_map/ppermute | solution.py:22
  139.7 30.0 %collective-permute-start.14 = (bf16[256,2048]{1,0:T(8,128)(2,1)S(1)}, bf16[256,2048]{1,0:T(8,128)(2,1)}, u32[]{:S(2)}, u32[]{:S(2)}) collective-permute-start(bf16[256,2048]{1,0:T(8,128)(2,1)S(1)} %bitcast.255), channel_id=1, source_target_pairs={{0,4},{4,0},{1,5},{5,1},{2,6},{6,2},{3,7},{7,3},{8,12},{12,8},{9,1... | collective-permute-start | bytes 3145736 | tf_op jit(solution)/shard_map/ppermute | solution.py:26
  146.9 35.2 %all-to-all-start.3 = ((bf16[4,128,704]{1,2,0:T(8,128)(2,1)}), bf16[4,128,704]{1,2,0:T(8,128)(2,1)}, u32[]{:S(2)}, u32[]{:S(2)}) async-start(bf16[4,128,704]{1,2,0:T(8,128)(2,1)} %bitcast.322), calls=%async_computation.3 | async-start | bytes 1441792 | tf_op jit(solution)/shard_map/all_to_all | solution.py:704
  151.1 190.5 %all-gather.11.cloned.1.call-start = ((), (), s32[]{:S(2)}) async-start(), calls=%async_computation.16 | async-start | bytes 3932160 | tf_op jit(solution)/shard_map/all_gather | solution.py:789
  156.1 28.4 %collective-permute-start.12 = (bf16[4,2,144,128]{3,2,1,0:T(8,128)(2,1)S(1)}, bf16[4,2,144,128]{3,2,1,0:T(8,128)(2,1)S(1)}, u32[]{:S(2)}, u32[]{:S(2)}) collective-permute-start(bf16[4,2,144,128]{3,2,1,0:T(8,128)(2,1)S(1)} %collective-permute-done.11.refs_8_), channel_id=1, source_target_pairs={{0,8},{8,16},{16,24},{1,9},{9,17},{17,25},{2,10},{10,18},{18,26},{... | collective-permute-start | bytes 884744 | tf_op jit(solution)/shard_map/ppermute | solution.py:118
  212.1 25.7 %collective-permute-start.20 = (bf16[2,256,1024]{2,1,0:T(8,128)(2,1)}, bf16[2,256,1024]{2,1,0:T(8,128)(2,1)}, u32[]{:S(2)}, u32[]{:S(2)}) collective-permute-start(bf16[2,256,1024]{2,1,0:T(8,128)(2,1)} %get-tuple-element.188), channel_id=1, source_target_pairs={{0,2},{2,0},{1,3},{3,1},{4,6},{6,4},{5,7},{7,5},{8,10},{10,8},{9,1... | collective-permute-start | bytes 3145736 | tf_op jit(solution)/shard_map/ppermute | solution.py:22
  220.8 25.1 %collective-permute-start.21 = (bf16[2,256,1024]{2,1,0:T(8,128)(2,1)}, bf16[2,256,1024]{2,1,0:T(8,128)(2,1)}, u32[]{:S(2)}, u32[]{:S(2)}) collective-permute-start(bf16[2,256,1024]{2,1,0:T(8,128)(2,1)} %get-tuple-element.189), channel_id=1, source_target_pairs={{0,4},{4,0},{1,5},{5,1},{2,6},{6,2},{3,7},{7,3},{8,12},{12,8},{9,1... | collective-permute-start | bytes 3145736 | tf_op jit(solution)/shard_map/ppermute | solution.py:26
  222.3 213.8 %reduce-scatter.6.cloned.1.call-start = ((), (), s32[]{:S(2)}) async-start(), calls=%async_computation.18 | async-start | bytes 3604480 | tf_op jit(solution)/shard_map/reduce_scatter | solution.py:862
  269.7 25.6 %collective-permute-start.24 = (bf16[256,2048]{1,0:T(8,128)(2,1)S(1)}, bf16[256,2048]{1,0:T(8,128)(2,1)S(1)}, u32[]{:S(2)}, u32[]{:S(2)}) collective-permute-start(bf16[256,2048]{1,0:T(8,128)(2,1)S(1)} %multiply_convert_fusion.refs_0_), channel_id=1, source_target_pairs={{0,2},{2,0},{1,3},{3,1},{4,6},{6,4},{5,7},{7,5},{8,10},{10,8},{9,1... | collective-permute-start | bytes 3145736 | tf_op jit(solution)/shard_map/ppermute | solution.py:22
  270.3 25.3 %collective-permute-start.25 = (bf16[256,2048]{1,0:T(8,128)(2,1)S(1)}, bf16[256,2048]{1,0:T(8,128)(2,1)S(1)}, u32[]{:S(2)}, u32[]{:S(2)}) collective-permute-start(bf16[256,2048]{1,0:T(8,128)(2,1)S(1)} %multiply_convert_fusion.refs_0_), channel_id=1, source_target_pairs={{0,4},{4,0},{1,5},{5,1},{2,6},{6,2},{3,7},{7,3},{8,12},{12,8},{9,1... | collective-permute-start | bytes 3145736 | tf_op jit(solution)/shard_map/ppermute | solution.py:26
  378.0 190.2 %reduce-scatter.8.cloned.1.call-start = ((), (), s32[]{:S(2)}) async-start(), calls=%async_computation.19 | async-start | bytes 7208960 | tf_op jit(solution)/shard_map/reduce_scatter | solution.py:862
  394.5 25.7 %collective-permute-start.39 = (bf16[2,256,1024]{2,1,0:T(8,128)(2,1)}, bf16[2,256,1024]{2,1,0:T(8,128)(2,1)}, u32[]{:S(2)}, u32[]{:S(2)}) collective-permute-start(bf16[2,256,1024]{2,1,0:T(8,128)(2,1)} %slice_bitcast_fusion.17), channel_id=1, source_target_pairs={{0,2},{2,0},{1,3},{3,1},{4,6},{6,4},{5,7},{7,5},{8,10},{10,8},{9,1... | collective-permute-start | bytes 3145736 | tf_op jit(solution)/shard_map/ppermute | solution.py:22
  395.9 25.3 %collective-permute-start.40 = (bf16[2,256,1024]{2,1,0:T(8,128)(2,1)}, bf16[2,256,1024]{2,1,0:T(8,128)(2,1)S(1)}, u32[]{:S(2)}, u32[]{:S(2)}) collective-permute-start(bf16[2,256,1024]{2,1,0:T(8,128)(2,1)} %slice_bitcast_fusion.16), channel_id=1, source_target_pairs={{0,4},{4,0},{1,5},{5,1},{2,6},{6,2},{3,7},{7,3},{8,12},{12,8},{9,1... | collective-permute-start | bytes 3145736 | tf_op jit(solution)/shard_map/ppermute | solution.py:26
  402.5 44.9 %collective-permute-start.45 = (bf16[1024,2048]{1,0:T(8,128)(2,1)}, bf16[1024,2048]{1,0:T(8,128)(2,1)}, u32[]{:S(2)}, u32[]{:S(2)}) collective-permute-start(bf16[1024,2048]{1,0:T(8,128)(2,1)} %convolution_convert_fusion.2), channel_id=1, source_target_pairs={{0,1},{1,0},{2,3},{3,2},{4,5},{5,4},{6,7},{7,6},{8,9},{9,8},{10,11... | collective-permute-start | bytes 12582920 | tf_op jit(solution)/shard_map/ppermute | solution.py:30
  446.8 23.1 %collective-permute-start.44 = (bf16[256,2048]{1,0:T(8,128)(2,1)S(1)}, bf16[256,2048]{1,0:T(8,128)(2,1)S(1)}, u32[]{:S(2)}, u32[]{:S(2)}) collective-permute-start(bf16[256,2048]{1,0:T(8,128)(2,1)S(1)} %fusion.11.refs_0_), channel_id=1, source_target_pairs={{0,4},{4,0},{1,5},{5,1},{2,6},{6,2},{3,7},{7,3},{8,12},{12,8},{9,1... | collective-permute-start | bytes 3145736 | tf_op jit(solution)/shard_map/ppermute | solution.py:26
  487.0 26.2 %collective-permute-start.49 = (bf16[2,256,1024]{2,1,0:T(8,128)(2,1)}, bf16[2,256,1024]{2,1,0:T(8,128)(2,1)S(1)}, u32[]{:S(2)}, u32[]{:S(2)}) collective-permute-start(bf16[2,256,1024]{2,1,0:T(8,128)(2,1)} %slice_bitcast_fusion.13), channel_id=1, source_target_pairs={{0,2},{2,0},{1,3},{3,1},{4,6},{6,4},{5,7},{7,5},{8,10},{10,8},{9,1... | collective-permute-start | bytes 3145736 | tf_op jit(solution)/shard_map/ppermute | solution.py:22
  488.4 25.6 %collective-permute-start.50 = (bf16[2,256,1024]{2,1,0:T(8,128)(2,1)S(1)}, bf16[2,256,1024]{2,1,0:T(8,128)(2,1)S(1)}, u32[]{:S(2)}, u32[]{:S(2)}) collective-permute-start(bf16[2,256,1024]{2,1,0:T(8,128)(2,1)S(1)} %slice_bitcast_fusion.12), channel_id=1, source_target_pairs={{0,4},{4,0},{1,5},{5,1},{2,6},{6,2},{3,7},{7,3},{8,12},{12,8},{9,1... | collective-permute-start | bytes 3145736 | tf_op jit(solution)/shard_map/ppermute | solution.py:26
  514.1 24.7 %collective-permute-start.51 = (bf16[4,2,144,128]{3,2,1,0:T(8,128)(2,1)S(1)}, bf16[4,2,144,128]{3,2,1,0:T(8,128)(2,1)S(1)}, u32[]{:S(2)}, u32[]{:S(2)}) collective-permute-start(bf16[4,2,144,128]{3,2,1,0:T(8,128)(2,1)S(1)} %get-tuple-element.248), channel_id=1, source_target_pairs={{8,0},{16,8},{24,16},{9,1},{17,9},{25,17},{10,2},{18,10},{26,18},{... | collective-permute-start | bytes 884744 | tf_op jit(solution)/shard_map/ppermute | solution.py:118
  568.2 26.2 %all-to-all-start.5 = ((bf16[4,128,1408]{2,1,0:T(8,128)(2,1)}), bf16[4,128,1408]{2,1,0:T(8,128)(2,1)}, u32[]{:S(2)}, u32[]{:S(2)}) async-start(bf16[4,128,1408]{2,1,0:T(8,128)(2,1)} %bitcast.316), calls=%async_computation.7 | async-start | bytes 2883584 | tf_op jit(solution)/shard_map/all_to_all | solution.py:704
  572.5 55.6 %reduce-scatter.12.cloned.1.call-start = ((), (), s32[]{:S(2)}) async-start(), calls=%async_computation.21 | async-start | bytes 2621440 | tf_op jit(solution)/shard_map/reduce_scatter | solution.py:862
  574.2 78.4 %reduce-scatter.10.cloned.1.call-start = ((), (), s32[]{:S(2)}) async-start(), calls=%async_computation.20 | async-start | bytes 1310720 | tf_op jit(solution)/shard_map/reduce_scatter | solution.py:862
  622.6 72.8 %reduce-scatter.14.cloned.1.call-start = ((), (), s32[]{:S(2)}) async-start(), calls=%async_computation.22 | async-start | bytes 2621440 | tf_op jit(solution)/shard_map/reduce_scatter | solution.py:862
  652.6 30.8 %collective-permute-start.58 = (bf16[2,256,1024]{2,1,0:T(8,128)(2,1)}, bf16[2,256,1024]{2,1,0:T(8,128)(2,1)}, u32[]{:S(2)}, u32[]{:S(2)}) collective-permute-start(bf16[2,256,1024]{2,1,0:T(8,128)(2,1)} %slice_bitcast_fusion.9), channel_id=1, source_target_pairs={{0,2},{2,0},{1,3},{3,1},{4,6},{6,4},{5,7},{7,5},{8,10},{10,8},{9,1... | collective-permute-start | bytes 3145736 | tf_op jit(solution)/shard_map/ppermute | solution.py:22
  654.4 29.0 %collective-permute-start.59 = (bf16[2,256,1024]{2,1,0:T(8,128)(2,1)}, bf16[2,256,1024]{2,1,0:T(8,128)(2,1)}, u32[]{:S(2)}, u32[]{:S(2)}) collective-permute-start(bf16[2,256,1024]{2,1,0:T(8,128)(2,1)} %slice_bitcast_fusion.8), channel_id=1, source_target_pairs={{0,4},{4,0},{1,5},{5,1},{2,6},{6,2},{3,7},{7,3},{8,12},{12,8},{9,1... | collective-permute-start | bytes 3145736 | tf_op jit(solution)/shard_map/ppermute | solution.py:26
  695.4 30.4 %collective-permute-start.60 = (bf16[256,1024]{1,0:T(8,128)(2,1)}, bf16[256,1024]{1,0:T(8,128)(2,1)}, u32[]{:S(2)}, u32[]{:S(2)}) collective-permute-start(bf16[256,1024]{1,0:T(8,128)(2,1)} %fusion.30), channel_id=1, source_target_pairs={{0,4},{4,0},{1,5},{5,1},{2,6},{6,2},{3,7},{7,3},{8,12},{12,8},{9,1... | collective-permute-start | bytes 1572872 | tf_op jit(solution)/shard_map/ppermute | solution.py:26
  696.9 28.9 %collective-permute-start.61 = (bf16[256,1024]{1,0:T(8,128)(2,1)}, bf16[256,1024]{1,0:T(8,128)(2,1)}, u32[]{:S(2)}, u32[]{:S(2)}) collective-permute-start(bf16[256,1024]{1,0:T(8,128)(2,1)} %fusion.31), channel_id=1, source_target_pairs={{0,2},{2,0},{1,3},{3,1},{4,6},{6,4},{5,7},{7,5},{8,10},{10,8},{9,1... | collective-permute-start | bytes 1572872 | tf_op jit(solution)/shard_map/ppermute | solution.py:22
  (160 other events, 1184.5 us)
Sparse Core Ops, SparseCore 0:
  9.6 30.6 all-gather.14
  43.1 44.7 all-gather.6
  90.1 45.9 all-gather.8
  138.2 113.2 all-gather.12
  252.9 63.9 all-gather.10
  378.1 58.0 reduce-scatter.5
  438.5 108.4 reduce-scatter.7
  575.7 44.8 reduce-scatter.11
  623.5 27.1 reduce-scatter.9
  652.8 42.4 reduce-scatter.13

commit v5 on v4

--- a/solution.py
+++ b/solution.py
@@ -1012,7 +1012,7 @@
         (states,),
         {2: 0},
     )
-    all_grads, pair_back = join(all_grads, pair_back)
+    all_grads, pair_back, grad_out = join(all_grads, pair_back, grad_out)
     all_grads = all_grads.reshape(2 * half, 4 * wide)
     zv_part = contract_rows(normed_all, all_grads[:, 2 * wide :]).astype(bf16)
     late_grads, zv_part = join(all_grads, zv_part)

time: 752 us -> 752 us (level)
    ppermute x6, waiting for transfers between devices: 25 us -> 35.6 us  [hop(): return lax.ppermute(packed, 'z', pairs)]
    unnamed x226 -> x230, local copies, waits for them, and re-layouts: 33.4 us -> 33.5 us
where the time goes in v5:
time: 752 us; the launch traced here: 741 us
  waiting for transfers between devices  184 us (24%)
  Pallas kernels  128 us (17%)
  matrix products  125 us (17%)
  local copies, waits for them, and re-layouts  106 us (14%)
  starting transfers between devices  93 us (12%)
  other arithmetic  69.5 us (9%)
  blocking collectives  17.9 us (2%)
  between operations  16.2 us (2%)
    ppermute x16, waiting for transfers between devices, swap_x(): return lax.ppermute(a, 'x', swap)  61.4 us
    pallas_call x5, Pallas kernels, local_call(): pl.pallas_call(kernel, grid_spec=pltpu.PrefetchScalarGridSpec(num_scalar_...  57.2 us
    dot_general x8, matrix products, times_transpose(): lax.dot_general(left, right, (NT, ((), ())), preferred_element_type=f32)  54.6 us
    ppermute x16, waiting for transfers between devices, swap_y(): return lax.ppermute(a, 'y', swap)  53.9 us
    dot_general x6, matrix products, contract_rows(): lax.dot_general(left, right, (TN, ((), ())), preferred_element_type=f32)  49.3 us
    pallas_call x6, Pallas kernels, big_call(): pl.pallas_call(kernel, grid=grid, in_specs=in_specs, out_shape=out_shapes...  47.8 us
    ppermute x6, waiting for transfers between devices, hop(): return lax.ppermute(packed, 'z', pairs)  35.6 us
    unnamed x230, local copies, waits for them, and re-layouts  33.5 us
  transfers between devices with their start and end apart: 81, of which 41 were waited for; matrix products, arithmetic and copies ran while one was open for 34% of the time, Pallas kernels for 15%

profile of v5, /device:TPU:0, one launch (start us, length us, event | category | flops | bytes accessed | tf_op | source)
XLA Modules:
  0.0 741.0 jit_solution(643446126651796657)
XLA Ops:
  9.3 7.3 all-to-all-start
  24.0 17.9 %all_to_all.53 = bf16[8,2,64,512]{3,2,1,0:T(8,128)(2,1)S(1)} all-to-all(bf16[8,2,64,512]{3,2,1,0:T(8,128)(2,1)S(1)} %copy.85), channel_id=1, replica_groups=mesh['z'=4,'y'=2,'x'=2,'row'=2] {'y','x','row'}, dimensions={0} | all-to-all | bytes 2097152 | tf_op jit(solution)/shard_map/all_to_all | solution.py:701
  53.0 16.1 %collective-permute-done.1.refs_1_ = bf16[256,2048]{1,0:T(8,128)(2,1)S(1)} collective-permute-done((bf16[256,2048]{1,0:T(8,128)(2,1)S(1)}, bf16[256,2048]{1,0:T(8,128)(2,1)S(1)}, u32[]{:S(2)}, u32[]{:S(2)}) %collective-permute-start.1) | collective-permute-done | bytes 1048608 | tf_op jit(solution)/shard_map/ppermute | solution.py:22
  73.5 12.0 %collective-permute-done.3.refs_3_ = bf16[128,2048]{1,0:T(8,128)(2,1)} collective-permute-done((bf16[128,2048]{1,0:T(8,128)(2,1)}, bf16[128,2048]{1,0:T(8,128)(2,1)}, u32[]{:S(2)}, u32[]{:S(2)}) %collective-permute-start.3) | collective-permute-done | bytes 524320 | tf_op jit(solution)/shard_map/ppermute | solution.py:26
  89.2 6.8 shard_map.254
  96.1 10.7 %fusion.48 = f32[2048,512]{1,0:T(8,128)} fusion(bf16[2048,2048]{1,0:T(8,128)(2,1)} %shard_map.254, bf16[2048,512]{1,0:T(8,128)(2,1)} %all-gather.7.cloned.1.call-done), kind=kOutput, calls=%fused_computation.169 | convolution fusion | flops 4294967296 | bytes 14680064 | tf_op jit(solution)/shard_map/dot_general | solution.py:645
  112.9 8.3 %shard_map.255 = (bf16[4,2,144,128]{3,2,1,0:T(8,128)(2,1)S(1)}, f32[8,2,128,256]{3,2,1,0:T(8,128)S(1)}) custom-call(s32[2]{0:T(128)S(1)} %pad_add_fusion.1.at_ref.refs_0_, s32[4,4]{1,0:T(4,128)S(1)} %pad_add_fusion.docs_ref.refs_1_, f32[8,2,128,512]{3,2,1,0:T(8,128)} %bitcast.265, f32[1,256]{1,0:T(1,128)S(1)} %get-tuple-element.329.bias_ref.refs_5_), custom_call_target="tpu_custom_call" | custom-call | tf_op jit(solution)/shard_map/pallas_call | solution.py:461
  156.1 7.2 collective-permute-start.12
  171.6 10.6 %fusion.49 = f32[2048,512]{1,0:T(8,128)} fusion(bf16[2048,2048]{1,0:T(8,128)(2,1)} %shard_map.254, bf16[2048,512]{1,0:T(8,128)(2,1)} %all-gather.9.cloned.1.call-done), kind=kOutput, calls=%fused_computation.170 | convolution fusion | flops 4294967296 | bytes 14680064 | tf_op jit(solution)/shard_map/dot_general | solution.py:645
  184.4 7.6 %shard_map.257 = (f32[4,2,128,256]{3,2,1,0:T(8,128)S(1)}, bf16[4,2,128,256]{3,2,1,0:T(8,128)(2,1)S(1)}, f32[4,2,2,128,128]{4,3,2,1,0:T(8,128)S(1)}, f32[4,2,2,128,128]{4,3,2,1,0:T(8,128)S(1)}) custom-call(s32[2]{0:T(128)S(1)} %pad_add_fusion.1.at_ref.refs_0_, s32[4,4]{1,0:T(4,128)S(1)} %pad_add_fusion.docs_ref.refs_1_, f32[8,2,128,512]{3,2,1,0:T(8,128)} %bitcast.270, ...), custom_call_target="tpu_custom_call" | custom-call | tf_op jit(solution)/shard_map/pallas_call | solution.py:461
  196.3 7.6 %shard_map.256 = (f32[4,2,128,256]{3,2,1,0:T(8,128)S(1)}, bf16[4,2,128,256]{3,2,1,0:T(8,128)(2,1)S(1)}, f32[4,2,2,128,128]{4,3,2,1,0:T(8,128)S(1)}, f32[4,2,2,128,128]{4,3,2,1,0:T(8,128)S(1)}) custom-call(s32[2]{0:T(128)S(1)} %pad_add_fusion.1.at_ref.refs_0_, s32[4,4]{1,0:T(4,128)S(1)} %pad_add_fusion.docs_ref.refs_1_, f32[8,2,128,512]{3,2,1,0:T(8,128)} %bitcast.271, ...), custom_call_target="tpu_custom_call" | custom-call | tf_op jit(solution)/shard_map/pallas_call | solution.py:461
  222.8 14.9 %collective-permute-done.20 = bf16[2,256,1024]{2,1,0:T(8,128)(2,1)} collective-permute-done((bf16[2,256,1024]{2,1,0:T(8,128)(2,1)}, bf16[2,256,1024]{2,1,0:T(8,128)(2,1)}, u32[]{:S(2)}, u32[]{:S(2)}) %collective-permute-start.20) | collective-permute-done | bytes 1048608 | tf_op jit(solution)/shard_map/ppermute | solution.py:22
  237.7 8.2 %collective-permute-done.21 = bf16[2,256,1024]{2,1,0:T(8,128)(2,1)} collective-permute-done((bf16[2,256,1024]{2,1,0:T(8,128)(2,1)}, bf16[2,256,1024]{2,1,0:T(8,128)(2,1)}, u32[]{:S(2)}, u32[]{:S(2)}) %collective-permute-start.21) | collective-permute-done | bytes 1048608 | tf_op jit(solution)/shard_map/ppermute | solution.py:26
  275.6 7.4 shard_map.262.grad_ref
  283.0 12.3 %collective-permute-done.24.refs_1_ = bf16[256,2048]{1,0:T(8,128)(2,1)S(1)} collective-permute-done((bf16[256,2048]{1,0:T(8,128)(2,1)S(1)}, bf16[256,2048]{1,0:T(8,128)(2,1)S(1)}, u32[]{:S(2)}, u32[]{:S(2)}) %collective-permute-start.24) | collective-permute-done | bytes 1048608 | tf_op jit(solution)/shard_map/ppermute | solution.py:22
  298.4 11.7 %collective-permute-done.31.refs_3_ = bf16[128,2048]{1,0:T(8,128)(2,1)S(1)} collective-permute-done((bf16[128,2048]{1,0:T(8,128)(2,1)S(1)}, bf16[128,2048]{1,0:T(8,128)(2,1)S(1)}, u32[]{:S(2)}, u32[]{:S(2)}) %collective-permute-start.31) | collective-permute-done | bytes 524320 | tf_op jit(solution)/shard_map/ppermute | solution.py:26
  319.5 20.4 %shard_map.264 = (f32[2,2048,704]{2,1,0:T(8,128)}, bf16[2048,704]{1,0:T(8,128)(2,1)S(1)}) custom-call(bf16[2048,2048]{1,0:T(8,128)(2,1)} %shard_map.263.in_ref, bf16[2048,1408]{1,0:T(8,128)(2,1)} %all-gather.13.cloned.1.call-done.pair_ref), custom_call_target="tpu_custom_call" | custom-call | tf_op jit(solution)/shard_map/pallas_call | solution.py:479
  343.5 16.3 %shard_map.265 = bf16[2048,1408]{1,0:T(8,128)(2,1)} custom-call(bf16[2048,2048]{1,0:T(8,128)(2,1)} %shard_map.262.grad_ref, bf16[2048,704]{1,0:T(8,128)(2,1)S(1)} %copy-done.3, f32[2,2048,704]{2,1,0:T(8,128)} %get-tuple-element.210.slope_ref), custom_call_target="tpu_custom_call" | custom-call | tf_op jit(solution)/shard_map/pallas_call | solution.py:479
  359.8 10.2 %convolution_convert_fusion.1 = bf16[1024,2048]{1,0:T(8,128)(2,1)} fusion(bf16[2048,1408]{1,0:T(8,128)(2,1)S(1)} %copy-done.64, bf16[2048,1408]{1,0:T(8,128)(2,1)} %shard_map.265), kind=kOutput, calls=%fused_computation.5 | convolution fusion | flops 5907677184 | bytes 12845056 | tf_op jit(solution)/shard_map/dot_general | solution.py:641
  370.2 7.7 %convolution_convert_fusion.4 = bf16[2048,704]{0,1:T(8,128)(2,1)} fusion(bf16[2048,2048]{1,0:T(8,128)(2,1)S(1)} %bitcast.281, bf16[2048,704]{1,0:T(8,128)(2,1)S(1)} %copy-done.31), kind=kOutput, calls=%fused_computation.8 | convolution fusion | flops 5907021824 | bytes 14155776 | tf_op jit(solution)/shard_map/dot_general | solution.py:637
  378.0 10.4 %convert_add_fusion.2 = f32[1024,2048]{1,0:T(8,128)S(1)} fusion(bf16[1024,2048]{1,0:T(8,128)(2,1)} %collective-permute-done.38, bf16[2048,1408]{1,0:T(8,128)(2,1)} %all-gather.13.cloned.1.call-done.pair_ref, bf16[2048,1408]{1,0:T(8,128)(2,1)} %shard_map.265), kind=kOutput, calls=%fused_computation.2 | convolution fusion | flops 5909774336 | bytes 21233664 | tf_op jit(solution)/shard_map/dot_general | solution.py:641
  402.5 15.7 %convolution_convert_fusion = bf16[2048,1408]{1,0:T(8,128)(2,1)} fusion(bf16[2048,2048]{1,0:T(8,128)(2,1)S(1)} %bitcast.283, bf16[2048,1408]{1,0:T(8,128)(2,1)S(1)} %bitcast.303), kind=kOutput, calls=%fused_computation.3 | convolution fusion | flops 11814043648 | bytes 19922944 | tf_op jit(solution)/shard_map/dot_general | solution.py:637
  448.4 7.7 %convert_add_fusion.1 = f32[1024,2048]{1,0:T(8,128)} fusion(bf16[1024,2048]{1,0:T(8,128)(2,1)} %collective-permute-done.45, bf16[2048,704]{1,0:T(8,128)(2,1)S(1)} %copy-done.5, bf16[2048,704]{1,0:T(8,128)(2,1)S(1)} %copy-done.33), kind=kOutput, calls=%fused_computation.1 | convolution fusion | flops 2956984320 | bytes 17301504 | tf_op jit(solution)/shard_map/dot_general | solution.py:641
  472.1 8.8 %collective-permute-done.46.refs_3_ = bf16[128,2048]{1,0:T(8,128)(2,1)S(1)} collective-permute-done((bf16[128,2048]{1,0:T(8,128)(2,1)S(1)}, bf16[128,2048]{1,0:T(8,128)(2,1)S(1)}, u32[]{:S(2)}, u32[]{:S(2)}) %collective-permute-start.46) | collective-permute-done | bytes 524320 | tf_op jit(solution)/shard_map/ppermute | solution.py:26
  494.6 17.7 %shard_map.267 = (bf16[8,2,128,1024]{3,2,1,0:T(8,128)(2,1)}, f32[8,2,128,256]{3,2,1,0:T(8,128)S(1)}, f32[8,2,128,256]{3,2,1,0:T(8,128)S(1)}, bf16[4,2,144,128]{3,2,1,0:T(8,128)(2,1)S(1)}, f32[8,2,2,128,128]{4,3,2,1,0:T(8,128)}) custom-call(s32[2]{0:T(128)S(1)} %pad_add_fusion.1.at_ref.refs_0_, s32[4,4]{1,0:T(4,128)S(1)} %pad_add_fusion.docs_ref.refs_1_, ...), custom_call_target="tpu_custom_call" | custom-call | tf_op jit(solution)/shard_map/pallas_call | solution.py:461
  544.9 10.0 %convolution_convert_fusion.6 = bf16[2048,512]{1,0:T(8,128)(2,1)} fusion(bf16[2048,2048]{1,0:T(8,128)(2,1)} %shard_map.254, bf16[2048,1024]{1,0:T(8,128)(2,1)} %bitcast.306), kind=kOutput, calls=%fused_computation.10 | convolution fusion | flops 4296015872 | bytes 12582912 | tf_op jit(solution)/shard_map/dot_general | solution.py:637
  558.6 21.4 %collective-permute-done.55.rest_2_ = bf16[4,2,144,128]{3,2,1,0:T(8,128)(2,1)S(1)} collective-permute-done((bf16[4,2,144,128]{3,2,1,0:T(8,128)(2,1)}, bf16[4,2,144,128]{3,2,1,0:T(8,128)(2,1)S(1)}, u32[]{:S(2)}, u32[]{:S(2)}) %collective-permute-start.55) | collective-permute-done | bytes 294944 | tf_op jit(solution)/shard_map/ppermute | solution.py:118
  590.9 16.0 %shard_map.268 = (bf16[8,2,128,1024]{3,2,1,0:T(8,128)(2,1)}, f32[1,256]{1,0:T(1,128)S(1)}) custom-call(s32[2]{0:T(128)S(1)} %pad_add_fusion.1.at_ref.refs_0_, s32[4,4]{1,0:T(4,128)S(1)} %pad_add_fusion.docs_ref.refs_1_, bf16[8,2,128,1024]{3,2,1,0:T(8,128)(2,1)} %get-tuple-element.232.kept_ref, ...), custom_call_target="tpu_custom_call", output_to_operand_aliasing={{0}: (2, {})} | custom-call | tf_op jit(solution)/shard_map/pallas_call | solution.py:461
  606.9 10.0 %convolution_convert_fusion.5 = bf16[2048,512]{1,0:T(8,128)(2,1)} fusion(bf16[2048,2048]{1,0:T(8,128)(2,1)} %shard_map.254, bf16[2048,1024]{1,0:T(8,128)(2,1)} %bitcast.307), kind=kOutput, calls=%fused_computation.9 | convolution fusion | flops 4296015872 | bytes 12582912 | tf_op jit(solution)/shard_map/dot_general | solution.py:637
  616.9 9.6 %convolution_convert_fusion.3 = bf16[1024,2048]{1,0:T(8,128)(2,1)} fusion(bf16[2048,1024]{1,0:T(8,128)(2,1)} %pad_maximum_fusion, bf16[2048,1024]{1,0:T(8,128)(2,1)} %bitcast.308), kind=kOutput, calls=%fused_computation.7 | convolution fusion | flops 4297064448 | bytes 10485760 | tf_op jit(solution)/shard_map/dot_general | solution.py:641
  636.9 9.0 %convert_add_fusion = f32[1024,2048]{1,0:T(8,128)S(1)} fusion(bf16[1024,2048]{1,0:T(8,128)(2,1)} %collective-permute-done.57, bf16[2048,1024]{1,0:T(8,128)(2,1)} %pad_maximum_fusion, bf16[2048,1024]{1,0:T(8,128)(2,1)} %bitcast.309), kind=kOutput, calls=%fused_computation | convolution fusion | flops 4299161600 | bytes 18874368 | tf_op jit(solution)/shard_map/dot_general | solution.py:641
  705.9 9.9 %all-to-all-done.7 = bf16[8,64,512]{2,1,0:T(8,128)(2,1)} async-done(((bf16[8,64,512]{2,1,0:T(8,128)(2,1)}), bf16[8,64,512]{2,1,0:T(8,128)(2,1)}, u32[]{:S(2)}, u32[]{:S(2)}) %all-to-all-start.7) | async-done | bytes 524320 | tf_op jit(solution)/shard_map/all_to_all | solution.py:701
  (546 shorter events, 357.6 us)
Async XLA Ops:
  7.2 37.3 %all-gather.15.cloned.1.call-start = ((), (), s32[]{:S(2)}) async-start(), calls=%async_computation.23 | async-start | bytes 1310720 | tf_op jit(solution)/shard_map/all_gather | solution.py:692
  16.7 79.4 %all-gather.7.cloned.1.call-start = ((), (), s32[]{:S(2)}) async-start(), calls=%async_computation.14 | async-start | bytes 2621440 | tf_op jit(solution)/shard_map/all_gather | solution.py:708
  43.0 128.5 %all-gather.9.cloned.1.call-start = ((), (), s32[]{:S(2)}) async-start(), calls=%async_computation.15 | async-start | bytes 2621440 | tf_op jit(solution)/shard_map/all_gather | solution.py:708
  44.8 24.2 %collective-permute-start.1 = (bf16[256,2048]{1,0:T(8,128)(2,1)S(1)}, bf16[256,2048]{1,0:T(8,128)(2,1)S(1)}, u32[]{:S(2)}, u32[]{:S(2)}) collective-permute-start(bf16[256,2048]{1,0:T(8,128)(2,1)S(1)} %fusion.19.refs_0_), channel_id=1, source_target_pairs={{0,2},{2,0},{1,3},{3,1},{4,6},{6,4},{5,7},{7,5},{8,10},{10,8},{9,1... | collective-permute-start | bytes 3145736 | tf_op jit(solution)/shard_map/ppermute | solution.py:22
  45.3 24.7 %collective-permute-start.2 = (bf16[256,2048]{1,0:T(8,128)(2,1)S(1)}, bf16[256,2048]{1,0:T(8,128)(2,1)S(1)}, u32[]{:S(2)}, u32[]{:S(2)}) collective-permute-start(bf16[256,2048]{1,0:T(8,128)(2,1)S(1)} %fusion.19.refs_0_), channel_id=1, source_target_pairs={{0,4},{4,0},{1,5},{5,1},{2,6},{6,2},{3,7},{7,3},{8,12},{12,8},{9,1... | collective-permute-start | bytes 3145736 | tf_op jit(solution)/shard_map/ppermute | solution.py:26
  111.3 208.3 %all-gather.13.cloned.1.call-start = ((), (), s32[]{:S(2)}) async-start(), calls=%async_computation.17 | async-start | bytes 7208960 | tf_op jit(solution)/shard_map/all_gather | solution.py:783
  138.4 26.1 %collective-permute-start.13 = (bf16[256,2048]{1,0:T(8,128)(2,1)S(1)}, bf16[256,2048]{1,0:T(8,128)(2,1)}, u32[]{:S(2)}, u32[]{:S(2)}) collective-permute-start(bf16[256,2048]{1,0:T(8,128)(2,1)S(1)} %bitcast.254), channel_id=1, source_target_pairs={{0,2},{2,0},{1,3},{3,1},{4,6},{6,4},{5,7},{7,5},{8,10},{10,8},{9,1... | collective-permute-start | bytes 3145736 | tf_op jit(solution)/shard_map/ppermute | solution.py:22
  139.7 30.0 %collective-permute-start.14 = (bf16[256,2048]{1,0:T(8,128)(2,1)S(1)}, bf16[256,2048]{1,0:T(8,128)(2,1)}, u32[]{:S(2)}, u32[]{:S(2)}) collective-permute-start(bf16[256,2048]{1,0:T(8,128)(2,1)S(1)} %bitcast.255), channel_id=1, source_target_pairs={{0,4},{4,0},{1,5},{5,1},{2,6},{6,2},{3,7},{7,3},{8,12},{12,8},{9,1... | collective-permute-start | bytes 3145736 | tf_op jit(solution)/shard_map/ppermute | solution.py:26
  146.9 35.2 %all-to-all-start.3 = ((bf16[4,128,704]{1,2,0:T(8,128)(2,1)}), bf16[4,128,704]{1,2,0:T(8,128)(2,1)}, u32[]{:S(2)}, u32[]{:S(2)}) async-start(bf16[4,128,704]{1,2,0:T(8,128)(2,1)} %bitcast.322), calls=%async_computation.3 | async-start | bytes 1441792 | tf_op jit(solution)/shard_map/all_to_all | solution.py:704
  151.1 190.5 %all-gather.11.cloned.1.call-start = ((), (), s32[]{:S(2)}) async-start(), calls=%async_computation.16 | async-start | bytes 3932160 | tf_op jit(solution)/shard_map/all_gather | solution.py:789
  156.1 28.4 %collective-permute-start.12 = (bf16[4,2,144,128]{3,2,1,0:T(8,128)(2,1)S(1)}, bf16[4,2,144,128]{3,2,1,0:T(8,128)(2,1)S(1)}, u32[]{:S(2)}, u32[]{:S(2)}) collective-permute-start(bf16[4,2,144,128]{3,2,1,0:T(8,128)(2,1)S(1)} %collective-permute-done.11.refs_8_), channel_id=1, source_target_pairs={{0,8},{8,16},{16,24},{1,9},{9,17},{17,25},{2,10},{10,18},{18,26},{... | collective-permute-start | bytes 884744 | tf_op jit(solution)/shard_map/ppermute | solution.py:118
  212.1 25.7 %collective-permute-start.20 = (bf16[2,256,1024]{2,1,0:T(8,128)(2,1)}, bf16[2,256,1024]{2,1,0:T(8,128)(2,1)}, u32[]{:S(2)}, u32[]{:S(2)}) collective-permute-start(bf16[2,256,1024]{2,1,0:T(8,128)(2,1)} %get-tuple-element.189), channel_id=1, source_target_pairs={{0,2},{2,0},{1,3},{3,1},{4,6},{6,4},{5,7},{7,5},{8,10},{10,8},{9,1... | collective-permute-start | bytes 3145736 | tf_op jit(solution)/shard_map/ppermute | solution.py:22
  220.8 25.1 %collective-permute-start.21 = (bf16[2,256,1024]{2,1,0:T(8,128)(2,1)}, bf16[2,256,1024]{2,1,0:T(8,128)(2,1)}, u32[]{:S(2)}, u32[]{:S(2)}) collective-permute-start(bf16[2,256,1024]{2,1,0:T(8,128)(2,1)} %get-tuple-element.190), channel_id=1, source_target_pairs={{0,4},{4,0},{1,5},{5,1},{2,6},{6,2},{3,7},{7,3},{8,12},{12,8},{9,1... | collective-permute-start | bytes 3145736 | tf_op jit(solution)/shard_map/ppermute | solution.py:26
  222.3 213.9 %reduce-scatter.6.cloned.1.call-start = ((), (), s32[]{:S(2)}) async-start(), calls=%async_computation.18 | async-start | bytes 3604480 | tf_op jit(solution)/shard_map/reduce_scatter | solution.py:862
  269.7 25.6 %collective-permute-start.24 = (bf16[256,2048]{1,0:T(8,128)(2,1)S(1)}, bf16[256,2048]{1,0:T(8,128)(2,1)S(1)}, u32[]{:S(2)}, u32[]{:S(2)}) collective-permute-start(bf16[256,2048]{1,0:T(8,128)(2,1)S(1)} %multiply_convert_fusion.refs_0_), channel_id=1, source_target_pairs={{0,2},{2,0},{1,3},{3,1},{4,6},{6,4},{5,7},{7,5},{8,10},{10,8},{9,1... | collective-permute-start | bytes 3145736 | tf_op jit(solution)/shard_map/ppermute | solution.py:22
  270.3 25.3 %collective-permute-start.25 = (bf16[256,2048]{1,0:T(8,128)(2,1)S(1)}, bf16[256,2048]{1,0:T(8,128)(2,1)S(1)}, u32[]{:S(2)}, u32[]{:S(2)}) collective-permute-start(bf16[256,2048]{1,0:T(8,128)(2,1)S(1)} %multiply_convert_fusion.refs_0_), channel_id=1, source_target_pairs={{0,4},{4,0},{1,5},{5,1},{2,6},{6,2},{3,7},{7,3},{8,12},{12,8},{9,1... | collective-permute-start | bytes 3145736 | tf_op jit(solution)/shard_map/ppermute | solution.py:26
  378.0 202.8 %reduce-scatter.8.cloned.1.call-start = ((), (), s32[]{:S(2)}) async-start(), calls=%async_computation.19 | async-start | bytes 7208960 | tf_op jit(solution)/shard_map/reduce_scatter | solution.py:862
  394.5 25.7 %collective-permute-start.39 = (bf16[2,256,1024]{2,1,0:T(8,128)(2,1)}, bf16[2,256,1024]{2,1,0:T(8,128)(2,1)}, u32[]{:S(2)}, u32[]{:S(2)}) collective-permute-start(bf16[2,256,1024]{2,1,0:T(8,128)(2,1)} %slice_bitcast_fusion.17), channel_id=1, source_target_pairs={{0,2},{2,0},{1,3},{3,1},{4,6},{6,4},{5,7},{7,5},{8,10},{10,8},{9,1... | collective-permute-start | bytes 3145736 | tf_op jit(solution)/shard_map/ppermute | solution.py:22
  395.9 25.3 %collective-permute-start.40 = (bf16[2,256,1024]{2,1,0:T(8,128)(2,1)}, bf16[2,256,1024]{2,1,0:T(8,128)(2,1)S(1)}, u32[]{:S(2)}, u32[]{:S(2)}) collective-permute-start(bf16[2,256,1024]{2,1,0:T(8,128)(2,1)} %slice_bitcast_fusion.16), channel_id=1, source_target_pairs={{0,4},{4,0},{1,5},{5,1},{2,6},{6,2},{3,7},{7,3},{8,12},{12,8},{9,1... | collective-permute-start | bytes 3145736 | tf_op jit(solution)/shard_map/ppermute | solution.py:26
  402.5 44.9 %collective-permute-start.45 = (bf16[1024,2048]{1,0:T(8,128)(2,1)}, bf16[1024,2048]{1,0:T(8,128)(2,1)}, u32[]{:S(2)}, u32[]{:S(2)}) collective-permute-start(bf16[1024,2048]{1,0:T(8,128)(2,1)} %convolution_convert_fusion.2), channel_id=1, source_target_pairs={{0,1},{1,0},{2,3},{3,2},{4,5},{5,4},{6,7},{7,6},{8,9},{9,8},{10,11... | collective-permute-start | bytes 12582920 | tf_op jit(solution)/shard_map/ppermute | solution.py:30
  446.8 23.1 %collective-permute-start.44 = (bf16[256,2048]{1,0:T(8,128)(2,1)S(1)}, bf16[256,2048]{1,0:T(8,128)(2,1)S(1)}, u32[]{:S(2)}, u32[]{:S(2)}) collective-permute-start(bf16[256,2048]{1,0:T(8,128)(2,1)S(1)} %fusion.11.refs_0_), channel_id=1, source_target_pairs={{0,4},{4,0},{1,5},{5,1},{2,6},{6,2},{3,7},{7,3},{8,12},{12,8},{9,1... | collective-permute-start | bytes 3145736 | tf_op jit(solution)/shard_map/ppermute | solution.py:26
  487.1 25.9 %collective-permute-start.49 = (bf16[2,256,1024]{2,1,0:T(8,128)(2,1)S(1)}, bf16[2,256,1024]{2,1,0:T(8,128)(2,1)S(1)}, u32[]{:S(2)}, u32[]{:S(2)}) collective-permute-start(bf16[2,256,1024]{2,1,0:T(8,128)(2,1)S(1)} %copy-done.84), channel_id=1, source_target_pairs={{0,2},{2,0},{1,3},{3,1},{4,6},{6,4},{5,7},{7,5},{8,10},{10,8},{9,1... | collective-permute-start | bytes 3145736 | tf_op jit(solution)/shard_map/ppermute | solution.py:22
  488.5 25.6 %collective-permute-start.50 = (bf16[2,256,1024]{2,1,0:T(8,128)(2,1)S(1)}, bf16[2,256,1024]{2,1,0:T(8,128)(2,1)S(1)}, u32[]{:S(2)}, u32[]{:S(2)}) collective-permute-start(bf16[2,256,1024]{2,1,0:T(8,128)(2,1)S(1)} %slice_bitcast_fusion.12), channel_id=1, source_target_pairs={{0,4},{4,0},{1,5},{5,1},{2,6},{6,2},{3,7},{7,3},{8,12},{12,8},{9,1... | collective-permute-start | bytes 3145736 | tf_op jit(solution)/shard_map/ppermute | solution.py:26
  514.1 24.7 %collective-permute-start.51 = (bf16[4,2,144,128]{3,2,1,0:T(8,128)(2,1)S(1)}, bf16[4,2,144,128]{3,2,1,0:T(8,128)(2,1)S(1)}, u32[]{:S(2)}, u32[]{:S(2)}) collective-permute-start(bf16[4,2,144,128]{3,2,1,0:T(8,128)(2,1)S(1)} %get-tuple-element.249), channel_id=1, source_target_pairs={{8,0},{16,8},{24,16},{9,1},{17,9},{25,17},{10,2},{18,10},{26,18},{... | collective-permute-start | bytes 884744 | tf_op jit(solution)/shard_map/ppermute | solution.py:118
  525.6 81.3 %reduce-scatter.10.cloned.1.call-start = ((), (), s32[]{:S(2)}) async-start(), calls=%async_computation.20 | async-start | bytes 1310720 | tf_op jit(solution)/shard_map/reduce_scatter | solution.py:862
  580.8 26.1 %all-to-all-start.5 = ((bf16[4,128,1408]{2,1,0:T(8,128)(2,1)}), bf16[4,128,1408]{2,1,0:T(8,128)(2,1)}, u32[]{:S(2)}, u32[]{:S(2)}) async-start(bf16[4,128,1408]{2,1,0:T(8,128)(2,1)} %bitcast.316), calls=%async_computation.7 | async-start | bytes 2883584 | tf_op jit(solution)/shard_map/all_to_all | solution.py:704
  585.1 47.4 %reduce-scatter.12.cloned.1.call-start = ((), (), s32[]{:S(2)}) async-start(), calls=%async_computation.21 | async-start | bytes 2621440 | tf_op jit(solution)/shard_map/reduce_scatter | solution.py:862
  586.8 108.1 %reduce-scatter.14.cloned.1.call-start = ((), (), s32[]{:S(2)}) async-start(), calls=%async_computation.22 | async-start | bytes 2621440 | tf_op jit(solution)/shard_map/reduce_scatter | solution.py:862
  656.0 31.0 %collective-permute-start.58 = (bf16[2,256,1024]{2,1,0:T(8,128)(2,1)}, bf16[2,256,1024]{2,1,0:T(8,128)(2,1)}, u32[]{:S(2)}, u32[]{:S(2)}) collective-permute-start(bf16[2,256,1024]{2,1,0:T(8,128)(2,1)} %slice_bitcast_fusion.9), channel_id=1, source_target_pairs={{0,2},{2,0},{1,3},{3,1},{4,6},{6,4},{5,7},{7,5},{8,10},{10,8},{9,1... | collective-permute-start | bytes 3145736 | tf_op jit(solution)/shard_map/ppermute | solution.py:22
  657.8 29.2 %collective-permute-start.59 = (bf16[2,256,1024]{2,1,0:T(8,128)(2,1)}, bf16[2,256,1024]{2,1,0:T(8,128)(2,1)}, u32[]{:S(2)}, u32[]{:S(2)}) collective-permute-start(bf16[2,256,1024]{2,1,0:T(8,128)(2,1)} %slice_bitcast_fusion.8), channel_id=1, source_target_pairs={{0,4},{4,0},{1,5},{5,1},{2,6},{6,2},{3,7},{7,3},{8,12},{12,8},{9,1... | collective-permute-start | bytes 3145736 | tf_op jit(solution)/shard_map/ppermute | solution.py:26
  694.9 30.6 %collective-permute-start.60 = (bf16[256,1024]{1,0:T(8,128)(2,1)}, bf16[256,1024]{1,0:T(8,128)(2,1)}, u32[]{:S(2)}, u32[]{:S(2)}) collective-permute-start(bf16[256,1024]{1,0:T(8,128)(2,1)} %fusion.30), channel_id=1, source_target_pairs={{0,4},{4,0},{1,5},{5,1},{2,6},{6,2},{3,7},{7,3},{8,12},{12,8},{9,1... | collective-permute-start | bytes 1572872 | tf_op jit(solution)/shard_map/ppermute | solution.py:26
  695.4 30.1 %collective-permute-start.61 = (bf16[256,1024]{1,0:T(8,128)(2,1)}, bf16[256,1024]{1,0:T(8,128)(2,1)}, u32[]{:S(2)}, u32[]{:S(2)}) collective-permute-start(bf16[256,1024]{1,0:T(8,128)(2,1)} %fusion.31), channel_id=1, source_target_pairs={{0,2},{2,0},{1,3},{3,1},{4,6},{6,4},{5,7},{7,5},{8,10},{10,8},{9,1... | collective-permute-start | bytes 1572872 | tf_op jit(solution)/shard_map/ppermute | solution.py:22
  (162 other events, 1206.3 us)
Sparse Core Ops, SparseCore 0:
  9.6 30.6 all-gather.14
  43.1 44.7 all-gather.6
  90.1 46.0 all-gather.8
  138.2 113.2 all-gather.12
  252.9 63.9 all-gather.10
  378.1 58.0 reduce-scatter.5
  438.5 108.4 reduce-scatter.7
  549.8 33.9 reduce-scatter.9
  588.3 44.1 reduce-scatter.11
  634.6 43.4 reduce-scatter.13

commit v6 on v5

--- a/solution.py
+++ b/solution.py
@@ -1038,12 +1038,13 @@
         state, block_output, grad_out, over_group(grad_qr.reshape(members, share, 2 * wide))
     )
     grad_out = grad_out.astype(f32)
-    state, (query_back, outgate_back), grad_out, block_output, (grad_gate, grad_up) = join(
-        scatter_second(*state), join_heads(grad_qr), grad_out, block_output, pair_parts(pair_back)
-    )
-    state, grad_zv = join(scatter_sums(*state), grad_zv)
-    state, (forget_back, input_back) = join(
+    state, grad_out, block_output, (grad_gate, grad_up) = join(
+        scatter_second(*state), grad_out, block_output, pair_parts(pair_back)
+    )
+    state, grad_zv, grad_qr = join(scatter_sums(*state), grad_zv, grad_qr)
+    state, (query_back, outgate_back), (forget_back, input_back) = join(
         scatter_fourth(*state),
+        join_heads(grad_qr),
         join_heads(over_group(grad_zv.reshape(members, share, 2 * wide))),
     )
     grad_normed = scatter_last(*state)

time: 752 us -> 758 us (level)
  waiting for transfers between devices: 184 us -> 193 us
    all_to_all x1, waiting for transfers between devices: 3.94 us -> 20.6 us  [on_device(): lax.all_to_all(bias_placed.reshape(groups * members, share), everywhere,...]
    all_to_all x2, waiting for transfers between devices: 9.86 us -> 0.25 us  [over_group(): return lax.all_to_all(cut, group, 0, 0, tiled=True)]
    unnamed x230 -> x232, local copies, waits for them, and re-layouts: 33.5 us -> 33.5 us
where the time goes in v6:
time: 758 us; the launch traced here: 748 us
  waiting for transfers between devices  193 us (25%)
  Pallas kernels  128 us (17%)
  matrix products  125 us (16%)
  local copies, waits for them, and re-layouts  106 us (14%)
  starting transfers between devices  92 us (12%)
  other arithmetic  69.2 us (9%)
  blocking collectives  17.9 us (2%)
  between operations  16.2 us (2%)
    ppermute x16, waiting for transfers between devices, swap_x(): return lax.ppermute(a, 'x', swap)  61.6 us
    pallas_call x5, Pallas kernels, local_call(): pl.pallas_call(kernel, grid_spec=pltpu.PrefetchScalarGridSpec(num_scalar_...  57.1 us
    dot_general x8, matrix products, times_transpose(): lax.dot_general(left, right, (NT, ((), ())), preferred_element_type=f32)  54.7 us
    ppermute x16, waiting for transfers between devices, swap_y(): return lax.ppermute(a, 'y', swap)  53.9 us
    dot_general x6, matrix products, contract_rows(): lax.dot_general(left, right, (TN, ((), ())), preferred_element_type=f32)  49.3 us
    pallas_call x6, Pallas kernels, big_call(): pl.pallas_call(kernel, grid=grid, in_specs=in_specs, out_shape=out_shapes...  47.7 us
    ppermute x6, waiting for transfers between devices, hop(): return lax.ppermute(packed, 'z', pairs)  35.6 us
    unnamed x232, local copies, waits for them, and re-layouts  33.5 us
  transfers between devices with their start and end apart: 81, of which 41 were waited for; matrix products, arithmetic and copies ran while one was open for 34% of the time, Pallas kernels for 15%

profile of v6, /device:TPU:0, one launch (start us, length us, event | category | flops | bytes accessed | tf_op | source)
XLA Modules:
  0.0 747.7 jit_solution(15740276023812039429)
XLA Ops:
  9.3 7.3 all-to-all-start
  24.0 17.9 %all_to_all.53 = bf16[8,2,64,512]{3,2,1,0:T(8,128)(2,1)S(1)} all-to-all(bf16[8,2,64,512]{3,2,1,0:T(8,128)(2,1)S(1)} %copy.85), channel_id=1, replica_groups=mesh['z'=4,'y'=2,'x'=2,'row'=2] {'y','x','row'}, dimensions={0} | all-to-all | bytes 2097152 | tf_op jit(solution)/shard_map/all_to_all | solution.py:701
  53.0 16.0 %collective-permute-done.1.refs_1_ = bf16[256,2048]{1,0:T(8,128)(2,1)S(1)} collective-permute-done((bf16[256,2048]{1,0:T(8,128)(2,1)S(1)}, bf16[256,2048]{1,0:T(8,128)(2,1)S(1)}, u32[]{:S(2)}, u32[]{:S(2)}) %collective-permute-start.1) | collective-permute-done | bytes 1048608 | tf_op jit(solution)/shard_map/ppermute | solution.py:22
  73.5 12.0 %collective-permute-done.3.refs_3_ = bf16[128,2048]{1,0:T(8,128)(2,1)} collective-permute-done((bf16[128,2048]{1,0:T(8,128)(2,1)}, bf16[128,2048]{1,0:T(8,128)(2,1)}, u32[]{:S(2)}, u32[]{:S(2)}) %collective-permute-start.3) | collective-permute-done | bytes 524320 | tf_op jit(solution)/shard_map/ppermute | solution.py:26
  89.2 6.8 shard_map.254
  96.1 10.7 %fusion.48 = f32[2048,512]{1,0:T(8,128)} fusion(bf16[2048,2048]{1,0:T(8,128)(2,1)} %shard_map.254, bf16[2048,512]{1,0:T(8,128)(2,1)} %all-gather.7.cloned.1.call-done), kind=kOutput, calls=%fused_computation.169 | convolution fusion | flops 4294967296 | bytes 14680064 | tf_op jit(solution)/shard_map/dot_general | solution.py:645
  112.8 8.3 %shard_map.255 = (bf16[4,2,144,128]{3,2,1,0:T(8,128)(2,1)S(1)}, f32[8,2,128,256]{3,2,1,0:T(8,128)S(1)}) custom-call(s32[2]{0:T(128)S(1)} %pad_add_fusion.1.at_ref.refs_0_, s32[4,4]{1,0:T(4,128)S(1)} %pad_add_fusion.docs_ref.refs_1_, f32[8,2,128,512]{3,2,1,0:T(8,128)} %bitcast.265, f32[1,256]{1,0:T(1,128)S(1)} %get-tuple-element.331.bias_ref.refs_5_), custom_call_target="tpu_custom_call" | custom-call | tf_op jit(solution)/shard_map/pallas_call | solution.py:461
  156.1 7.2 collective-permute-start.12
  171.6 10.6 %fusion.49 = f32[2048,512]{1,0:T(8,128)} fusion(bf16[2048,2048]{1,0:T(8,128)(2,1)} %shard_map.254, bf16[2048,512]{1,0:T(8,128)(2,1)} %all-gather.9.cloned.1.call-done), kind=kOutput, calls=%fused_computation.170 | convolution fusion | flops 4294967296 | bytes 14680064 | tf_op jit(solution)/shard_map/dot_general | solution.py:645
  184.4 7.6 %shard_map.257 = (f32[4,2,128,256]{3,2,1,0:T(8,128)S(1)}, bf16[4,2,128,256]{3,2,1,0:T(8,128)(2,1)S(1)}, f32[4,2,2,128,128]{4,3,2,1,0:T(8,128)S(1)}, f32[4,2,2,128,128]{4,3,2,1,0:T(8,128)S(1)}) custom-call(s32[2]{0:T(128)S(1)} %pad_add_fusion.1.at_ref.refs_0_, s32[4,4]{1,0:T(4,128)S(1)} %pad_add_fusion.docs_ref.refs_1_, f32[8,2,128,512]{3,2,1,0:T(8,128)} %bitcast.270, ...), custom_call_target="tpu_custom_call" | custom-call | tf_op jit(solution)/shard_map/pallas_call | solution.py:461
  196.3 7.6 %shard_map.256 = (f32[4,2,128,256]{3,2,1,0:T(8,128)S(1)}, bf16[4,2,128,256]{3,2,1,0:T(8,128)(2,1)S(1)}, f32[4,2,2,128,128]{4,3,2,1,0:T(8,128)S(1)}, f32[4,2,2,128,128]{4,3,2,1,0:T(8,128)S(1)}) custom-call(s32[2]{0:T(128)S(1)} %pad_add_fusion.1.at_ref.refs_0_, s32[4,4]{1,0:T(4,128)S(1)} %pad_add_fusion.docs_ref.refs_1_, f32[8,2,128,512]{3,2,1,0:T(8,128)} %bitcast.271, ...), custom_call_target="tpu_custom_call" | custom-call | tf_op jit(solution)/shard_map/pallas_call | solution.py:461
  222.8 15.0 %collective-permute-done.20 = bf16[2,256,1024]{2,1,0:T(8,128)(2,1)} collective-permute-done((bf16[2,256,1024]{2,1,0:T(8,128)(2,1)}, bf16[2,256,1024]{2,1,0:T(8,128)(2,1)}, u32[]{:S(2)}, u32[]{:S(2)}) %collective-permute-start.20) | collective-permute-done | bytes 1048608 | tf_op jit(solution)/shard_map/ppermute | solution.py:22
  237.7 8.2 %collective-permute-done.21 = bf16[2,256,1024]{2,1,0:T(8,128)(2,1)} collective-permute-done((bf16[2,256,1024]{2,1,0:T(8,128)(2,1)}, bf16[2,256,1024]{2,1,0:T(8,128)(2,1)}, u32[]{:S(2)}, u32[]{:S(2)}) %collective-permute-start.21) | collective-permute-done | bytes 1048608 | tf_op jit(solution)/shard_map/ppermute | solution.py:26
  275.6 7.4 shard_map.262.grad_ref
  283.0 12.3 %collective-permute-done.24.refs_1_ = bf16[256,2048]{1,0:T(8,128)(2,1)S(1)} collective-permute-done((bf16[256,2048]{1,0:T(8,128)(2,1)S(1)}, bf16[256,2048]{1,0:T(8,128)(2,1)S(1)}, u32[]{:S(2)}, u32[]{:S(2)}) %collective-permute-start.24) | collective-permute-done | bytes 1048608 | tf_op jit(solution)/shard_map/ppermute | solution.py:22
  298.4 11.7 %collective-permute-done.31.refs_3_ = bf16[128,2048]{1,0:T(8,128)(2,1)S(1)} collective-permute-done((bf16[128,2048]{1,0:T(8,128)(2,1)S(1)}, bf16[128,2048]{1,0:T(8,128)(2,1)S(1)}, u32[]{:S(2)}, u32[]{:S(2)}) %collective-permute-start.31) | collective-permute-done | bytes 524320 | tf_op jit(solution)/shard_map/ppermute | solution.py:26
  319.5 20.4 %shard_map.264 = (f32[2,2048,704]{2,1,0:T(8,128)}, bf16[2048,704]{1,0:T(8,128)(2,1)S(1)}) custom-call(bf16[2048,2048]{1,0:T(8,128)(2,1)} %shard_map.263.in_ref, bf16[2048,1408]{1,0:T(8,128)(2,1)} %all-gather.13.cloned.1.call-done.pair_ref), custom_call_target="tpu_custom_call" | custom-call | tf_op jit(solution)/shard_map/pallas_call | solution.py:479
  343.5 16.3 %shard_map.265 = bf16[2048,1408]{1,0:T(8,128)(2,1)} custom-call(bf16[2048,2048]{1,0:T(8,128)(2,1)} %shard_map.262.grad_ref, bf16[2048,704]{1,0:T(8,128)(2,1)S(1)} %copy-done.3, f32[2,2048,704]{2,1,0:T(8,128)} %get-tuple-element.211.slope_ref), custom_call_target="tpu_custom_call" | custom-call | tf_op jit(solution)/shard_map/pallas_call | solution.py:479
  359.8 10.3 %convolution_convert_fusion.1 = bf16[1024,2048]{1,0:T(8,128)(2,1)} fusion(bf16[2048,1408]{1,0:T(8,128)(2,1)S(1)} %copy-done.65, bf16[2048,1408]{1,0:T(8,128)(2,1)} %shard_map.265), kind=kOutput, calls=%fused_computation.5 | convolution fusion | flops 5907677184 | bytes 12845056 | tf_op jit(solution)/shard_map/dot_general | solution.py:641
  370.3 7.7 %convolution_convert_fusion.4 = bf16[2048,704]{0,1:T(8,128)(2,1)} fusion(bf16[2048,2048]{1,0:T(8,128)(2,1)S(1)} %bitcast.281, bf16[2048,704]{1,0:T(8,128)(2,1)S(1)} %copy-done.31), kind=kOutput, calls=%fused_computation.8 | convolution fusion | flops 5907021824 | bytes 14155776 | tf_op jit(solution)/shard_map/dot_general | solution.py:637
  378.1 10.4 %convert_add_fusion.2 = f32[1024,2048]{1,0:T(8,128)S(1)} fusion(bf16[1024,2048]{1,0:T(8,128)(2,1)} %collective-permute-done.38, bf16[2048,1408]{1,0:T(8,128)(2,1)} %all-gather.13.cloned.1.call-done.pair_ref, bf16[2048,1408]{1,0:T(8,128)(2,1)} %shard_map.265), kind=kOutput, calls=%fused_computation.2 | convolution fusion | flops 5909774336 | bytes 21233664 | tf_op jit(solution)/shard_map/dot_general | solution.py:641
  402.6 15.6 %convolution_convert_fusion = bf16[2048,1408]{1,0:T(8,128)(2,1)} fusion(bf16[2048,2048]{1,0:T(8,128)(2,1)S(1)} %bitcast.283, bf16[2048,1408]{1,0:T(8,128)(2,1)S(1)} %bitcast.303), kind=kOutput, calls=%fused_computation.3 | convolution fusion | flops 11814043648 | bytes 19922944 | tf_op jit(solution)/shard_map/dot_general | solution.py:637
  448.5 7.7 %convert_add_fusion.1 = f32[1024,2048]{1,0:T(8,128)} fusion(bf16[1024,2048]{1,0:T(8,128)(2,1)} %collective-permute-done.45, bf16[2048,704]{1,0:T(8,128)(2,1)S(1)} %copy-done.5, bf16[2048,704]{1,0:T(8,128)(2,1)S(1)} %copy-done.33), kind=kOutput, calls=%fused_computation.1 | convolution fusion | flops 2956984320 | bytes 17301504 | tf_op jit(solution)/shard_map/dot_general | solution.py:641
  472.2 8.8 %collective-permute-done.46.refs_3_ = bf16[128,2048]{1,0:T(8,128)(2,1)S(1)} collective-permute-done((bf16[128,2048]{1,0:T(8,128)(2,1)S(1)}, bf16[128,2048]{1,0:T(8,128)(2,1)S(1)}, u32[]{:S(2)}, u32[]{:S(2)}) %collective-permute-start.46) | collective-permute-done | bytes 524320 | tf_op jit(solution)/shard_map/ppermute | solution.py:26
  494.8 17.6 %shard_map.267 = (bf16[8,2,128,1024]{3,2,1,0:T(8,128)(2,1)}, f32[8,2,128,256]{3,2,1,0:T(8,128)S(1)}, f32[8,2,128,256]{3,2,1,0:T(8,128)S(1)}, bf16[4,2,144,128]{3,2,1,0:T(8,128)(2,1)S(1)}, f32[8,2,2,128,128]{4,3,2,1,0:T(8,128)}) custom-call(s32[2]{0:T(128)S(1)} %pad_add_fusion.1.at_ref.refs_0_, s32[4,4]{1,0:T(4,128)S(1)} %pad_add_fusion.docs_ref.refs_1_, ...), custom_call_target="tpu_custom_call" | custom-call | tf_op jit(solution)/shard_map/pallas_call | solution.py:461
  545.0 10.0 %convolution_convert_fusion.6 = bf16[2048,512]{1,0:T(8,128)(2,1)} fusion(bf16[2048,2048]{1,0:T(8,128)(2,1)} %shard_map.254, bf16[2048,1024]{1,0:T(8,128)(2,1)} %bitcast.306), kind=kOutput, calls=%fused_computation.10 | convolution fusion | flops 4296015872 | bytes 12582912 | tf_op jit(solution)/shard_map/dot_general | solution.py:637
  558.7 21.4 %collective-permute-done.55.rest_2_ = bf16[4,2,144,128]{3,2,1,0:T(8,128)(2,1)S(1)} collective-permute-done((bf16[4,2,144,128]{3,2,1,0:T(8,128)(2,1)}, bf16[4,2,144,128]{3,2,1,0:T(8,128)(2,1)S(1)}, u32[]{:S(2)}, u32[]{:S(2)}) %collective-permute-start.55) | collective-permute-done | bytes 294944 | tf_op jit(solution)/shard_map/ppermute | solution.py:118
  590.9 16.0 %shard_map.268 = (bf16[8,2,128,1024]{3,2,1,0:T(8,128)(2,1)}, f32[1,256]{1,0:T(1,128)S(1)}) custom-call(s32[2]{0:T(128)S(1)} %pad_add_fusion.1.at_ref.refs_0_, s32[4,4]{1,0:T(4,128)S(1)} %pad_add_fusion.docs_ref.refs_1_, bf16[8,2,128,1024]{3,2,1,0:T(8,128)(2,1)} %get-tuple-element.233.kept_ref, ...), custom_call_target="tpu_custom_call", output_to_operand_aliasing={{0}: (2, {})} | custom-call | tf_op jit(solution)/shard_map/pallas_call | solution.py:461
  606.9 10.0 %convolution_convert_fusion.5 = bf16[2048,512]{1,0:T(8,128)(2,1)} fusion(bf16[2048,2048]{1,0:T(8,128)(2,1)} %shard_map.254, bf16[2048,1024]{1,0:T(8,128)(2,1)} %bitcast.307), kind=kOutput, calls=%fused_computation.9 | convolution fusion | flops 4296015872 | bytes 12582912 | tf_op jit(solution)/shard_map/dot_general | solution.py:637
  616.9 9.6 %convolution_convert_fusion.3 = bf16[1024,2048]{1,0:T(8,128)(2,1)} fusion(bf16[2048,1024]{1,0:T(8,128)(2,1)} %pad_maximum_fusion, bf16[2048,1024]{1,0:T(8,128)(2,1)} %bitcast.308), kind=kOutput, calls=%fused_computation.7 | convolution fusion | flops 4297064448 | bytes 10485760 | tf_op jit(solution)/shard_map/dot_general | solution.py:641
  636.9 9.0 %convert_add_fusion = f32[1024,2048]{1,0:T(8,128)S(1)} fusion(bf16[1024,2048]{1,0:T(8,128)(2,1)} %collective-permute-done.57, bf16[2048,1024]{1,0:T(8,128)(2,1)} %pad_maximum_fusion, bf16[2048,1024]{1,0:T(8,128)(2,1)} %bitcast.309), kind=kOutput, calls=%fused_computation | convolution fusion | flops 4299161600 | bytes 18874368 | tf_op jit(solution)/shard_map/dot_general | solution.py:641
  658.5 20.6 %all-to-all-done.8 = f32[32,1,64]{2,1,0:T(1,128)S(1)} async-done(((f32[32,1,64]{2,1,0:T(1,128)}), f32[32,1,64]{2,1,0:T(1,128)S(1)}, u32[]{:S(2)}, u32[]{:S(2)}) %all-to-all-start.8) | async-done | bytes 8224 | tf_op jit(solution)/shard_map/all_to_all | solution.py:1025
  (548 shorter events, 353.5 us)
Async XLA Ops:
  7.2 37.3 %all-gather.15.cloned.1.call-start = ((), (), s32[]{:S(2)}) async-start(), calls=%async_computation.23 | async-start | bytes 1310720 | tf_op jit(solution)/shard_map/all_gather | solution.py:692
  16.7 79.4 %all-gather.7.cloned.1.call-start = ((), (), s32[]{:S(2)}) async-start(), calls=%async_computation.14 | async-start | bytes 2621440 | tf_op jit(solution)/shard_map/all_gather | solution.py:708
  43.0 128.5 %all-gather.9.cloned.1.call-start = ((), (), s32[]{:S(2)}) async-start(), calls=%async_computation.15 | async-start | bytes 2621440 | tf_op jit(solution)/shard_map/all_gather | solution.py:708
  44.8 24.2 %collective-permute-start.1 = (bf16[256,2048]{1,0:T(8,128)(2,1)S(1)}, bf16[256,2048]{1,0:T(8,128)(2,1)S(1)}, u32[]{:S(2)}, u32[]{:S(2)}) collective-permute-start(bf16[256,2048]{1,0:T(8,128)(2,1)S(1)} %fusion.19.refs_0_), channel_id=1, source_target_pairs={{0,2},{2,0},{1,3},{3,1},{4,6},{6,4},{5,7},{7,5},{8,10},{10,8},{9,1... | collective-permute-start | bytes 3145736 | tf_op jit(solution)/shard_map/ppermute | solution.py:22
  45.3 24.7 %collective-permute-start.2 = (bf16[256,2048]{1,0:T(8,128)(2,1)S(1)}, bf16[256,2048]{1,0:T(8,128)(2,1)S(1)}, u32[]{:S(2)}, u32[]{:S(2)}) collective-permute-start(bf16[256,2048]{1,0:T(8,128)(2,1)S(1)} %fusion.19.refs_0_), channel_id=1, source_target_pairs={{0,4},{4,0},{1,5},{5,1},{2,6},{6,2},{3,7},{7,3},{8,12},{12,8},{9,1... | collective-permute-start | bytes 3145736 | tf_op jit(solution)/shard_map/ppermute | solution.py:26
  111.2 208.3 %all-gather.13.cloned.1.call-start = ((), (), s32[]{:S(2)}) async-start(), calls=%async_computation.17 | async-start | bytes 7208960 | tf_op jit(solution)/shard_map/all_gather | solution.py:783
  138.4 26.1 %collective-permute-start.13 = (bf16[256,2048]{1,0:T(8,128)(2,1)S(1)}, bf16[256,2048]{1,0:T(8,128)(2,1)}, u32[]{:S(2)}, u32[]{:S(2)}) collective-permute-start(bf16[256,2048]{1,0:T(8,128)(2,1)S(1)} %bitcast.254), channel_id=1, source_target_pairs={{0,2},{2,0},{1,3},{3,1},{4,6},{6,4},{5,7},{7,5},{8,10},{10,8},{9,1... | collective-permute-start | bytes 3145736 | tf_op jit(solution)/shard_map/ppermute | solution.py:22
  139.7 30.0 %collective-permute-start.14 = (bf16[256,2048]{1,0:T(8,128)(2,1)S(1)}, bf16[256,2048]{1,0:T(8,128)(2,1)}, u32[]{:S(2)}, u32[]{:S(2)}) collective-permute-start(bf16[256,2048]{1,0:T(8,128)(2,1)S(1)} %bitcast.255), channel_id=1, source_target_pairs={{0,4},{4,0},{1,5},{5,1},{2,6},{6,2},{3,7},{7,3},{8,12},{12,8},{9,1... | collective-permute-start | bytes 3145736 | tf_op jit(solution)/shard_map/ppermute | solution.py:26
  146.9 35.2 %all-to-all-start.3 = ((bf16[4,128,704]{1,2,0:T(8,128)(2,1)}), bf16[4,128,704]{1,2,0:T(8,128)(2,1)}, u32[]{:S(2)}, u32[]{:S(2)}) async-start(bf16[4,128,704]{1,2,0:T(8,128)(2,1)} %bitcast.322), calls=%async_computation.3 | async-start | bytes 1441792 | tf_op jit(solution)/shard_map/all_to_all | solution.py:704
  151.1 190.5 %all-gather.11.cloned.1.call-start = ((), (), s32[]{:S(2)}) async-start(), calls=%async_computation.16 | async-start | bytes 3932160 | tf_op jit(solution)/shard_map/all_gather | solution.py:789
  156.1 28.4 %collective-permute-start.12 = (bf16[4,2,144,128]{3,2,1,0:T(8,128)(2,1)S(1)}, bf16[4,2,144,128]{3,2,1,0:T(8,128)(2,1)S(1)}, u32[]{:S(2)}, u32[]{:S(2)}) collective-permute-start(bf16[4,2,144,128]{3,2,1,0:T(8,128)(2,1)S(1)} %collective-permute-done.11.refs_8_), channel_id=1, source_target_pairs={{0,8},{8,16},{16,24},{1,9},{9,17},{17,25},{2,10},{10,18},{18,26},{... | collective-permute-start | bytes 884744 | tf_op jit(solution)/shard_map/ppermute | solution.py:118
  212.0 25.7 %collective-permute-start.20 = (bf16[2,256,1024]{2,1,0:T(8,128)(2,1)}, bf16[2,256,1024]{2,1,0:T(8,128)(2,1)}, u32[]{:S(2)}, u32[]{:S(2)}) collective-permute-start(bf16[2,256,1024]{2,1,0:T(8,128)(2,1)} %get-tuple-element.190), channel_id=1, source_target_pairs={{0,2},{2,0},{1,3},{3,1},{4,6},{6,4},{5,7},{7,5},{8,10},{10,8},{9,1... | collective-permute-start | bytes 3145736 | tf_op jit(solution)/shard_map/ppermute | solution.py:22
  220.8 25.1 %collective-permute-start.21 = (bf16[2,256,1024]{2,1,0:T(8,128)(2,1)}, bf16[2,256,1024]{2,1,0:T(8,128)(2,1)}, u32[]{:S(2)}, u32[]{:S(2)}) collective-permute-start(bf16[2,256,1024]{2,1,0:T(8,128)(2,1)} %get-tuple-element.191), channel_id=1, source_target_pairs={{0,4},{4,0},{1,5},{5,1},{2,6},{6,2},{3,7},{7,3},{8,12},{12,8},{9,1... | collective-permute-start | bytes 3145736 | tf_op jit(solution)/shard_map/ppermute | solution.py:26
  222.3 213.9 %reduce-scatter.6.cloned.1.call-start = ((), (), s32[]{:S(2)}) async-start(), calls=%async_computation.18 | async-start | bytes 3604480 | tf_op jit(solution)/shard_map/reduce_scatter | solution.py:862
  269.7 25.6 %collective-permute-start.24 = (bf16[256,2048]{1,0:T(8,128)(2,1)S(1)}, bf16[256,2048]{1,0:T(8,128)(2,1)S(1)}, u32[]{:S(2)}, u32[]{:S(2)}) collective-permute-start(bf16[256,2048]{1,0:T(8,128)(2,1)S(1)} %multiply_convert_fusion.refs_0_), channel_id=1, source_target_pairs={{0,2},{2,0},{1,3},{3,1},{4,6},{6,4},{5,7},{7,5},{8,10},{10,8},{9,1... | collective-permute-start | bytes 3145736 | tf_op jit(solution)/shard_map/ppermute | solution.py:22
  270.3 25.3 %collective-permute-start.25 = (bf16[256,2048]{1,0:T(8,128)(2,1)S(1)}, bf16[256,2048]{1,0:T(8,128)(2,1)S(1)}, u32[]{:S(2)}, u32[]{:S(2)}) collective-permute-start(bf16[256,2048]{1,0:T(8,128)(2,1)S(1)} %multiply_convert_fusion.refs_0_), channel_id=1, source_target_pairs={{0,4},{4,0},{1,5},{5,1},{2,6},{6,2},{3,7},{7,3},{8,12},{12,8},{9,1... | collective-permute-start | bytes 3145736 | tf_op jit(solution)/shard_map/ppermute | solution.py:26
  378.0 202.8 %reduce-scatter.8.cloned.1.call-start = ((), (), s32[]{:S(2)}) async-start(), calls=%async_computation.19 | async-start | bytes 7208960 | tf_op jit(solution)/shard_map/reduce_scatter | solution.py:862
  394.5 25.7 %collective-permute-start.39 = (bf16[2,256,1024]{2,1,0:T(8,128)(2,1)}, bf16[2,256,1024]{2,1,0:T(8,128)(2,1)}, u32[]{:S(2)}, u32[]{:S(2)}) collective-permute-start(bf16[2,256,1024]{2,1,0:T(8,128)(2,1)} %slice_bitcast_fusion.17), channel_id=1, source_target_pairs={{0,2},{2,0},{1,3},{3,1},{4,6},{6,4},{5,7},{7,5},{8,10},{10,8},{9,1... | collective-permute-start | bytes 3145736 | tf_op jit(solution)/shard_map/ppermute | solution.py:22
  396.0 25.3 %collective-permute-start.40 = (bf16[2,256,1024]{2,1,0:T(8,128)(2,1)}, bf16[2,256,1024]{2,1,0:T(8,128)(2,1)S(1)}, u32[]{:S(2)}, u32[]{:S(2)}) collective-permute-start(bf16[2,256,1024]{2,1,0:T(8,128)(2,1)} %slice_bitcast_fusion.16), channel_id=1, source_target_pairs={{0,4},{4,0},{1,5},{5,1},{2,6},{6,2},{3,7},{7,3},{8,12},{12,8},{9,1... | collective-permute-start | bytes 3145736 | tf_op jit(solution)/shard_map/ppermute | solution.py:26
  402.5 44.9 %collective-permute-start.45 = (bf16[1024,2048]{1,0:T(8,128)(2,1)}, bf16[1024,2048]{1,0:T(8,128)(2,1)}, u32[]{:S(2)}, u32[]{:S(2)}) collective-permute-start(bf16[1024,2048]{1,0:T(8,128)(2,1)} %convolution_convert_fusion.2), channel_id=1, source_target_pairs={{0,1},{1,0},{2,3},{3,2},{4,5},{5,4},{6,7},{7,6},{8,9},{9,8},{10,11... | collective-permute-start | bytes 12582920 | tf_op jit(solution)/shard_map/ppermute | solution.py:30
  487.2 25.9 %collective-permute-start.49 = (bf16[2,256,1024]{2,1,0:T(8,128)(2,1)S(1)}, bf16[2,256,1024]{2,1,0:T(8,128)(2,1)S(1)}, u32[]{:S(2)}, u32[]{:S(2)}) collective-permute-start(bf16[2,256,1024]{2,1,0:T(8,128)(2,1)S(1)} %copy-done.85), channel_id=1, source_target_pairs={{0,2},{2,0},{1,3},{3,1},{4,6},{6,4},{5,7},{7,5},{8,10},{10,8},{9,1... | collective-permute-start | bytes 3145736 | tf_op jit(solution)/shard_map/ppermute | solution.py:22
  488.6 25.6 %collective-permute-start.50 = (bf16[2,256,1024]{2,1,0:T(8,128)(2,1)S(1)}, bf16[2,256,1024]{2,1,0:T(8,128)(2,1)S(1)}, u32[]{:S(2)}, u32[]{:S(2)}) collective-permute-start(bf16[2,256,1024]{2,1,0:T(8,128)(2,1)S(1)} %slice_bitcast_fusion.12), channel_id=1, source_target_pairs={{0,4},{4,0},{1,5},{5,1},{2,6},{6,2},{3,7},{7,3},{8,12},{12,8},{9,1... | collective-permute-start | bytes 3145736 | tf_op jit(solution)/shard_map/ppermute | solution.py:26
  514.2 24.6 %collective-permute-start.51 = (bf16[4,2,144,128]{3,2,1,0:T(8,128)(2,1)S(1)}, bf16[4,2,144,128]{3,2,1,0:T(8,128)(2,1)S(1)}, u32[]{:S(2)}, u32[]{:S(2)}) collective-permute-start(bf16[4,2,144,128]{3,2,1,0:T(8,128)(2,1)S(1)} %get-tuple-element.250), channel_id=1, source_target_pairs={{8,0},{16,8},{24,16},{9,1},{17,9},{25,17},{10,2},{18,10},{26,18},{... | collective-permute-start | bytes 884744 | tf_op jit(solution)/shard_map/ppermute | solution.py:118
  525.6 81.3 %reduce-scatter.10.cloned.1.call-start = ((), (), s32[]{:S(2)}) async-start(), calls=%async_computation.20 | async-start | bytes 1310720 | tf_op jit(solution)/shard_map/reduce_scatter | solution.py:862
  580.8 26.1 %all-to-all-start.5 = ((bf16[4,128,1408]{2,1,0:T(8,128)(2,1)}), bf16[4,128,1408]{2,1,0:T(8,128)(2,1)}, u32[]{:S(2)}, u32[]{:S(2)}) async-start(bf16[4,128,1408]{2,1,0:T(8,128)(2,1)} %bitcast.316), calls=%async_computation.7 | async-start | bytes 2883584 | tf_op jit(solution)/shard_map/all_to_all | solution.py:704
  585.2 47.4 %reduce-scatter.12.cloned.1.call-start = ((), (), s32[]{:S(2)}) async-start(), calls=%async_computation.21 | async-start | bytes 2621440 | tf_op jit(solution)/shard_map/reduce_scatter | solution.py:862
  586.8 113.8 %reduce-scatter.14.cloned.1.call-start = ((), (), s32[]{:S(2)}) async-start(), calls=%async_computation.22 | async-start | bytes 2621440 | tf_op jit(solution)/shard_map/reduce_scatter | solution.py:862
  651.7 41.5 %collective-permute-start.58 = (bf16[2,256,1024]{2,1,0:T(8,128)(2,1)}, bf16[2,256,1024]{2,1,0:T(8,128)(2,1)}, u32[]{:S(2)}, u32[]{:S(2)}) collective-permute-start(bf16[2,256,1024]{2,1,0:T(8,128)(2,1)} %slice_bitcast_fusion.9), channel_id=1, source_target_pairs={{0,2},{2,0},{1,3},{3,1},{4,6},{6,4},{5,7},{7,5},{8,10},{10,8},{9,1... | collective-permute-start | bytes 3145736 | tf_op jit(solution)/shard_map/ppermute | solution.py:22
  653.7 39.6 %collective-permute-start.59 = (bf16[2,256,1024]{2,1,0:T(8,128)(2,1)}, bf16[2,256,1024]{2,1,0:T(8,128)(2,1)}, u32[]{:S(2)}, u32[]{:S(2)}) collective-permute-start(bf16[2,256,1024]{2,1,0:T(8,128)(2,1)} %slice_bitcast_fusion.8), channel_id=1, source_target_pairs={{0,4},{4,0},{1,5},{5,1},{2,6},{6,2},{3,7},{7,3},{8,12},{12,8},{9,1... | collective-permute-start | bytes 3145736 | tf_op jit(solution)/shard_map/ppermute | solution.py:26
  655.9 23.2 %all-to-all-start.8 = ((f32[32,1,64]{2,1,0:T(1,128)}), f32[32,1,64]{2,1,0:T(1,128)S(1)}, u32[]{:S(2)}, u32[]{:S(2)}) async-start(f32[32,1,64]{2,1,0:T(1,128)} %bitcast.108), calls=%async_computation.13 | async-start | bytes 32768 | tf_op jit(solution)/shard_map/all_to_all | solution.py:1025
  700.7 31.6 %collective-permute-start.60 = (bf16[256,1024]{1,0:T(8,128)(2,1)}, bf16[256,1024]{1,0:T(8,128)(2,1)}, u32[]{:S(2)}, u32[]{:S(2)}) collective-permute-start(bf16[256,1024]{1,0:T(8,128)(2,1)} %fusion.30), channel_id=1, source_target_pairs={{0,4},{4,0},{1,5},{5,1},{2,6},{6,2},{3,7},{7,3},{8,12},{12,8},{9,1... | collective-permute-start | bytes 1572872 | tf_op jit(solution)/shard_map/ppermute | solution.py:26
  702.1 30.1 %collective-permute-start.61 = (bf16[256,1024]{1,0:T(8,128)(2,1)}, bf16[256,1024]{1,0:T(8,128)(2,1)}, u32[]{:S(2)}, u32[]{:S(2)}) collective-permute-start(bf16[256,1024]{1,0:T(8,128)(2,1)} %fusion.31), channel_id=1, source_target_pairs={{0,2},{2,0},{1,3},{3,1},{4,6},{6,4},{5,7},{7,5},{8,10},{10,8},{9,1... | collective-permute-start | bytes 1572872 | tf_op jit(solution)/shard_map/ppermute | solution.py:22
  (163 other events, 1221.9 us)
Sparse Core Ops, SparseCore 0:
  9.6 30.6 all-gather.14
  43.1 44.7 all-gather.6
  90.1 46.0 all-gather.8
  138.2 113.1 all-gather.12
  252.9 63.9 all-gather.10
  378.1 58.0 reduce-scatter.5
  438.5 108.4 reduce-scatter.7
  549.9 33.9 reduce-scatter.9
  588.4 44.1 reduce-scatter.11
  634.7 43.4 reduce-scatter.13
